TPU v7x, 256 devices: a whole 4x4x8 slice. The times are simulated.
256 devices in a mesh: ctx: 64 (over y, x, z_lo), head: 4 (over z_hi, core).
Axes of the slice: x: 4, y: 4, z: 8 (z_hi: 2, z_lo: 4; z = z_hi * 4 + z_lo), core: 2. Of those that a mesh axis runs over, the one named last changes fastest.
Arguments:
- queries: bfloat16 [32768, 16, 128], P('ctx', 'head'), may hold values from -6 to 6, as said below
- keys: bfloat16 [32768, 4, 128], P('ctx', 'head'), may hold values from -6 to 6, as said below
- values: bfloat16 [32768, 4, 128], P('ctx', 'head'), may hold values from -6 to 6
- w_out: bfloat16 [2048, 4096], P('head'), may hold values from -0.125 to 0.125
- block_order: int32 [64], replicated, may hold values from 0 to 63, as said below
- chosen: int32 [64, 4, 3], P('ctx', 'head'), may hold values from 0 to 62, as said below
Outputs:
- projected: bfloat16 [32768, 4096], P('ctx', 'head')
Inputs may be any that keep to these rules, and one draw needn't show every extreme that they name: `block_order`: A permutation of the sequence blocks; tokens keep their sequence order inside a stored block. For stored block s with sequence block b = block_order[s]: the entries of chosen[s, k] are distinct and below b, except that when b < 3 the last 3 - b entries equal b and choose nothing. `queries`: bounded entries. `keys`: bounded entries.
All inputs are finite; a program needn't handle non-finite values.
Results may differ from a plain program's by a relative error of at most 0.0056.
Values may be sent and summed in bfloat16 or wider, within the bound.
No kernel may reach another device: no remote copies, remote signals or barrier semaphores. Data moves between devices by JAX's collectives and lax.ppermute only.
A program may use at most 128 MiB of HBM per device.

v0:
```python
import jax
import jax.numpy as jnp
from jax import lax
from jax.sharding import PartitionSpec as P

BLK = 512


def attend_block(query_blk, keys_sel, values_sel, slot_ok, keys_own, values_own):
    n_rows, kv_heads, per_group, head_dim = query_blk.shape
    factor = head_dim ** (-0.5)
    far_scores = (
        jnp.einsum("tkgd,kjsd->tkgjs", query_blk, keys_sel, preferred_element_type=jnp.float32)
        * factor
    )
    far_scores = far_scores.reshape(n_rows, kv_heads, per_group, -1)
    near_scores = (
        jnp.einsum("tkgd,skd->tkgs", query_blk, keys_own, preferred_element_type=jnp.float32)
        * factor
    )
    scores = jnp.concatenate([far_scores, near_scores], axis=3)
    far_ok = jnp.repeat(slot_ok, n_rows, axis=1)
    far_ok = jnp.broadcast_to(far_ok[None, :, None, :], far_scores.shape)
    causal = jnp.arange(n_rows)[None, :] <= jnp.arange(n_rows)[:, None]
    near_ok = jnp.broadcast_to(causal[:, None, None, :], near_scores.shape)
    allowed = jnp.concatenate([far_ok, near_ok], axis=3)
    highest = jnp.max(jnp.where(allowed, scores, -jnp.inf), axis=3, keepdims=True)
    weights = jnp.where(allowed, jnp.exp(scores - highest), 0.0)
    totals = jnp.sum(weights, axis=3, keepdims=True)
    all_values = jnp.concatenate(
        [values_sel.reshape(kv_heads, -1, head_dim), jnp.transpose(values_own, (1, 0, 2))], axis=1
    )
    blended = jnp.einsum(
        "tkgs,ksd->tkgd",
        weights.astype(jnp.bfloat16),
        all_values,
        preferred_element_type=jnp.float32,
    )
    return (blended / totals).astype(jnp.bfloat16).reshape(n_rows, -1)


def local(queries, keys, values, w_out, block_order, chosen):
    tok_dev, q_local, head_dim = queries.shape
    kv_local = keys.shape[1]
    per_group = q_local // kv_local
    blocks_here = tok_dev // BLK
    n_blocks = block_order.shape[0]
    first_slot = lax.axis_index("ctx") * blocks_here
    own_blocks = lax.dynamic_slice_in_dim(block_order, first_slot, blocks_here)
    matches = block_order[None, None, None, :] == chosen[:, :, :, None]
    chosen_slots = jnp.sum(jnp.where(matches, jnp.arange(n_blocks, dtype=jnp.int32), 0), axis=3)
    slot_ok = chosen != own_blocks[:, None, None]
    head_ids = jnp.arange(kv_local, dtype=jnp.int32)[None, :, None]
    blank_rows = jnp.zeros(chosen.shape + (BLK, head_dim), jnp.bfloat16)
    key_piece = lax.all_gather(keys, "ctx", axis=0, tiled=True)
    value_piece = lax.all_gather(values, "ctx", axis=0, tiled=True)
    piece_blocks = key_piece.shape[0] // BLK
    inside = (chosen_slots >= 0) & (chosen_slots < piece_blocks)

    def merge_blocks(current):
        clipped = jnp.clip(chosen_slots, 0, piece_blocks - 1)
        key_blocks = key_piece.reshape(piece_blocks, BLK, kv_local, head_dim)[clipped, :, head_ids]
        value_blocks = value_piece.reshape(piece_blocks, BLK, kv_local, head_dim)[
            clipped, :, head_ids
        ]
        keep = inside[..., None, None]
        return (jnp.where(keep, key_blocks, current[0]), jnp.where(keep, value_blocks, current[1]))

    keys_sel, values_sel = lax.cond(
        jnp.any(inside), merge_blocks, lambda current: current, (blank_rows, blank_rows)
    )

    def one_block(pieces):
        query_blk, keys_own, values_own, keys_got, values_got, ok_here = pieces
        return attend_block(query_blk, keys_got, values_got, ok_here, keys_own, values_own)

    attended = lax.map(
        one_block,
        (
            queries.reshape(blocks_here, BLK, kv_local, per_group, head_dim),
            keys.reshape(blocks_here, BLK, kv_local, head_dim),
            values.reshape(blocks_here, BLK, kv_local, head_dim),
            keys_sel,
            values_sel,
            slot_ok,
        ),
    )
    attended = attended.reshape(tok_dev, q_local * head_dim)
    partial_out = jnp.dot(attended, w_out, preferred_element_type=jnp.float32)
    return lax.psum_scatter(partial_out, "head", scatter_dimension=1, tiled=True).astype(
        jnp.bfloat16
    )


def solution(mesh):
    in_specs = (
        P("ctx", "head", None),
        P("ctx", "head", None),
        P("ctx", "head", None),
        P("head", None),
        P(),
        P("ctx", "head", None),
    )
    out_specs = P("ctx", "head")
    return jax.shard_map(local, mesh=mesh, in_specs=in_specs, out_specs=out_specs, check_vma=False)
```

profile of v0, /device:TPU:1, one launch (start us, length us, event | category | flops | bytes accessed | tf_op | source)
XLA Modules:
  0.0 971.1 jit_solution(8593012877253410438)
XLA Ops:
  6.5 0.7 all-gather.3.cloned.1.call-update
  7.3 0.0 all-gather.5.cloned.1.call-start
  7.3 0.7 all-gather.5.cloned.1.call-update
  8.0 0.0 reduce-scatter.2.cloned.1.call-start
  8.1 1.0 copy.23
  9.1 1.2 dynamic_slice.19
  10.3 1.3 compare_bitcast_fusion
  11.6 0.1 broadcast_in_dim.93
  11.7 0.9 fusion.19
  12.6 0.6 and_reduce_fusion
  13.9 0.1 iota_compare_fusion
  14.0 5.0 multiply_bitcast_fusion.2
  19.0 330.1 %all-gather.3.cloned.1.call-done = bf16[32768,1,128]{2,0,1:T(8,128)(2,1)} async-done(((bf16[512,1,128]{2,0,1:T(8,128)(2,1)}), bf16[32768,1,128]{2,0,1:T(8,128)(2,1)}) %all-gather.3.cloned.1.call-update) | async-done | bytes 8388624 | tf_op jit(solution)/shard_map/all_gather | solution.py:55
  349.2 379.5 %all-gather.5.cloned.1.call-done = bf16[32768,1,128]{2,0,1:T(8,128)(2,1)} async-done(((bf16[512,1,128]{2,0,1:T(8,128)(2,1)}), bf16[32768,1,128]{2,0,1:T(8,128)(2,1)}) %all-gather.5.cloned.1.call-update) | async-done | bytes 8388624 | tf_op jit(solution)/shard_map/all_gather | solution.py:56
  728.7 8.7 conditional.1
  728.7 4.0 gather_fusion.1
  732.8 0.1 broadcast_in_dim.76
  732.9 0.3 bitcast_select_fusion
  733.1 0.2 copy.33
  733.3 4.0 gather_fusion
  737.3 0.1 broadcast_select_fusion
  737.5 6.4 multiply_bitcast_fusion
  743.8 10.6 %copy.26 = f32[512,1,4,3,512]{0,4,3,2,1:T(8,128)} copy(f32[512,1,4,3,512]{0,4,2,3,1:T(8,128)} %multiply_bitcast_fusion) | data formatting | bytes 25165824 | tf_op jit(solution)/shard_map/while/body/eval_jaxpr/mul | solution.py:13
  754.4 0.3 broadcast_in_dim.98
  754.7 11.0 %select_reduce_fusion.1 = f32[512,4]{0,1:T(4,128)S(1)} fusion(pred[512,1,4,512]{0,3,2,1:T(8,128)(4,1)S(1)} %broadcast_in_dim.98, f32[512,1,4,512]{0,3,2,1:T(8,128)} %get-tuple-element.65, f32[512,1,4,1536]{0,3,2,1:T(8,128)} %bitcast.56, pred[2048]{0:T(1024)(128)(4,1)S(1)} %pad.8.clone), kind=kLoop, calls=%fused_computation.15 | loop fusion | flops 16775168 | bytes 17836032 | tf_op jit(solution)/shard_map/while/body/eval_jaxpr/reduce_max | solution.py:27
  765.7 8.3 select_reduce_fusion
  774.0 0.3 broadcast_in_dim.96
  774.3 9.6 divide_convert_fusion
  783.9 7.8 fusion.28
  791.6 0.0 reduce-scatter.2.cloned.1.call-update
  791.7 170.1 %reduce-scatter.2.cloned.1.call-done = f32[512,1024]{1,0:T(8,128)} async-done(((f32[512,4096]{1,0:T(8,128)}), f32[512,1024]{1,0:T(8,128)}) %reduce-scatter.2.cloned.1.call-update) | async-done | bytes 2097168 | tf_op jit(solution)/shard_map/reduce_scatter | solution.py:90
  961.8 2.7 convert_element_type.24
  (16 shorter events, 0.1 us)
Async XLA Ops:
  6.5 730.9 %copy-start.2 = (bf16[512,4,128]{2,1,0:T(4,128)(2,1)S(1)}, bf16[512,4,128]{2,1,0:T(4,128)(2,1)}, u32[]{:S(2)}) copy-start(bf16[512,4,128]{2,1,0:T(4,128)(2,1)} %param.8) | copy-start | bytes 1572868
  6.5 342.6 %all-gather.3.cloned.1.call-start = ((), (), s32[]{:S(2)}) async-start(), calls=%async_computation.1 | async-start | bytes 8519680 | tf_op jit(solution)/shard_map/all_gather | solution.py:55
  7.3 721.4 %all-gather.5.cloned.1.call-start = ((), (), s32[]{:S(2)}) async-start(), calls=%async_computation.2 | async-start | bytes 8519680 | tf_op jit(solution)/shard_map/all_gather | solution.py:56
  8.0 953.8 %reduce-scatter.2.cloned.1.call-start = ((), (), s32[]{:S(2)}) async-start(), calls=%async_computation.3 | async-start | bytes 10485760 | tf_op jit(solution)/shard_map/reduce_scatter | solution.py:90
  737.5 16.9 %copy-start.3 = (bf16[1,1536,128]{1,2,0:T(8,128)(2,1)}, bf16[1,1536,128]{1,2,0:T(8,128)(2,1)S(1)}, u32[]{:S(2)}) copy-start(bf16[1,1536,128]{1,2,0:T(8,128)(2,1)S(1)} %get-tuple-element.64) | copy-start | bytes 1179652
  754.7 11.0 %copy-start = (f32[512,1,4,3,512]{0,4,3,2,1:T(8,128)S(1)}, f32[512,1,4,3,512]{0,4,3,2,1:T(8,128)}, u32[]{:S(2)}) copy-start(f32[512,1,4,3,512]{0,4,3,2,1:T(8,128)} %copy.26) | copy-start | bytes 37748740
  754.7 11.0 %copy-start.1 = (f32[512,1,4,512]{0,3,2,1:T(8,128)S(1)}, f32[512,1,4,512]{0,3,2,1:T(8,128)}, u32[]{:S(2)}) copy-start(f32[512,1,4,512]{0,3,2,1:T(8,128)} %get-tuple-element.65) | copy-start | bytes 12582916
Sparse Core Ops, SparseCore 0:
  9.1 339.9 all-gather.2
  351.0 377.6 all-gather.4
  791.8 169.9 reduce-scatter.1
where the time goes:
time: 971 us
  waiting for transfers between devices  881 us (91%)
  matrix products  28.7 us (3%)
  other arithmetic  25.3 us (3%)
  local copies, waits for them, and re-layouts  21.8 us (2%)
  between operations  13.9 us (1%)
    all_gather x1, waiting for transfers between devices, local(): value_piece = lax.all_gather(values, 'ctx', axis=0, tiled=True)  380 us
    all_gather x1, waiting for transfers between devices, local(): key_piece = lax.all_gather(keys, 'ctx', axis=0, tiled=True)  330 us
    reduce_scatter x1, waiting for transfers between devices, local(): lax.psum_scatter(partial_out, 'head', scatter_dimension=1, tiled=True)  170 us
  transfers between devices with their start and end apart: 3, of which 3 were waited for; matrix products, arithmetic and copies ran while one was open for 1% of the time, Pallas kernels for 0%

commit v1 on v0

v1 whole, which is shorter than its diff:
```python
import functools

import jax
import jax.numpy as jnp
from jax import lax
from jax.experimental import pallas as pl
from jax.experimental.pallas import tpu as pltpu
from jax.sharding import PartitionSpec as P

BLK = 512
HEAD = 128
TOPK = 3
PIECE = 16
FACTOR = HEAD ** -0.5
LOG2E = 1.4426950408889634

SWAP_Z = [(0, 2), (2, 0), (1, 3), (3, 1)]
SWAP_CORE = [(0, 1), (1, 0), (2, 3), (3, 2)]


def pack_kernel(slots_ref, held_ref, out_ref):
    n_dst = out_ref.shape[0]

    def body(dst, carry):
        for j in range(TOPK):
            slot = slots_ref[dst * TOPK + j]
            out_ref[dst, j * PIECE : (j + 1) * PIECE, :] = held_ref[slot, :PIECE, :]
        return carry

    lax.fori_loop(0, n_dst, body, 0, unroll=4)


def attend_kernel(ok_ref, q_ref, k_ref, v_ref, got_ref, out_ref, *, rows):
    half = got_ref.shape[0] // 2
    heads = q_ref.shape[0]
    contract = (((1,), (1,)), ((), ()))
    for h in range(heads):
        for r in range(0, BLK, rows):
            q = q_ref[h, r : r + rows, :]
            seen = r + rows
            near = lax.dot_general(q, k_ref[:seen, :], contract, preferred_element_type=jnp.float32)
            row = lax.broadcasted_iota(jnp.int32, near.shape, 0) + r
            col = lax.broadcasted_iota(jnp.int32, near.shape, 1)
            near = jnp.where(col <= row, near, -jnp.inf)
            far = []
            for j in range(TOPK):
                k_j = got_ref[:half, j * PIECE : (j + 1) * PIECE, :].reshape(BLK, HEAD)
                s = lax.dot_general(q, k_j, contract, preferred_element_type=jnp.float32)
                far.append(jnp.where(ok_ref[j] != 0, s, -jnp.inf))
            highest = jnp.max(near, axis=1, keepdims=True)
            for s in far:
                highest = jnp.maximum(highest, jnp.max(s, axis=1, keepdims=True))
            w = jnp.exp2((near - highest) * (FACTOR * LOG2E))
            total = jnp.sum(w, axis=1, keepdims=True)
            acc = jnp.dot(w.astype(jnp.bfloat16), v_ref[:seen, :], preferred_element_type=jnp.float32)
            for j in range(TOPK):
                v_j = got_ref[half:, j * PIECE : (j + 1) * PIECE, :].reshape(BLK, HEAD)
                w = jnp.exp2((far[j] - highest) * (FACTOR * LOG2E))
                total = total + jnp.sum(w, axis=1, keepdims=True)
                acc = acc + jnp.dot(w.astype(jnp.bfloat16), v_j, preferred_element_type=jnp.float32)
            out_ref[r : r + rows, h * HEAD : (h + 1) * HEAD] = (acc / total).astype(jnp.bfloat16)


def local(queries, keys, values, w_out, block_order, chosen):
    n_blocks = block_order.shape[0]
    head_at = lax.axis_index("head")
    z_hi, core = head_at // 2, head_at % 2
    cols = w_out.shape[1] // 4
    bf16 = jnp.bfloat16

    kv = jnp.concatenate([keys[:, 0, :], values[:, 0, :]], axis=0).reshape(n_blocks, PIECE, HEAD)
    picks = jnp.pad(chosen.reshape(1, 1, TOPK).astype(bf16), ((0, 0), (0, PIECE - 1), (0, HEAD - TOPK)))
    picks = jnp.broadcast_to(picks, (n_blocks, PIECE, HEAD))
    held = lax.all_to_all(jnp.concatenate([kv, picks], axis=1), "ctx", 0, 0, tiled=True)

    picked = held[:, PIECE, :TOPK].astype(jnp.int32)
    same = block_order[None, None, :] == picked[:, :, None]
    slots = jnp.sum(jnp.where(same, jnp.arange(n_blocks, dtype=jnp.int32), 0), axis=2).reshape(-1)
    smem = pl.BlockSpec(memory_space=pltpu.SMEM)
    vmem = pl.BlockSpec(memory_space=pltpu.VMEM)
    packed = pl.pallas_call(
        pack_kernel,
        out_shape=jax.ShapeDtypeStruct((n_blocks, TOPK * PIECE, HEAD), bf16),
        in_specs=[smem, vmem],
        out_specs=vmem,
        name="pack",
    )(slots, held)
    got = lax.all_to_all(packed, "ctx", 0, 0, tiled=True)

    far_cols = lax.dynamic_slice_in_dim(w_out, (1 - z_hi) * 2 * cols, 2 * cols, axis=1)
    near_cols = lax.dynamic_slice_in_dim(w_out, z_hi * 2 * cols, 2 * cols, axis=1)
    far_rows = lax.ppermute(far_cols, "head", SWAP_Z)

    def mine(a):
        return lax.dynamic_slice_in_dim(a, core * cols, cols, axis=1)

    def other(a):
        return lax.dynamic_slice_in_dim(a, (1 - core) * cols, cols, axis=1)

    w_own, w_z = mine(near_cols), mine(far_rows)
    w_core = lax.ppermute(other(near_cols), "head", SWAP_CORE)
    w_zc = lax.ppermute(other(far_rows), "head", SWAP_CORE)

    own = lax.dynamic_slice_in_dim(block_order, lax.axis_index("ctx"), 1)
    ok = (chosen[0, 0] != own).astype(jnp.int32)
    q = jnp.transpose(queries, (1, 0, 2))
    a_own = pl.pallas_call(
        functools.partial(attend_kernel, rows=256),
        out_shape=jax.ShapeDtypeStruct((BLK, queries.shape[1] * HEAD), bf16),
        in_specs=[smem, vmem, vmem, vmem, vmem],
        out_specs=vmem,
        compiler_params=pltpu.CompilerParams(vmem_limit_bytes=48 * 1024 * 1024),
        name="attend",
    )(ok, q, keys[:, 0, :], values[:, 0, :], got)

    a_z = lax.ppermute(a_own, "head", SWAP_Z)
    a_core = lax.ppermute(a_own, "head", SWAP_CORE)
    a_zc = lax.ppermute(a_z, "head", SWAP_CORE)
    dot = functools.partial(jnp.dot, preferred_element_type=jnp.float32)
    out = dot(a_own, w_own) + dot(a_core, w_core) + dot(a_z, w_z) + dot(a_zc, w_zc)
    return out.astype(bf16)


def solution(mesh):
    in_specs = (
        P("ctx", "head", None),
        P("ctx", "head", None),
        P("ctx", "head", None),
        P("head", None),
        P(),
        P("ctx", "head", None),
    )
    out_specs = P("ctx", "head")
    return jax.shard_map(local, mesh=mesh, in_specs=in_specs, out_specs=out_specs, check_vma=False)
```

time: 971 us -> 196 us (0.20)
  waiting for transfers between devices: 881 us -> 132 us
  starting transfers between devices: 0.08 us -> 33.2 us
  other arithmetic: 25.3 us -> 3.36 us
  matrix products: 28.7 us -> 7.71 us
  between operations: 13.9 us -> 0.18 us
  local copies, waits for them, and re-layouts: 21.8 us -> 9.93 us
    all_gather x2 -> x0, waiting for transfers between devices: 710 us -> none  [the longest x1 380 us: local(): value_piece = lax.all_gather(values, 'ctx', axis=0, tiled=True)]
    reduce_scatter x1 -> x0, waiting for transfers between devices: 170 us -> none  [local(): lax.psum_scatter(partial_out, 'head', scatter_dimension=1, tiled=True)]
    all_to_all x0 -> x2, waiting for transfers between devices: none -> 116 us  [the longest x1 99.9 us: local(): lax.all_to_all(jnp.concatenate([kv, picks], axis=1), 'ctx', 0, 0, tiled=T...]
    dot_general x4, matrix products: 28.7 us -> 7.71 us  [the longest x1 2.96 us: local(): dot(a_zc, w_zc)]
    all_to_all x0 -> x2, starting transfers between devices: none -> 17.3 us  [the longest x1 12.6 us: local(): lax.all_to_all(jnp.concatenate([kv, picks], axis=1), 'ctx', 0, 0, tiled=T...]
    ppermute x0 -> x6, starting transfers between devices: none -> 15.8 us  [the longest x1 4.53 us: local(): a_z = lax.ppermute(a_own, 'head', SWAP_Z)]
    ppermute x0 -> x6, waiting for transfers between devices: none -> 15.7 us  [the longest x1 15.7 us: local(): a_z = lax.ppermute(a_own, 'head', SWAP_Z)]
    reduce_max x1 -> x0, other arithmetic: 11 us -> none  [attend_block(): jnp.max(jnp.where(allowed, scores, -jnp.inf), axis=3, keepdims=True)]
  transfers between devices with their start and end apart: 3 -> 8, of which waited for: 3 -> 3; matrix products, arithmetic and copies ran while one was open for 1% -> 8% of each run, Pallas kernels for 0% -> 5%
where the time goes in v1:
time: 196 us
  waiting for transfers between devices  132 us (67%)
  starting transfers between devices  33.2 us (17%)
  local copies, waits for them, and re-layouts  9.93 us (5%)
  Pallas kernels  9.27 us (5%)
  matrix products  7.71 us (4%)
  other arithmetic  3.36 us (2%)
    all_to_all x1, waiting for transfers between devices, local(): lax.all_to_all(jnp.concatenate([kv, picks], axis=1), 'ctx', 0, 0, tiled=T...  99.9 us
    all_to_all x1, waiting for transfers between devices, local(): got = lax.all_to_all(packed, 'ctx', 0, 0, tiled=True)  16.5 us
    ppermute x1, waiting for transfers between devices, local(): a_z = lax.ppermute(a_own, 'head', SWAP_Z)  15.7 us
    all_to_all x1, starting transfers between devices, local(): lax.all_to_all(jnp.concatenate([kv, picks], axis=1), 'ctx', 0, 0, tiled=T...  12.6 us
    pallas_call x1, Pallas kernels, local(): pl.pallas_call(functools.partial(attend_kernel, rows=256), out_shape=jax....  7.03 us
    dynamic_slice x2, local copies, waits for them, and re-layouts, other(): return lax.dynamic_slice_in_dim(a, (1 - core) * cols, cols, axis=1)  5.12 us
    all_to_all x1, starting transfers between devices, local(): got = lax.all_to_all(packed, 'ctx', 0, 0, tiled=True)  4.79 us
    ppermute x1, starting transfers between devices, local(): a_z = lax.ppermute(a_own, 'head', SWAP_Z)  4.53 us
  transfers between devices with their start and end apart: 8, of which 3 were waited for; matrix products, arithmetic and copies ran while one was open for 8% of the time, Pallas kernels for 5%

profile of v1, /device:TPU:1, one launch (start us, length us, event | category | flops | bytes accessed | tf_op | source)
XLA Modules:
  0.0 195.7 jit_solution(9771539249921314669)
XLA Ops:
  0.0 0.7 convert_element_type.25
  0.7 1.0 pad_maximum_fusion.1
  1.7 0.8 pad_maximum_fusion
  2.5 12.6 %all-to-all-start = ((bf16[64,32,128]{2,1,0:T(8,128)(2,1)}), bf16[64,32,128]{2,1,0:T(8,128)(2,1)S(1)}, u32[]{:S(2)}, u32[]{:S(2)}) async-start(bf16[64,32,128]{2,1,0:T(8,128)(2,1)} %pad_maximum_fusion), calls=%async_computation | async-start | bytes 1048576 | tf_op jit(solution)/shard_map/all_to_all | solution.py:74
  15.1 0.0 copy-start.4
  15.1 3.2 %constant_dynamic-slice_fusion = bf16[512,2048]{1,0:T(8,128)(2,1)} fusion(bf16[512,4096]{1,0:T(8,128)(2,1)} %param.9, s32[]{:T(128)S(6)} %select_n.48), kind=kLoop, calls=%fused_computation.13 | loop fusion | bytes 4194308 | tf_op jit(solution)/shard_map/dynamic_slice | solution.py:90
  18.3 4.2 %collective-permute-start.3 = (bf16[512,2048]{1,0:T(8,128)(2,1)}, bf16[512,2048]{1,0:T(8,128)(2,1)}, u32[]{:S(2)}, u32[]{:S(2)}) collective-permute-start(bf16[512,2048]{1,0:T(8,128)(2,1)} %constant_dynamic-slice_fusion), channel_id=1, source_target_pairs={{0,2},{2,0},{1,3},{3,1},{4,6},{6,4},{5,7},{7,5},{8,10},{10,8},{9,1... | collective-permute-start | bytes 6291464 | tf_op jit(solution)/shard_map/ppermute | solution.py:92
  22.5 99.9 %all-to-all-done.held_ref = bf16[64,32,128]{2,1,0:T(8,128)(2,1)S(1)} async-done(((bf16[64,32,128]{2,1,0:T(8,128)(2,1)}), bf16[64,32,128]{2,1,0:T(8,128)(2,1)S(1)}, u32[]{:S(2)}, u32[]{:S(2)}) %all-to-all-start) | async-done | bytes 524320 | tf_op jit(solution)/shard_map/all_to_all | solution.py:74
  122.4 0.1 copy.10
  122.5 0.2 select_reduce_fusion
  122.7 0.1 copy.11
  122.8 0.7 reshape.19.slots_ref
  123.5 2.2 %pack.1 = bf16[64,48,128]{2,1,0:T(8,128)(2,1)} custom-call(s32[192]{0:T(256)} %reshape.19.slots_ref, bf16[64,32,128]{2,1,0:T(8,128)(2,1)} %copy-done.2), custom_call_target="tpu_custom_call" | custom-call | tf_op jit(solution)/shard_map/pack/pallas_call | solution.py:81
  125.8 4.8 %all-to-all-start.1 = ((bf16[64,48,128]{2,1,0:T(8,128)(2,1)}), bf16[64,48,128]{2,1,0:T(8,128)(2,1)S(1)}, u32[]{:S(2)}, u32[]{:S(2)}) async-start(bf16[64,48,128]{2,1,0:T(8,128)(2,1)} %pack.1), calls=%async_computation.1 | async-start | bytes 1572864 | tf_op jit(solution)/shard_map/all_to_all | solution.py:88
  130.6 2.9 %constant_dynamic-slice_fusion.1 = bf16[512,1024]{1,0:T(8,128)(2,1)} fusion(bf16[512,4096]{1,0:T(8,128)(2,1)} %param.9, s32[]{:T(128)S(6)} %dynamic_slice.28), kind=kLoop, calls=%fused_computation.14 | loop fusion | bytes 2097156 | tf_op jit(solution)/shard_map/dynamic_slice | solution.py:98
  133.5 1.9 collective-permute-start.1
  135.4 0.6 dynamic_slice.25
  136.0 0.1 copy.13
  136.1 0.6 fusion.6.ok_ref
  136.8 16.5 %all-to-all-done.1.got_ref = bf16[64,48,128]{2,1,0:T(8,128)(2,1)S(1)} async-done(((bf16[64,48,128]{2,1,0:T(8,128)(2,1)}), bf16[64,48,128]{2,1,0:T(8,128)(2,1)S(1)}, u32[]{:S(2)}, u32[]{:S(2)}) %all-to-all-start.1) | async-done | bytes 786464 | tf_op jit(solution)/shard_map/all_to_all | solution.py:88
  153.3 7.0 %attend.1 = bf16[512,512]{1,0:T(8,128)(2,1)S(1)} custom-call(s32[3]{0:T(128)S(1)} %fusion.6.ok_ref, bf16[4,512,128]{2,1,0:T(8,128)(2,1)S(1)} %bitcast.18, bf16[512,128]{1,0:T(8,128)(2,1)S(1)} %bitcast.20, bf16[512,128]{1,0:T(8,128)(2,1)S(1)} %bitcast.22, bf16[64,48,128]{2,1,0:T(8,128)(2,1)S(1)} %all-to-all-done.1.got_ref), custom_call_target="tpu_custom_call" | custom-call | tf_op jit(solution)/shard_map/attend/pallas_call | solution.py:107
  160.3 4.5 %collective-permute-start.2 = (bf16[512,512]{1,0:T(8,128)(2,1)S(1)}, bf16[512,512]{1,0:T(8,128)(2,1)S(1)}, u32[]{:S(2)}, u32[]{:S(2)}) collective-permute-start(bf16[512,512]{1,0:T(8,128)(2,1)S(1)} %attend.1), channel_id=1, source_target_pairs={{0,2},{2,0},{1,3},{3,1},{4,6},{6,4},{5,7},{7,5},{8,10},{10,8},{9,1... | collective-permute-start | bytes 1572872 | tf_op jit(solution)/shard_map/ppermute | solution.py:116
  164.8 0.0 collective-permute-done.3
  164.8 2.3 %constant_dynamic-slice_fusion.2 = bf16[512,1024]{1,0:T(8,128)(2,1)} fusion(bf16[512,2048]{1,0:T(8,128)(2,1)} %collective-permute-done.3, s32[]{:T(128)S(6)} %select_n.46), kind=kLoop, calls=%fused_computation.16 | loop fusion | bytes 2097156 | tf_op jit(solution)/shard_map/dynamic_slice | solution.py:98
  167.1 2.5 %collective-permute-start.5 = (bf16[512,1024]{1,0:T(8,128)(2,1)}, bf16[512,1024]{1,0:T(8,128)(2,1)}, u32[]{:S(2)}, u32[]{:S(2)}) collective-permute-start(bf16[512,1024]{1,0:T(8,128)(2,1)} %constant_dynamic-slice_fusion.2), channel_id=1, source_target_pairs={{0,1},{1,0},{2,3},{3,2},{4,5},{5,4},{6,7},{7,6},{8,9},{9,8},{10,11... | collective-permute-start | bytes 3145736 | tf_op jit(solution)/shard_map/ppermute | solution.py:102
  169.6 2.1 %fusion.2 = f32[512,1024]{1,0:T(8,128)S(1)} fusion(bf16[512,512]{1,0:T(8,128)(2,1)S(1)} %attend.1, bf16[512,4096]{1,0:T(8,128)(2,1)} %param.9, s32[]{:T(128)S(6)} %dynamic_slice.26), kind=kOutput, calls=%fused_computation.3 | convolution fusion | flops 536870912 | bytes 3670020 | tf_op jit(solution)/shard_map/dot_general | solution.py:120
  171.7 15.7 %collective-permute-done.2 = bf16[512,512]{1,0:T(8,128)(2,1)S(1)} collective-permute-done((bf16[512,512]{1,0:T(8,128)(2,1)S(1)}, bf16[512,512]{1,0:T(8,128)(2,1)S(1)}, u32[]{:S(2)}, u32[]{:S(2)}) %collective-permute-start.2) | collective-permute-done | bytes 524320 | tf_op jit(solution)/shard_map/ppermute | solution.py:116
  187.3 2.7 %collective-permute-start.4 = (bf16[512,512]{1,0:T(8,128)(2,1)S(1)}, bf16[512,512]{1,0:T(8,128)(2,1)S(1)}, u32[]{:S(2)}, u32[]{:S(2)}) collective-permute-start(bf16[512,512]{1,0:T(8,128)(2,1)S(1)} %collective-permute-done.2), channel_id=1, source_target_pairs={{0,1},{1,0},{2,3},{3,2},{4,5},{5,4},{6,7},{7,6},{8,9},{9,8},{10,11... | collective-permute-start | bytes 1572872 | tf_op jit(solution)/shard_map/ppermute | solution.py:118
  190.0 1.9 fusion
  192.0 0.0 collective-permute-done.1
  192.0 0.7 fusion.7
  192.7 3.0 %add_convert_fusion = bf16[512,1024]{1,0:T(8,128)(2,1)} fusion(f32[512,1024]{1,0:T(8,128)S(1)} %fusion, f32[512,1024]{1,0:T(8,128)S(1)} %fusion.2, f32[512,1024]{1,0:T(8,128)S(1)} %fusion.7, bf16[512,512]{1,0:T(8,128)(2,1)S(1)} %collective-permute-done.4, bf16[512,1024]{1,0:T(8,128)(2,1)} %collective-permute-done.5), kind=kOutput, calls=%fused_computation | convolution fusion | flops 538968064 | bytes 8912896 | tf_op jit(solution)/shard_map/dot_general | solution.py:120
  (18 shorter events, 0.1 us)
Async XLA Ops:
  2.5 119.8 %all-to-all-start = ((bf16[64,32,128]{2,1,0:T(8,128)(2,1)}), bf16[64,32,128]{2,1,0:T(8,128)(2,1)S(1)}, u32[]{:S(2)}, u32[]{:S(2)}) async-start(bf16[64,32,128]{2,1,0:T(8,128)(2,1)} %pad_maximum_fusion), calls=%async_computation | async-start | bytes 1048576 | tf_op jit(solution)/shard_map/all_to_all | solution.py:74
  15.1 107.4 %copy-start.4 = (s32[64]{0:T(128)S(1)}, s32[64]{0:T(128)}, u32[]{:S(2)}) copy-start(s32[64]{0:T(128)} %param.10) | copy-start | bytes 772
  18.3 146.5 %collective-permute-start.3 = (bf16[512,2048]{1,0:T(8,128)(2,1)}, bf16[512,2048]{1,0:T(8,128)(2,1)}, u32[]{:S(2)}, u32[]{:S(2)}) collective-permute-start(bf16[512,2048]{1,0:T(8,128)(2,1)} %constant_dynamic-slice_fusion), channel_id=1, source_target_pairs={{0,2},{2,0},{1,3},{3,1},{4,6},{6,4},{5,7},{7,5},{8,10},{10,8},{9,1... | collective-permute-start | bytes 6291464 | tf_op jit(solution)/shard_map/ppermute | solution.py:92
  122.4 1.1 copy-start.2
  125.8 10.3 %copy-start.3 = (bf16[512,4,128]{2,1,0:T(4,128)(2,1)S(1)}, bf16[512,4,128]{2,1,0:T(4,128)(2,1)}, u32[]{:S(2)}) copy-start(bf16[512,4,128]{2,1,0:T(4,128)(2,1)} %param.6) | copy-start | bytes 1572868
  125.8 10.3 %copy-start.5 = (s32[1,1,3]{2,1,0:T(1,128)S(1)}, s32[1,1,3]{2,1,0:T(1,128)}, u32[]{:S(2)}) copy-start(s32[1,1,3]{2,1,0:T(1,128)} %param.11) | copy-start | bytes 40
  125.8 27.5 %copy-start = (bf16[512,1,128]{2,0,1:T(8,128)(2,1)S(1)}, bf16[512,1,128]{2,0,1:T(8,128)(2,1)}, u32[]{:S(2)}) copy-start(bf16[512,1,128]{2,0,1:T(8,128)(2,1)} %param.7) | copy-start | bytes 393220
  125.8 27.5 %copy-start.1 = (bf16[512,1,128]{2,0,1:T(8,128)(2,1)S(1)}, bf16[512,1,128]{2,0,1:T(8,128)(2,1)}, u32[]{:S(2)}) copy-start(bf16[512,1,128]{2,0,1:T(8,128)(2,1)} %param.8) | copy-start | bytes 393220
  125.8 27.5 %all-to-all-start.1 = ((bf16[64,48,128]{2,1,0:T(8,128)(2,1)}), bf16[64,48,128]{2,1,0:T(8,128)(2,1)S(1)}, u32[]{:S(2)}, u32[]{:S(2)}) async-start(bf16[64,48,128]{2,1,0:T(8,128)(2,1)} %pack.1), calls=%async_computation.1 | async-start | bytes 1572864 | tf_op jit(solution)/shard_map/all_to_all | solution.py:88
  133.5 58.5 %collective-permute-start.1 = (bf16[512,1024]{1,0:T(8,128)(2,1)}, bf16[512,1024]{1,0:T(8,128)(2,1)S(1)}, u32[]{:S(2)}, u32[]{:S(2)}) collective-permute-start(bf16[512,1024]{1,0:T(8,128)(2,1)} %constant_dynamic-slice_fusion.1), channel_id=1, source_target_pairs={{0,1},{1,0},{2,3},{3,2},{4,5},{5,4},{6,7},{7,6},{8,9},{9,8},{10,11... | collective-permute-start | bytes 3145736 | tf_op jit(solution)/shard_map/ppermute | solution.py:101
  160.3 27.0 %collective-permute-start.2 = (bf16[512,512]{1,0:T(8,128)(2,1)S(1)}, bf16[512,512]{1,0:T(8,128)(2,1)S(1)}, u32[]{:S(2)}, u32[]{:S(2)}) collective-permute-start(bf16[512,512]{1,0:T(8,128)(2,1)S(1)} %attend.1), channel_id=1, source_target_pairs={{0,2},{2,0},{1,3},{3,1},{4,6},{6,4},{5,7},{7,5},{8,10},{10,8},{9,1... | collective-permute-start | bytes 1572872 | tf_op jit(solution)/shard_map/ppermute | solution.py:116
  167.1 25.6 %collective-permute-start.5 = (bf16[512,1024]{1,0:T(8,128)(2,1)}, bf16[512,1024]{1,0:T(8,128)(2,1)}, u32[]{:S(2)}, u32[]{:S(2)}) collective-permute-start(bf16[512,1024]{1,0:T(8,128)(2,1)} %constant_dynamic-slice_fusion.2), channel_id=1, source_target_pairs={{0,1},{1,0},{2,3},{3,2},{4,5},{5,4},{6,7},{7,6},{8,9},{9,8},{10,11... | collective-permute-start | bytes 3145736 | tf_op jit(solution)/shard_map/ppermute | solution.py:102
  169.6 22.4 %collective-permute-start = (bf16[512,512]{1,0:T(8,128)(2,1)S(1)}, bf16[512,512]{1,0:T(8,128)(2,1)S(1)}, u32[]{:S(2)}, u32[]{:S(2)}) collective-permute-start(bf16[512,512]{1,0:T(8,128)(2,1)S(1)} %attend.1), channel_id=1, source_target_pairs={{0,1},{1,0},{2,3},{3,2},{4,5},{5,4},{6,7},{7,6},{8,9},{9,8},{10,11... | collective-permute-start | bytes 1572872 | tf_op jit(solution)/shard_map/ppermute | solution.py:117
  187.3 5.4 %collective-permute-start.4 = (bf16[512,512]{1,0:T(8,128)(2,1)S(1)}, bf16[512,512]{1,0:T(8,128)(2,1)S(1)}, u32[]{:S(2)}, u32[]{:S(2)}) collective-permute-start(bf16[512,512]{1,0:T(8,128)(2,1)S(1)} %collective-permute-done.2), channel_id=1, source_target_pairs={{0,1},{1,0},{2,3},{3,2},{4,5},{5,4},{6,7},{7,6},{8,9},{9,8},{10,11... | collective-permute-start | bytes 1572872 | tf_op jit(solution)/shard_map/ppermute | solution.py:118

commit v2 on v1

v2 whole, which is shorter than its diff:
```python
import functools

import jax
import jax.numpy as jnp
from jax import lax
from jax.experimental import pallas as pl
from jax.experimental.pallas import tpu as pltpu
from jax.sharding import PartitionSpec as P

BLK = 512
HEAD = 128
TOPK = 3
PIECE = 16
NOTE = 8
VMEM_MB = 16
FACTOR = HEAD ** -0.5
LOG2E = 1.4426950408889634
PARTS = 2

SWAP_CORE = [(0, 1), (1, 0), (2, 3), (3, 2)]
SWAP_Z = [(0, 2), (2, 0), (1, 3), (3, 1)]


def along_x(step):
    return [(c, c // 16 * 16 + (c // 4 + step) % 4 * 4 + c % 4) for c in range(64)]


def along_y(step):
    return [(c, (c // 16 + step) % 4 * 16 + c % 16) for c in range(64)]


def along_z(step):
    pairs = []
    for xy in range(16):
        for z in range(8):
            to = (z + step) % 8
            for core in range(2):
                pairs.append(((xy * 4 + z % 4) * 4 + z // 4 * 2 + core, (xy * 4 + to % 4) * 4 + to // 4 * 2 + core))
    return pairs


def over_z(a, step):
    for _ in range(2):
        a = lax.ppermute(a, ("ctx", "head"), along_z(step))
    return a


def cut_kernel(w_ref, same_ref, other_ref, sems):
    share, cols = same_ref.shape
    at = lax.axis_index("head")
    row = pl.multiple_of(lax.shift_right_logical(lax.axis_index("ctx"), 2) * share, share)
    rows = pl.ds(row, share)
    same_col = pl.multiple_of(lax.bitwise_xor(at, 2) * cols, cols)
    other_col = pl.multiple_of(lax.bitwise_xor(at, 3) * cols, cols)
    copies = (
        pltpu.make_async_copy(w_ref.at[rows, pl.ds(same_col, cols)], same_ref, sems.at[0]),
        pltpu.make_async_copy(w_ref.at[rows, pl.ds(other_col, cols)], other_ref, sems.at[1]),
    )
    for copy in copies:
        copy.start()
    for copy in copies:
        copy.wait()


def spread_kernel(chosen_ref, k_ref, v_ref, out_ref):
    half = out_ref.shape[0] // 2
    lane = lax.broadcasted_iota(jnp.int32, (NOTE, HEAD), 1)
    note = jnp.where(lane == 0, chosen_ref[0], jnp.where(lane == 1, chosen_ref[1], chosen_ref[2]))
    note = note.astype(jnp.float32).astype(jnp.bfloat16)
    for c in range(half):
        piece = slice(c * PIECE, (c + 1) * PIECE)
        out_ref[c] = jnp.concatenate([k_ref[piece, :], note], axis=0)
        out_ref[half + c] = jnp.concatenate([v_ref[piece, :], note], axis=0)


def pack_kernel(order_ref, picked_ref, held_ref, same_ref, other_ref, out_ref, slot_of):
    n_dst = out_ref.shape[0]
    for s in range(n_dst):
        slot_of[order_ref[s]] = s
    for first in range(0, n_dst, 8):
        todo = [(d, j) for d in range(first, first + 8) for j in range(TOPK)]
        slots = [slot_of[picked_ref[d, j]] for d, j in todo]
        pieces = [held_ref[slot, :PIECE, :] for slot in slots]
        for (d, j), piece in zip(todo, pieces):
            out_ref[d, j * PIECE : (j + 1) * PIECE, :] = piece


def merge_x_kernel(*refs):
    out_ref = refs[-1]
    x = lax.bitwise_and(lax.shift_right_logical(lax.axis_index("ctx"), 2), 3)
    for k in range(4):
        at = lax.bitwise_and(x + (4 - k), 3)
        for a in range(2):
            out_ref[a, at] = refs[k][a]


def weights_kernel(*refs):
    *quarter_refs, w_ref, core_ref, out_ref, sems = refs
    half, cols = core_ref.shape
    y = lax.shift_right_logical(lax.axis_index("ctx"), 4)
    own = pl.ds(pl.multiple_of(lax.axis_index("head") * cols, cols), cols)
    copies = [
        pltpu.make_async_copy(w_ref.at[:, own], out_ref.at[0], sems.at[0]),
        pltpu.make_async_copy(core_ref, out_ref.at[1], sems.at[1]),
    ]
    for copy in copies:
        copy.start()
    for k, ref in enumerate(quarter_refs):
        at = pl.multiple_of(lax.bitwise_and(y + (4 - k), 3) * HEAD, HEAD)
        for a in range(2):
            out_ref[2 + a, pl.ds(at, HEAD), :] = ref[a].reshape(HEAD, cols)
    for copy in copies:
        copy.wait()


def attend_kernel(ok_ref, q_ref, k_ref, v_ref, got_ref, pass_ref, *out_refs, rows):
    out_refs = out_refs[:PARTS]
    half = got_ref.shape[0] // 2
    heads = q_ref.shape[0]
    contract = (((1,), (1,)), ((), ()))
    for h in range(heads):
        for r in range(0, BLK, rows):
            q = q_ref[h, r : r + rows, :]
            seen = r + rows
            near = lax.dot_general(q, k_ref[:seen, :], contract, preferred_element_type=jnp.float32)
            row = lax.broadcasted_iota(jnp.int32, near.shape, 0) + r
            col = lax.broadcasted_iota(jnp.int32, near.shape, 1)
            near = jnp.where(col <= row, near, -jnp.inf)
            far = []
            for j in range(TOPK):
                k_j = got_ref[:half, j * PIECE : (j + 1) * PIECE, :].reshape(BLK, HEAD)
                s = lax.dot_general(q, k_j, contract, preferred_element_type=jnp.float32)
                far.append(jnp.where(ok_ref[j] != 0, s, -jnp.inf))
            highest = jnp.max(near, axis=1, keepdims=True)
            for s in far:
                highest = jnp.maximum(highest, jnp.max(s, axis=1, keepdims=True))
            w = jnp.exp2((near - highest) * (FACTOR * LOG2E))
            total = jnp.sum(w, axis=1, keepdims=True)
            acc = jnp.dot(w.astype(jnp.bfloat16), v_ref[:seen, :], preferred_element_type=jnp.float32)
            for j in range(TOPK):
                v_j = got_ref[half:, j * PIECE : (j + 1) * PIECE, :].reshape(BLK, HEAD)
                w = jnp.exp2((far[j] - highest) * (FACTOR * LOG2E))
                total = total + jnp.sum(w, axis=1, keepdims=True)
                acc = acc + jnp.dot(w.astype(jnp.bfloat16), v_j, preferred_element_type=jnp.float32)
            per = heads // len(out_refs)
            part, col = out_refs[h // per], h % per * HEAD
            part[r : r + rows, col : col + HEAD] = (acc / total).astype(jnp.bfloat16)


def project_kernel(*refs):
    *part_refs, w_ref, out_ref, lhs, sems = refs
    wide = part_refs[0].shape[1]
    copies = [
        pltpu.make_async_copy(ref, lhs.at[i // PARTS, :, i % PARTS * wide : (i % PARTS + 1) * wide], sems.at[i])
        for i, ref in enumerate(part_refs)
    ]
    for copy in copies:
        copy.start()
    total = None
    for i in range(4):
        for copy in copies[i * PARTS : (i + 1) * PARTS]:
            copy.wait()
        product = jnp.dot(lhs[i], w_ref[i], preferred_element_type=jnp.float32)
        total = product if total is None else total + product
    out_ref[...] = total.astype(jnp.bfloat16)


def local(queries, keys, values, w_out, block_order, chosen):
    n_blocks = block_order.shape[0]
    ctx = lax.axis_index("ctx")
    head_at = lax.axis_index("head")
    cols = w_out.shape[1] // 4
    share = BLK // 16
    bf16 = jnp.bfloat16
    smem = pl.BlockSpec(memory_space=pltpu.SMEM)
    vmem = pl.BlockSpec(memory_space=pltpu.VMEM)
    hbm = pl.BlockSpec(memory_space=pl.ANY)
    params = pltpu.CompilerParams(vmem_limit_bytes=VMEM_MB * 1024 * 1024)
    k_own, v_own = keys[:, 0, :], values[:, 0, :]

    piece = jax.ShapeDtypeStruct((share, cols), bf16)
    far_same, far_other = pl.pallas_call(
        cut_kernel,
        out_shape=(piece, piece),
        in_specs=[hbm],
        out_specs=(vmem, vmem),
        scratch_shapes=[pltpu.SemaphoreType.DMA((2,))],
        name="cut",
    )(w_out)
    far_same = lax.ppermute(far_same, "head", SWAP_Z)
    far_other = lax.ppermute(far_other, "head", SWAP_Z)

    spread = pl.pallas_call(
        spread_kernel,
        out_shape=jax.ShapeDtypeStruct((n_blocks, PIECE + NOTE, HEAD), bf16),
        in_specs=[smem, vmem, vmem],
        out_specs=vmem,
        name="spread",
    )(chosen.reshape(TOPK), k_own, v_own)
    held = lax.all_to_all(spread, "ctx", 0, 0, tiled=True)

    both = jnp.stack([far_same, lax.ppermute(far_other, "head", SWAP_CORE)])
    quarter = pl.pallas_call(
        merge_x_kernel,
        out_shape=jax.ShapeDtypeStruct((2, 4, share, cols), bf16),
        in_specs=[vmem] * 4,
        out_specs=vmem,
        name="merge_x",
    )(both, *[lax.ppermute(both, "ctx", along_x(k)) for k in (1, 2, 3)])

    picked = held[:, PIECE, :TOPK].astype(jnp.int32)
    packed = pl.pallas_call(
        pack_kernel,
        out_shape=jax.ShapeDtypeStruct((n_blocks, TOPK * PIECE, HEAD), bf16),
        in_specs=[smem, smem, vmem, hbm, hbm],
        out_specs=vmem,
        scratch_shapes=[pltpu.SMEM((n_blocks,), jnp.int32)],
        name="pack",
    )(block_order, picked, held, far_same, far_other)
    got = lax.all_to_all(packed, "ctx", 0, 0, tiled=True)

    own = lax.dynamic_slice_in_dim(block_order, ctx, 1)
    ok = (chosen[0, 0] != own).astype(jnp.int32)
    q = jnp.transpose(queries, (1, 0, 2))
    part = jax.ShapeDtypeStruct((BLK, 4 // PARTS * HEAD), bf16)
    *a_own, quarter = pl.pallas_call(
        functools.partial(attend_kernel, rows=256),
        out_shape=(part,) * PARTS + (jax.ShapeDtypeStruct(quarter.shape, bf16),),
        in_specs=[smem, vmem, vmem, vmem, vmem, hbm],
        out_specs=(vmem,) * PARTS + (hbm,),
        input_output_aliases={5: PARTS},
        compiler_params=params,
        cost_estimate=pl.CostEstimate(flops=1 << 20, bytes_accessed=1 << 10, transcendentals=0),
        name="attend",
    )(ok, q, k_own, v_own, got, quarter)

    a_z = [over_z(a, step) for a, step in zip(a_own, (2, -2))]
    a_core = [lax.ppermute(a, "head", SWAP_CORE) for a in a_own]
    a_zc = [lax.ppermute(a, "head", SWAP_CORE) for a in a_z]
    w_core = lax.dynamic_slice_in_dim(w_out, lax.bitwise_xor(head_at, 1) * cols, cols, axis=1)
    w_core = lax.ppermute(w_core, "head", SWAP_CORE)
    weights = pl.pallas_call(
        weights_kernel,
        out_shape=jax.ShapeDtypeStruct((4, BLK, cols), bf16),
        in_specs=[vmem] * 4 + [hbm] * 2,
        out_specs=vmem,
        scratch_shapes=[pltpu.SemaphoreType.DMA((2,))],
        compiler_params=params,
        name="weights",
    )(quarter, *[lax.ppermute(quarter, "ctx", along_y(k)) for k in (1, 2, 3)], w_out, w_core)

    return pl.pallas_call(
        project_kernel,
        out_shape=jax.ShapeDtypeStruct((BLK, cols), bf16),
        in_specs=[vmem] * (4 * PARTS) + [vmem],
        out_specs=vmem,
        scratch_shapes=[pltpu.VMEM((4, BLK, 4 * HEAD), bf16), pltpu.SemaphoreType.DMA((4 * PARTS,))],
        compiler_params=params,
        cost_estimate=pl.CostEstimate(flops=1 << 31, bytes_accessed=4 << 20, transcendentals=0),
        name="project",
    )(*a_own, *a_core, *a_z, *a_zc, weights)


def solution(mesh):
    in_specs = (
        P("ctx", "head", None),
        P("ctx", "head", None),
        P("ctx", "head", None),
        P("head", None),
        P(),
        P("ctx", "head", None),
    )
    out_specs = P("ctx", "head")
    return jax.shard_map(local, mesh=mesh, in_specs=in_specs, out_specs=out_specs, check_vma=False)
```

time: 196 us -> 115 us (0.59)
  waiting for transfers between devices: 132 us -> 25.5 us
  starting transfers between devices: 33.2 us -> 58 us
  Pallas kernels: 9.27 us -> 18.9 us
  matrix products: 7.71 us -> 0 us
  other arithmetic: 3.36 us -> 1.38 us
    all_to_all x1, waiting for transfers between devices: 99.9 us -> 7.84 us  [local(): held = lax.all_to_all(spread, 'ctx', 0, 0, tiled=True)]
    ppermute x6 -> x18, starting transfers between devices: 15.8 us -> 36 us  [the longest x2 8.37 us: local(): a_core = [lax.ppermute(a, 'head', SWAP_CORE) for a in a_own]]
    all_to_all x1, waiting for transfers between devices: 16.5 us -> 0.01 us  [local(): got = lax.all_to_all(packed, 'ctx', 0, 0, tiled=True)]
    pallas_call x1 -> x6, Pallas kernels: 7.03 us -> 16.5 us  [the longest x1 7.03 us: local(): pl.pallas_call(functools.partial(attend_kernel, rows=256), out_shape=(par...]
    dot_general x4 -> x0, matrix products: 7.71 us -> none  [the longest x1 2.96 us: local(): dot(a_zc, w_zc)]
    unnamed x13 -> x35, local copies, waits for them, and re-layouts: 0.09 us -> 7.08 us
    dynamic_slice x4 -> x2, local copies, waits for them, and re-layouts: 8.91 us -> 2.92 us  [the longest x1 2.27 us: local(): lax.dynamic_slice_in_dim(w_out, lax.bitwise_xor(head_at, 1) * cols, cols,...]
    all_to_all x1, starting transfers between devices: 4.79 us -> 9.45 us  [local(): got = lax.all_to_all(packed, 'ctx', 0, 0, tiled=True)]
  transfers between devices with their start and end apart: 8 -> 20, of which waited for: 3 -> 8; matrix products, arithmetic and copies ran while one was open for 8% -> 4% of each run, Pallas kernels for 5% -> 10%
where the time goes in v2:
time: 115 us; the launch traced here: 114 us
  starting transfers between devices  58 us (50%)
  waiting for transfers between devices  25.5 us (22%)
  Pallas kernels  18.9 us (16%)
  local copies, waits for them, and re-layouts  10 us (9%)
  other arithmetic  1.38 us (1%)
    all_to_all x1, starting transfers between devices, local(): held = lax.all_to_all(spread, 'ctx', 0, 0, tiled=True)  12.6 us
    all_to_all x1, starting transfers between devices, local(): got = lax.all_to_all(packed, 'ctx', 0, 0, tiled=True)  9.45 us
    ppermute x4, waiting for transfers between devices, over_z(): a = lax.ppermute(a, ('ctx', 'head'), along_z(step))  8.54 us
    ppermute x2, starting transfers between devices, local(): a_core = [lax.ppermute(a, 'head', SWAP_CORE) for a in a_own]  8.37 us
    all_to_all x1, waiting for transfers between devices, local(): held = lax.all_to_all(spread, 'ctx', 0, 0, tiled=True)  7.84 us
    unnamed x35, local copies, waits for them, and re-layouts  7.08 us
    pallas_call x1, Pallas kernels, local(): pl.pallas_call(functools.partial(attend_kernel, rows=256), out_shape=(par...  7.03 us
    ppermute x4, starting transfers between devices, over_z(): a = lax.ppermute(a, ('ctx', 'head'), along_z(step))  7.01 us
  transfers between devices with their start and end apart: 20, of which 8 were waited for; matrix products, arithmetic and copies ran while one was open for 4% of the time, Pallas kernels for 10%

profile of v2, /device:TPU:1, one launch (start us, length us, event | category | flops | bytes accessed | tf_op | source)
XLA Modules:
  0.0 114.2 jit_solution(12190875026074318593)
XLA Ops:
  0.0 1.8 %spread.1 = bf16[64,24,128]{2,1,0:T(8,128)(2,1)} custom-call(s32[3]{0:T(128)} %bitcast.19, bf16[512,128]{1,0:T(8,128)(2,1)} %bitcast.12, bf16[512,128]{1,0:T(8,128)(2,1)} %bitcast.14), custom_call_target="tpu_custom_call" | custom-call | tf_op jit(solution)/shard_map/spread/pallas_call | solution.py:193
  1.8 12.6 %all-to-all-start = ((bf16[64,24,128]{2,1,0:T(8,128)(2,1)}), bf16[64,24,128]{2,1,0:T(8,128)(2,1)S(1)}, u32[]{:S(2)}, u32[]{:S(2)}) async-start(bf16[64,24,128]{2,1,0:T(8,128)(2,1)} %spread.1), calls=%async_computation | async-start | bytes 786432 | tf_op jit(solution)/shard_map/all_to_all | solution.py:200
  14.4 1.6 %cut.1 = (bf16[32,1024]{1,0:T(8,128)(2,1)}, bf16[32,1024]{1,0:T(8,128)(2,1)}) custom-call(bf16[512,4096]{1,0:T(8,128)(2,1)} %refs_4_.1), custom_call_target="tpu_custom_call" | custom-call | tf_op jit(solution)/shard_map/cut/pallas_call | solution.py:182
  16.0 4.3 %collective-permute-start.1 = (bf16[32,1024]{1,0:T(8,128)(2,1)}, bf16[32,1024]{1,0:T(8,128)(2,1)S(1)}, u32[]{:S(2)}, u32[]{:S(2)}) collective-permute-start(bf16[32,1024]{1,0:T(8,128)(2,1)} %get-tuple-element.11), channel_id=1, source_target_pairs={{0,2},{2,0},{1,3},{3,1},{4,6},{6,4},{5,7},{7,5},{8,10},{10,8},{9,1... | collective-permute-start | bytes 196616 | tf_op jit(solution)/shard_map/ppermute | solution.py:191
  20.3 1.2 %collective-permute-start = (bf16[32,1024]{1,0:T(8,128)(2,1)}, bf16[32,1024]{1,0:T(8,128)(2,1)S(1)}, u32[]{:S(2)}, u32[]{:S(2)}) collective-permute-start(bf16[32,1024]{1,0:T(8,128)(2,1)} %get-tuple-element.10), channel_id=1, source_target_pairs={{0,2},{2,0},{1,3},{3,1},{4,6},{6,4},{5,7},{7,5},{8,10},{10,8},{9,1... | collective-permute-start | bytes 196616 | tf_op jit(solution)/shard_map/ppermute | solution.py:190
  21.5 7.8 %all-to-all-done.held_ref = bf16[64,24,128]{2,1,0:T(8,128)(2,1)S(1)} async-done(((bf16[64,24,128]{2,1,0:T(8,128)(2,1)}), bf16[64,24,128]{2,1,0:T(8,128)(2,1)S(1)}, u32[]{:S(2)}, u32[]{:S(2)}) %all-to-all-start) | async-done | bytes 393248 | tf_op jit(solution)/shard_map/all_to_all | solution.py:200
  30.7 2.4 %pack.1 = bf16[64,48,128]{2,1,0:T(8,128)(2,1)} custom-call(s32[64]{0:T(128)} %order_ref.1, s32[64,3]{1,0:T(8,128)} %bitcast.17, bf16[64,24,128]{2,1,0:T(8,128)(2,1)} %copy-done.6, bf16[32,1024]{1,0:T(8,128)(2,1)} %copy-done.9, bf16[32,1024]{1,0:T(8,128)(2,1)} %copy-done.14), custom_call_target="tpu_custom_call" | custom-call | tf_op jit(solution)/shard_map/pack/pallas_call | solution.py:212
  33.1 9.5 %all-to-all-start.1 = ((bf16[64,48,128]{2,1,0:T(8,128)(2,1)}), bf16[64,48,128]{2,1,0:T(8,128)(2,1)S(1)}, u32[]{:S(2)}, u32[]{:S(2)}) async-start(bf16[64,48,128]{2,1,0:T(8,128)(2,1)} %pack.1), calls=%async_computation.1 | async-start | bytes 1572864 | tf_op jit(solution)/shard_map/all_to_all | solution.py:220
  42.6 2.3 %constant_dynamic-slice_fusion = bf16[512,1024]{1,0:T(8,128)(2,1)} fusion(bf16[512,4096]{1,0:T(8,128)(2,1)} %refs_4_.1, s32[]{:T(128)S(6)} %select_n.7), kind=kLoop, calls=%fused_computation.4 | loop fusion | bytes 2097156 | tf_op jit(solution)/shard_map/dynamic_slice | solution.py:240
  44.8 2.9 %collective-permute-start.17 = (bf16[512,1024]{1,0:T(8,128)(2,1)}, bf16[512,1024]{1,0:T(8,128)(2,1)S(1)}, u32[]{:S(2)}, u32[]{:S(2)}) collective-permute-start(bf16[512,1024]{1,0:T(8,128)(2,1)} %constant_dynamic-slice_fusion), channel_id=1, source_target_pairs={{0,1},{1,0},{2,3},{3,2},{4,5},{5,4},{6,7},{7,6},{8,9},{9,8},{10,11... | collective-permute-start | bytes 3145736 | tf_op jit(solution)/shard_map/ppermute | solution.py:241
  48.5 1.9 %collective-permute-done.2 = bf16[32,1024]{1,0:T(8,128)(2,1)S(1)} collective-permute-done((bf16[32,1024]{1,0:T(8,128)(2,1)}, bf16[32,1024]{1,0:T(8,128)(2,1)S(1)}, u32[]{:S(2)}, u32[]{:S(2)}) %collective-permute-start.2) | collective-permute-done | bytes 65568 | tf_op jit(solution)/shard_map/ppermute | solution.py:202
  50.4 1.4 %collective-permute-start.3 = (bf16[2,32,1024]{2,1,0:T(8,128)(2,1)S(1)}, bf16[2,32,1024]{2,1,0:T(8,128)(2,1)S(1)}, u32[]{:S(2)}, u32[]{:S(2)}) collective-permute-start(bf16[2,32,1024]{2,1,0:T(8,128)(2,1)S(1)} %pad_maximum_fusion.refs_0_), channel_id=1, source_target_pairs={{0,16},{4,20},{8,24},{12,28},{16,32},{20,36},{24,40},{28,44},{32,4... | collective-permute-start | bytes 393224 | tf_op jit(solution)/shard_map/ppermute | solution.py:209
  51.8 2.4 %collective-permute-start.4 = (bf16[2,32,1024]{2,1,0:T(8,128)(2,1)S(1)}, bf16[2,32,1024]{2,1,0:T(8,128)(2,1)S(1)}, u32[]{:S(2)}, u32[]{:S(2)}) collective-permute-start(bf16[2,32,1024]{2,1,0:T(8,128)(2,1)S(1)} %pad_maximum_fusion.refs_0_), channel_id=1, source_target_pairs={{0,32},{4,36},{8,40},{12,44},{16,48},{20,52},{24,56},{28,60},{32,0... | collective-permute-start | bytes 393224 | tf_op jit(solution)/shard_map/ppermute | solution.py:209
  54.2 1.2 %collective-permute-start.5 = (bf16[2,32,1024]{2,1,0:T(8,128)(2,1)S(1)}, bf16[2,32,1024]{2,1,0:T(8,128)(2,1)S(1)}, u32[]{:S(2)}, u32[]{:S(2)}) collective-permute-start(bf16[2,32,1024]{2,1,0:T(8,128)(2,1)S(1)} %pad_maximum_fusion.refs_0_), channel_id=1, source_target_pairs={{0,48},{4,52},{8,56},{12,60},{16,0},{20,4},{24,8},{28,12},{32,16},... | collective-permute-start | bytes 393224 | tf_op jit(solution)/shard_map/ppermute | solution.py:209
  56.0 1.7 %collective-permute-done.3.refs_1_ = bf16[2,32,1024]{2,1,0:T(8,128)(2,1)S(1)} collective-permute-done((bf16[2,32,1024]{2,1,0:T(8,128)(2,1)S(1)}, bf16[2,32,1024]{2,1,0:T(8,128)(2,1)S(1)}, u32[]{:S(2)}, u32[]{:S(2)}) %collective-permute-start.3) | collective-permute-done | bytes 131104 | tf_op jit(solution)/shard_map/ppermute | solution.py:209
  57.7 4.6 %collective-permute-done.4.refs_2_ = bf16[2,32,1024]{2,1,0:T(8,128)(2,1)S(1)} collective-permute-done((bf16[2,32,1024]{2,1,0:T(8,128)(2,1)S(1)}, bf16[2,32,1024]{2,1,0:T(8,128)(2,1)S(1)}, u32[]{:S(2)}, u32[]{:S(2)}) %collective-permute-start.4) | collective-permute-done | bytes 131104 | tf_op jit(solution)/shard_map/ppermute | solution.py:209
  63.6 1.9 %merge_x.1.pass_ref = bf16[2,4,32,1024]{3,2,1,0:T(8,128)(2,1)} custom-call(bf16[2,32,1024]{2,1,0:T(8,128)(2,1)} %copy-done.8, bf16[2,32,1024]{2,1,0:T(8,128)(2,1)} %copy-done.11, bf16[2,32,1024]{2,1,0:T(8,128)(2,1)} %copy-done.12, bf16[2,32,1024]{2,1,0:T(8,128)(2,1)} %copy-done.13), custom_call_target="tpu_custom_call" | custom-call | tf_op jit(solution)/shard_map/merge_x/pallas_call | solution.py:203
  66.6 7.0 %attend.1 = (bf16[512,256]{1,0:T(8,128)(2,1)S(1)}, bf16[512,256]{1,0:T(8,128)(2,1)S(1)}, bf16[2,4,32,1024]{3,2,1,0:T(8,128)(2,1)S(1)}) custom-call(s32[3]{0:T(128)S(1)} %compare_convert_fusion.ok_ref, bf16[4,512,128]{2,1,0:T(8,128)(2,1)S(1)} %bitcast.11, bf16[512,128]{1,0:T(8,128)(2,1)S(1)} %bitcast.13, ...), custom_call_target="tpu_custom_call", output_to_operand_aliasing={{2}: (5, {})} | custom-call | flops 1048576 | bytes 1024 | tf_op jit(solution)/shard_map/attend/pallas_call | solution.py:226
  73.6 3.2 %collective-permute-start.8 = (bf16[512,256]{1,0:T(8,128)(2,1)S(1)}, bf16[512,256]{1,0:T(8,128)(2,1)S(1)}, u32[]{:S(2)}, u32[]{:S(2)}) collective-permute-start(bf16[512,256]{1,0:T(8,128)(2,1)S(1)} %get-tuple-element.12.refs_0_), channel_id=1, source_target_pairs={{0,8},{1,9},{4,12},{5,13},{8,2},{9,3},{12,6},{13,7},{2,10},{3,11},... | collective-permute-start | bytes 786440 | tf_op jit(solution)/shard_map/ppermute | solution.py:44
  76.8 1.5 %collective-permute-start.10 = (bf16[512,256]{1,0:T(8,128)(2,1)S(1)}, bf16[512,256]{1,0:T(8,128)(2,1)S(1)}, u32[]{:S(2)}, u32[]{:S(2)}) collective-permute-start(bf16[512,256]{1,0:T(8,128)(2,1)S(1)} %get-tuple-element.13.refs_1_), channel_id=1, source_target_pairs={{0,10},{1,11},{4,14},{5,15},{8,0},{9,1},{12,4},{13,5},{2,8},{3,9},... | collective-permute-start | bytes 786440 | tf_op jit(solution)/shard_map/ppermute | solution.py:44
  78.3 1.5 %collective-permute-start.14 = (bf16[2,4,32,1024]{3,2,1,0:T(8,128)(2,1)S(1)}, bf16[2,4,32,1024]{3,2,1,0:T(8,128)(2,1)S(1)}, u32[]{:S(2)}, u32[]{:S(2)}) collective-permute-start(bf16[2,4,32,1024]{3,2,1,0:T(8,128)(2,1)S(1)} %get-tuple-element.14.refs_0_), channel_id=1, source_target_pairs={{0,64},{4,68},{8,72},{12,76},{16,80},{20,84},{24,88},{28,92},{32,9... | collective-permute-start | bytes 1572872 | tf_op jit(solution)/shard_map/ppermute | solution.py:250
  79.8 2.6 %collective-permute-start.15 = (bf16[2,4,32,1024]{3,2,1,0:T(8,128)(2,1)S(1)}, bf16[2,4,32,1024]{3,2,1,0:T(8,128)(2,1)S(1)}, u32[]{:S(2)}, u32[]{:S(2)}) collective-permute-start(bf16[2,4,32,1024]{3,2,1,0:T(8,128)(2,1)S(1)} %get-tuple-element.14.refs_0_), channel_id=1, source_target_pairs={{0,128},{4,132},{8,136},{12,140},{16,144},{20,148},{24,152},{28,15... | collective-permute-start | bytes 1572872 | tf_op jit(solution)/shard_map/ppermute | solution.py:250
  82.4 1.1 collective-permute-start.16
  84.3 3.0 %collective-permute-done.8 = bf16[512,256]{1,0:T(8,128)(2,1)S(1)} collective-permute-done((bf16[512,256]{1,0:T(8,128)(2,1)S(1)}, bf16[512,256]{1,0:T(8,128)(2,1)S(1)}, u32[]{:S(2)}, u32[]{:S(2)}) %collective-permute-start.8) | collective-permute-done | bytes 262176 | tf_op jit(solution)/shard_map/ppermute | solution.py:44
  87.3 1.7 %collective-permute-done.10 = bf16[512,256]{1,0:T(8,128)(2,1)S(1)} collective-permute-done((bf16[512,256]{1,0:T(8,128)(2,1)S(1)}, bf16[512,256]{1,0:T(8,128)(2,1)S(1)}, u32[]{:S(2)}, u32[]{:S(2)}) %collective-permute-start.10) | collective-permute-done | bytes 262176 | tf_op jit(solution)/shard_map/ppermute | solution.py:44
  89.0 2.3 %collective-permute-start.11 = (bf16[512,256]{1,0:T(8,128)(2,1)S(1)}, bf16[512,256]{1,0:T(8,128)(2,1)S(1)}, u32[]{:S(2)}, u32[]{:S(2)}) collective-permute-start(bf16[512,256]{1,0:T(8,128)(2,1)S(1)} %collective-permute-done.10), channel_id=1, source_target_pairs={{0,10},{1,11},{4,14},{5,15},{8,0},{9,1},{12,4},{13,5},{2,8},{3,9},... | collective-permute-start | bytes 786440 | tf_op jit(solution)/shard_map/ppermute | solution.py:44
  91.3 3.8 %collective-permute-done.9.refs_4_ = bf16[512,256]{1,0:T(8,128)(2,1)S(1)} collective-permute-done((bf16[512,256]{1,0:T(8,128)(2,1)S(1)}, bf16[512,256]{1,0:T(8,128)(2,1)S(1)}, u32[]{:S(2)}, u32[]{:S(2)}) %collective-permute-start.9) | collective-permute-done | bytes 262176 | tf_op jit(solution)/shard_map/ppermute | solution.py:44
  95.1 3.4 %collective-permute-start.6 = (bf16[512,256]{1,0:T(8,128)(2,1)S(1)}, bf16[512,256]{1,0:T(8,128)(2,1)S(1)}, u32[]{:S(2)}, u32[]{:S(2)}) collective-permute-start(bf16[512,256]{1,0:T(8,128)(2,1)S(1)} %get-tuple-element.12.refs_0_), channel_id=1, source_target_pairs={{0,1},{1,0},{2,3},{3,2},{4,5},{5,4},{6,7},{7,6},{8,9},{9,8},{10,11... | collective-permute-start | bytes 786440 | tf_op jit(solution)/shard_map/ppermute | solution.py:238
  98.5 5.0 %collective-permute-start.7 = (bf16[512,256]{1,0:T(8,128)(2,1)S(1)}, bf16[512,256]{1,0:T(8,128)(2,1)S(1)}, u32[]{:S(2)}, u32[]{:S(2)}) collective-permute-start(bf16[512,256]{1,0:T(8,128)(2,1)S(1)} %get-tuple-element.13.refs_1_), channel_id=1, source_target_pairs={{0,1},{1,0},{2,3},{3,2},{4,5},{5,4},{6,7},{7,6},{8,9},{9,8},{10,11... | collective-permute-start | bytes 786440 | tf_op jit(solution)/shard_map/ppermute | solution.py:238
  104.4 2.1 %collective-permute-start.13 = (bf16[512,256]{1,0:T(8,128)(2,1)S(1)}, bf16[512,256]{1,0:T(8,128)(2,1)S(1)}, u32[]{:S(2)}, u32[]{:S(2)}) collective-permute-start(bf16[512,256]{1,0:T(8,128)(2,1)S(1)} %collective-permute-done.11.refs_5_), channel_id=1, source_target_pairs={{0,1},{1,0},{2,3},{3,2},{4,5},{5,4},{6,7},{7,6},{8,9},{9,8},{10,11... | collective-permute-start | bytes 786440 | tf_op jit(solution)/shard_map/ppermute | solution.py:239
  106.5 2.2 %copy-done = bf16[512,4096]{1,0:T(8,128)(2,1)S(1)} copy-done((bf16[512,4096]{1,0:T(8,128)(2,1)S(1)}, bf16[512,4096]{1,0:T(8,128)(2,1)}, u32[]{:S(2)}) %copy-start) | copy-done | bytes 4194328
  110.2 3.8 %project.1 = bf16[512,1024]{1,0:T(8,128)(2,1)} custom-call(bf16[512,256]{1,0:T(8,128)(2,1)S(1)} %get-tuple-element.12.refs_0_, bf16[512,256]{1,0:T(8,128)(2,1)S(1)} %get-tuple-element.13.refs_1_, bf16[512,256]{1,0:T(8,128)(2,1)S(1)} %collective-permute-done.6.refs_2_, bf16[512,256]{1,0:T(8,128)(2,1)S(1)} %collective-permute-done.7.refs_3_, ...), custom_call_target="tpu_custom_call" | custom-call | flops 2147483648 | bytes 4194304 | tf_op jit(solution)/shard_map/project/pallas_call | solution.py:252
  (55 shorter events, 8.3 us)
Async XLA Ops:
  1.8 27.5 %all-to-all-start = ((bf16[64,24,128]{2,1,0:T(8,128)(2,1)}), bf16[64,24,128]{2,1,0:T(8,128)(2,1)S(1)}, u32[]{:S(2)}, u32[]{:S(2)}) async-start(bf16[64,24,128]{2,1,0:T(8,128)(2,1)} %spread.1), calls=%async_computation | async-start | bytes 786432 | tf_op jit(solution)/shard_map/all_to_all | solution.py:200
  14.3 33.4 %copy-start.15 = (s32[64]{0:T(128)S(1)}, s32[64]{0:T(128)}, u32[]{:S(2)}) copy-start(s32[64]{0:T(128)} %order_ref.1) | copy-start | bytes 772
  14.4 34.1 %copy-start.7 = (bf16[512,4,128]{2,1,0:T(4,128)(2,1)S(1)}, bf16[512,4,128]{2,1,0:T(4,128)(2,1)}, u32[]{:S(2)}) copy-start(bf16[512,4,128]{2,1,0:T(4,128)(2,1)} %param.6) | copy-start | bytes 1572868
  16.0 39.4 %copy-start.16 = (s32[1,1,3]{2,1,0:T(1,128)S(1)}, s32[1,1,3]{2,1,0:T(1,128)}, u32[]{:S(2)}) copy-start(s32[1,1,3]{2,1,0:T(1,128)} %param.11) | copy-start | bytes 40
  16.0 49.6 %copy-start.4 = (bf16[512,1,128]{2,0,1:T(8,128)(2,1)S(1)}, bf16[512,1,128]{2,0,1:T(8,128)(2,1)}, u32[]{:S(2)}) copy-start(bf16[512,1,128]{2,0,1:T(8,128)(2,1)} %param.7) | copy-start | bytes 393220
  16.0 49.5 %copy-start.5 = (bf16[512,1,128]{2,0,1:T(8,128)(2,1)S(1)}, bf16[512,1,128]{2,0,1:T(8,128)(2,1)}, u32[]{:S(2)}) copy-start(bf16[512,1,128]{2,0,1:T(8,128)(2,1)} %param.8) | copy-start | bytes 393220
  16.0 14.0 %collective-permute-start.1 = (bf16[32,1024]{1,0:T(8,128)(2,1)}, bf16[32,1024]{1,0:T(8,128)(2,1)S(1)}, u32[]{:S(2)}, u32[]{:S(2)}) collective-permute-start(bf16[32,1024]{1,0:T(8,128)(2,1)} %get-tuple-element.11), channel_id=1, source_target_pairs={{0,2},{2,0},{1,3},{3,1},{4,6},{6,4},{5,7},{7,5},{8,10},{10,8},{9,1... | collective-permute-start | bytes 196616 | tf_op jit(solution)/shard_map/ppermute | solution.py:191
  20.3 9.7 %collective-permute-start = (bf16[32,1024]{1,0:T(8,128)(2,1)}, bf16[32,1024]{1,0:T(8,128)(2,1)S(1)}, u32[]{:S(2)}, u32[]{:S(2)}) collective-permute-start(bf16[32,1024]{1,0:T(8,128)(2,1)} %get-tuple-element.10), channel_id=1, source_target_pairs={{0,2},{2,0},{1,3},{3,1},{4,6},{6,4},{5,7},{7,5},{8,10},{10,8},{9,1... | collective-permute-start | bytes 196616 | tf_op jit(solution)/shard_map/ppermute | solution.py:190
  33.1 17.3 %copy-start.10 = (bf16[32,1024]{1,0:T(8,128)(2,1)S(1)}, bf16[32,1024]{1,0:T(8,128)(2,1)}, u32[]{:S(2)}) copy-start(bf16[32,1024]{1,0:T(8,128)(2,1)} %copy-done.9) | copy-start | bytes 196612
  33.1 32.4 %all-to-all-start.1 = ((bf16[64,48,128]{2,1,0:T(8,128)(2,1)}), bf16[64,48,128]{2,1,0:T(8,128)(2,1)S(1)}, u32[]{:S(2)}, u32[]{:S(2)}) async-start(bf16[64,48,128]{2,1,0:T(8,128)(2,1)} %pack.1), calls=%async_computation.1 | async-start | bytes 1572864 | tf_op jit(solution)/shard_map/all_to_all | solution.py:220
  44.8 37.6 %collective-permute-start.17 = (bf16[512,1024]{1,0:T(8,128)(2,1)}, bf16[512,1024]{1,0:T(8,128)(2,1)S(1)}, u32[]{:S(2)}, u32[]{:S(2)}) collective-permute-start(bf16[512,1024]{1,0:T(8,128)(2,1)} %constant_dynamic-slice_fusion), channel_id=1, source_target_pairs={{0,1},{1,0},{2,3},{3,2},{4,5},{5,4},{6,7},{7,6},{8,9},{9,8},{10,11... | collective-permute-start | bytes 3145736 | tf_op jit(solution)/shard_map/ppermute | solution.py:241
  47.8 2.6 %collective-permute-start.2 = (bf16[32,1024]{1,0:T(8,128)(2,1)}, bf16[32,1024]{1,0:T(8,128)(2,1)S(1)}, u32[]{:S(2)}, u32[]{:S(2)}) collective-permute-start(bf16[32,1024]{1,0:T(8,128)(2,1)} %copy-done.14), channel_id=1, source_target_pairs={{0,1},{1,0},{2,3},{3,2},{4,5},{5,4},{6,7},{7,6},{8,9},{9,8},{10,11... | collective-permute-start | bytes 196616 | tf_op jit(solution)/shard_map/ppermute | solution.py:202
  50.4 11.9 %copy-start.8 = (bf16[2,32,1024]{2,1,0:T(8,128)(2,1)}, bf16[2,32,1024]{2,1,0:T(8,128)(2,1)S(1)}, u32[]{:S(2)}) copy-start(bf16[2,32,1024]{2,1,0:T(8,128)(2,1)S(1)} %pad_maximum_fusion.refs_0_) | copy-start | bytes 393220
  50.4 7.3 %collective-permute-start.3 = (bf16[2,32,1024]{2,1,0:T(8,128)(2,1)S(1)}, bf16[2,32,1024]{2,1,0:T(8,128)(2,1)S(1)}, u32[]{:S(2)}, u32[]{:S(2)}) collective-permute-start(bf16[2,32,1024]{2,1,0:T(8,128)(2,1)S(1)} %pad_maximum_fusion.refs_0_), channel_id=1, source_target_pairs={{0,16},{4,20},{8,24},{12,28},{16,32},{20,36},{24,40},{28,44},{32,4... | collective-permute-start | bytes 393224 | tf_op jit(solution)/shard_map/ppermute | solution.py:209
  51.8 10.5 %collective-permute-start.4 = (bf16[2,32,1024]{2,1,0:T(8,128)(2,1)S(1)}, bf16[2,32,1024]{2,1,0:T(8,128)(2,1)S(1)}, u32[]{:S(2)}, u32[]{:S(2)}) collective-permute-start(bf16[2,32,1024]{2,1,0:T(8,128)(2,1)S(1)} %pad_maximum_fusion.refs_0_), channel_id=1, source_target_pairs={{0,32},{4,36},{8,40},{12,44},{16,48},{20,52},{24,56},{28,60},{32,0... | collective-permute-start | bytes 393224 | tf_op jit(solution)/shard_map/ppermute | solution.py:209
  54.2 8.2 %collective-permute-start.5 = (bf16[2,32,1024]{2,1,0:T(8,128)(2,1)S(1)}, bf16[2,32,1024]{2,1,0:T(8,128)(2,1)S(1)}, u32[]{:S(2)}, u32[]{:S(2)}) collective-permute-start(bf16[2,32,1024]{2,1,0:T(8,128)(2,1)S(1)} %pad_maximum_fusion.refs_0_), channel_id=1, source_target_pairs={{0,48},{4,52},{8,56},{12,60},{16,0},{20,4},{24,8},{28,12},{32,16},... | collective-permute-start | bytes 393224 | tf_op jit(solution)/shard_map/ppermute | solution.py:209
  57.7 4.6 %copy-start.11 = (bf16[2,32,1024]{2,1,0:T(8,128)(2,1)}, bf16[2,32,1024]{2,1,0:T(8,128)(2,1)S(1)}, u32[]{:S(2)}) copy-start(bf16[2,32,1024]{2,1,0:T(8,128)(2,1)S(1)} %collective-permute-done.3.refs_1_) | copy-start | bytes 393220
  65.6 1.0 copy-start.1
  73.6 13.7 %collective-permute-start.8 = (bf16[512,256]{1,0:T(8,128)(2,1)S(1)}, bf16[512,256]{1,0:T(8,128)(2,1)S(1)}, u32[]{:S(2)}, u32[]{:S(2)}) collective-permute-start(bf16[512,256]{1,0:T(8,128)(2,1)S(1)} %get-tuple-element.12.refs_0_), channel_id=1, source_target_pairs={{0,8},{1,9},{4,12},{5,13},{8,2},{9,3},{12,6},{13,7},{2,10},{3,11},... | collective-permute-start | bytes 786440 | tf_op jit(solution)/shard_map/ppermute | solution.py:44
  76.8 12.2 %collective-permute-start.10 = (bf16[512,256]{1,0:T(8,128)(2,1)S(1)}, bf16[512,256]{1,0:T(8,128)(2,1)S(1)}, u32[]{:S(2)}, u32[]{:S(2)}) collective-permute-start(bf16[512,256]{1,0:T(8,128)(2,1)S(1)} %get-tuple-element.13.refs_1_), channel_id=1, source_target_pairs={{0,10},{1,11},{4,14},{5,15},{8,0},{9,1},{12,4},{13,5},{2,8},{3,9},... | collective-permute-start | bytes 786440 | tf_op jit(solution)/shard_map/ppermute | solution.py:44
  78.3 25.2 %collective-permute-start.14 = (bf16[2,4,32,1024]{3,2,1,0:T(8,128)(2,1)S(1)}, bf16[2,4,32,1024]{3,2,1,0:T(8,128)(2,1)S(1)}, u32[]{:S(2)}, u32[]{:S(2)}) collective-permute-start(bf16[2,4,32,1024]{3,2,1,0:T(8,128)(2,1)S(1)} %get-tuple-element.14.refs_0_), channel_id=1, source_target_pairs={{0,64},{4,68},{8,72},{12,76},{16,80},{20,84},{24,88},{28,92},{32,9... | collective-permute-start | bytes 1572872 | tf_op jit(solution)/shard_map/ppermute | solution.py:250
  79.8 24.6 %collective-permute-start.15 = (bf16[2,4,32,1024]{3,2,1,0:T(8,128)(2,1)S(1)}, bf16[2,4,32,1024]{3,2,1,0:T(8,128)(2,1)S(1)}, u32[]{:S(2)}, u32[]{:S(2)}) collective-permute-start(bf16[2,4,32,1024]{3,2,1,0:T(8,128)(2,1)S(1)} %get-tuple-element.14.refs_0_), channel_id=1, source_target_pairs={{0,128},{4,132},{8,136},{12,140},{16,144},{20,148},{24,152},{28,15... | collective-permute-start | bytes 1572872 | tf_op jit(solution)/shard_map/ppermute | solution.py:250
  82.4 24.1 %collective-permute-start.16 = (bf16[2,4,32,1024]{3,2,1,0:T(8,128)(2,1)S(1)}, bf16[2,4,32,1024]{3,2,1,0:T(8,128)(2,1)S(1)}, u32[]{:S(2)}, u32[]{:S(2)}) collective-permute-start(bf16[2,4,32,1024]{3,2,1,0:T(8,128)(2,1)S(1)} %get-tuple-element.14.refs_0_), channel_id=1, source_target_pairs={{0,192},{4,196},{8,200},{12,204},{16,208},{20,212},{24,216},{28,22... | collective-permute-start | bytes 1572872 | tf_op jit(solution)/shard_map/ppermute | solution.py:250
  83.5 0.8 copy-start.2
  87.3 7.8 %collective-permute-start.9 = (bf16[512,256]{1,0:T(8,128)(2,1)S(1)}, bf16[512,256]{1,0:T(8,128)(2,1)S(1)}, u32[]{:S(2)}, u32[]{:S(2)}) collective-permute-start(bf16[512,256]{1,0:T(8,128)(2,1)S(1)} %collective-permute-done.8), channel_id=1, source_target_pairs={{0,8},{1,9},{4,12},{5,13},{8,2},{9,3},{12,6},{13,7},{2,10},{3,11},... | collective-permute-start | bytes 786440 | tf_op jit(solution)/shard_map/ppermute | solution.py:44
  89.0 9.5 %collective-permute-start.11 = (bf16[512,256]{1,0:T(8,128)(2,1)S(1)}, bf16[512,256]{1,0:T(8,128)(2,1)S(1)}, u32[]{:S(2)}, u32[]{:S(2)}) collective-permute-start(bf16[512,256]{1,0:T(8,128)(2,1)S(1)} %collective-permute-done.10), channel_id=1, source_target_pairs={{0,10},{1,11},{4,14},{5,15},{8,0},{9,1},{12,4},{13,5},{2,8},{3,9},... | collective-permute-start | bytes 786440 | tf_op jit(solution)/shard_map/ppermute | solution.py:44
  95.1 15.1 %collective-permute-start.6 = (bf16[512,256]{1,0:T(8,128)(2,1)S(1)}, bf16[512,256]{1,0:T(8,128)(2,1)S(1)}, u32[]{:S(2)}, u32[]{:S(2)}) collective-permute-start(bf16[512,256]{1,0:T(8,128)(2,1)S(1)} %get-tuple-element.12.refs_0_), channel_id=1, source_target_pairs={{0,1},{1,0},{2,3},{3,2},{4,5},{5,4},{6,7},{7,6},{8,9},{9,8},{10,11... | collective-permute-start | bytes 786440 | tf_op jit(solution)/shard_map/ppermute | solution.py:238
  98.5 11.7 %collective-permute-start.7 = (bf16[512,256]{1,0:T(8,128)(2,1)S(1)}, bf16[512,256]{1,0:T(8,128)(2,1)S(1)}, u32[]{:S(2)}, u32[]{:S(2)}) collective-permute-start(bf16[512,256]{1,0:T(8,128)(2,1)S(1)} %get-tuple-element.13.refs_1_), channel_id=1, source_target_pairs={{0,1},{1,0},{2,3},{3,2},{4,5},{5,4},{6,7},{7,6},{8,9},{9,8},{10,11... | collective-permute-start | bytes 786440 | tf_op jit(solution)/shard_map/ppermute | solution.py:238
  103.5 6.7 %collective-permute-start.12 = (bf16[512,256]{1,0:T(8,128)(2,1)S(1)}, bf16[512,256]{1,0:T(8,128)(2,1)S(1)}, u32[]{:S(2)}, u32[]{:S(2)}) collective-permute-start(bf16[512,256]{1,0:T(8,128)(2,1)S(1)} %collective-permute-done.9.refs_4_), channel_id=1, source_target_pairs={{0,1},{1,0},{2,3},{3,2},{4,5},{5,4},{6,7},{7,6},{8,9},{9,8},{10,11... | collective-permute-start | bytes 786440 | tf_op jit(solution)/shard_map/ppermute | solution.py:239
  104.4 5.8 %collective-permute-start.13 = (bf16[512,256]{1,0:T(8,128)(2,1)S(1)}, bf16[512,256]{1,0:T(8,128)(2,1)S(1)}, u32[]{:S(2)}, u32[]{:S(2)}) collective-permute-start(bf16[512,256]{1,0:T(8,128)(2,1)S(1)} %collective-permute-done.11.refs_5_), channel_id=1, source_target_pairs={{0,1},{1,0},{2,3},{3,2},{4,5},{5,4},{6,7},{7,6},{8,9},{9,8},{10,11... | collective-permute-start | bytes 786440 | tf_op jit(solution)/shard_map/ppermute | solution.py:239
  106.5 2.2 %copy-start = (bf16[512,4096]{1,0:T(8,128)(2,1)S(1)}, bf16[512,4096]{1,0:T(8,128)(2,1)}, u32[]{:S(2)}) copy-start(bf16[512,4096]{1,0:T(8,128)(2,1)} %refs_4_.1) | copy-start | bytes 12582916
  108.7 1.0 copy-start.3
  (5 other events, 3.3 us)

commit v3 on v2

v3 whole, which is shorter than its diff:
```python
import functools

import jax
import jax.numpy as jnp
from jax import lax
from jax.experimental import pallas as pl
from jax.experimental.pallas import tpu as pltpu
from jax.sharding import PartitionSpec as P

BLK = 512
HEAD = 128
TOPK = 3
PIECE = 16
NOTE = 8
VMEM_MB = 16
FACTOR = HEAD ** -0.5
LOG2E = 1.4426950408889634
CALLS = 1
PARTS = 2

SWAP_CORE = [(0, 1), (1, 0), (2, 3), (3, 2)]
SWAP_Z = [(0, 2), (2, 0), (1, 3), (3, 1)]


def along_x(step):
    return [(c, c // 16 * 16 + (c // 4 + step) % 4 * 4 + c % 4) for c in range(64)]


def along_y(step):
    return [(c, (c // 16 + step) % 4 * 16 + c % 16) for c in range(64)]


def along_z(step):
    pairs = []
    for xy in range(16):
        for z in range(8):
            to = (z + step) % 8
            for core in range(2):
                pairs.append(((xy * 4 + z % 4) * 4 + z // 4 * 2 + core, (xy * 4 + to % 4) * 4 + to // 4 * 2 + core))
    return pairs


def over_z(a, step):
    for _ in range(2):
        a = lax.ppermute(a, ("ctx", "head"), along_z(step))
    return a


def cut_kernel(w_ref, same_ref, other_ref, core_ref, own_ref, sems):
    share, cols = same_ref.shape
    at = lax.axis_index("head")
    row = pl.multiple_of(lax.shift_right_logical(lax.axis_index("ctx"), 2) * share, share)
    rows = pl.ds(row, share)
    same_col = pl.multiple_of(lax.bitwise_xor(at, 2) * cols, cols)
    other_col = pl.multiple_of(lax.bitwise_xor(at, 3) * cols, cols)
    core_col = pl.multiple_of(lax.bitwise_xor(at, 1) * cols, cols)
    copies = (
        pltpu.make_async_copy(w_ref.at[rows, pl.ds(same_col, cols)], same_ref, sems.at[0]),
        pltpu.make_async_copy(w_ref.at[rows, pl.ds(other_col, cols)], other_ref, sems.at[1]),
        pltpu.make_async_copy(w_ref.at[:, pl.ds(core_col, cols)], core_ref, sems.at[2]),
        pltpu.make_async_copy(w_ref.at[:, pl.ds(pl.multiple_of(at * cols, cols), cols)], own_ref, sems.at[3]),
    )
    for copy in copies:
        copy.start()
    for copy in copies:
        copy.wait()


def spread_kernel(order_ref, chosen_ref, k_ref, v_ref, out_ref):
    half = out_ref.shape[0] // 2
    slots = [jnp.int32(0)] * TOPK
    for s in range(out_ref.shape[0]):
        slots = [jnp.where(order_ref[s] == chosen_ref[j], s, slot) for j, slot in enumerate(slots)]
    lane = lax.broadcasted_iota(jnp.int32, (NOTE, HEAD), 1)
    note = jnp.where(lane == 0, slots[0], jnp.where(lane == 1, slots[1], slots[2]))
    note = note.astype(jnp.float32).astype(jnp.bfloat16)
    for c in range(half):
        piece = slice(c * PIECE, (c + 1) * PIECE)
        out_ref[c] = jnp.concatenate([k_ref[piece, :], note], axis=0)
        out_ref[half + c] = jnp.concatenate([v_ref[piece, :], note], axis=0)


def pack_kernel(slots_ref, held_ref, first_ref, second_ref, out_ref):
    n_dst = out_ref.shape[0]
    for first in range(0, n_dst, 8):
        todo = [(d, j) for d in range(first, first + 8) for j in range(TOPK)]
        slots = [slots_ref[d, j] for d, j in todo]
        pieces = [held_ref[slot, :PIECE, :] for slot in slots]
        for (d, j), piece in zip(todo, pieces):
            out_ref[d, j * PIECE : (j + 1) * PIECE, :] = piece


def merge_x_kernel(*refs):
    *piece_refs, out_ref, sems = refs
    x = lax.bitwise_and(lax.shift_right_logical(lax.axis_index("ctx"), 2), 3)
    copies = []
    for k, ref in enumerate(piece_refs):
        at = lax.bitwise_and(x + (4 - k), 3)
        copies.append(pltpu.make_async_copy(ref, out_ref.at[:, at], sems.at[k]))
        copies[-1].start()
    for copy in copies:
        copy.wait()


def weights_kernel(*refs):
    *quarter_refs, out_ref, sems = refs
    y = lax.shift_right_logical(lax.axis_index("ctx"), 4)
    copies = []
    for k, ref in enumerate(quarter_refs):
        at = lax.bitwise_and(y + (4 - k), 3)
        copies.append(pltpu.make_async_copy(ref, out_ref.at[:, at], sems.at[k]))
        copies[-1].start()
    for copy in copies:
        copy.wait()


def attend_kernel(ok_ref, q_ref, k_ref, v_ref, got_ref, pass_ref, *out_refs, rows):
    out_refs = out_refs[:PARTS]
    half = got_ref.shape[0] // 2
    heads = q_ref.shape[0]
    contract = (((1,), (1,)), ((), ()))
    for h in range(heads):
        for r in range(0, BLK, rows):
            q = q_ref[h, r : r + rows, :]
            seen = r + rows
            near = lax.dot_general(q, k_ref[:seen, :], contract, preferred_element_type=jnp.float32)
            row = lax.broadcasted_iota(jnp.int32, near.shape, 0) + r
            col = lax.broadcasted_iota(jnp.int32, near.shape, 1)
            near = jnp.where(col <= row, near, -jnp.inf)
            far = []
            for j in range(TOPK):
                k_j = got_ref[:half, j * PIECE : (j + 1) * PIECE, :].reshape(BLK, HEAD)
                s = lax.dot_general(q, k_j, contract, preferred_element_type=jnp.float32)
                far.append(s)
            highest = jnp.max(near, axis=1, keepdims=True)
            for j, s in enumerate(far):
                here = jnp.max(s, axis=1, keepdims=True)
                highest = jnp.maximum(highest, jnp.where(ok_ref[j] != 0, here, -jnp.inf))
            w = jnp.exp2((near - highest) * (FACTOR * LOG2E))
            total = jnp.sum(w, axis=1, keepdims=True)
            acc = jnp.dot(w.astype(jnp.bfloat16), v_ref[:seen, :], preferred_element_type=jnp.float32)
            for j in range(TOPK):
                v_j = got_ref[half:, j * PIECE : (j + 1) * PIECE, :].reshape(BLK, HEAD)
                w = jnp.exp2((far[j] - jnp.where(ok_ref[j] != 0, highest, jnp.inf)) * (FACTOR * LOG2E))
                total = total + jnp.sum(w, axis=1, keepdims=True)
                acc = acc + jnp.dot(w.astype(jnp.bfloat16), v_j, preferred_element_type=jnp.float32)
            per = heads // len(out_refs)
            part, col = out_refs[h // per], h % per * HEAD
            part[r : r + rows, col : col + HEAD] = (acc / total).astype(jnp.bfloat16)


def fetch(part_refs, lhs, sems):
    wide = part_refs[0].shape[1]
    copies = [
        pltpu.make_async_copy(ref, lhs.at[:, i * wide : (i + 1) * wide], sems.at[i]) for i, ref in enumerate(part_refs)
    ]
    for copy in copies:
        copy.start()
    return copies


def near_kernel(*refs):
    *part_refs, own_ref, core_ref, out_ref, lhs, sems = refs
    for copy in fetch(part_refs, lhs, sems):
        copy.wait()
    half = own_ref.shape[0]
    out_ref[...] = jnp.dot(lhs[:, :half], own_ref[...], preferred_element_type=jnp.float32) + jnp.dot(
        lhs[:, half:], core_ref[...], preferred_element_type=jnp.float32
    )


def last_kernel(*refs):
    *part_refs, w_ref, near_ref, out_ref, lhs, sems = refs
    copies = fetch(part_refs, lhs, sems)
    for copy in copies:
        copy.wait()
    w = w_ref[...].reshape(lhs.shape[1], -1)
    far = jnp.dot(lhs[...], w, preferred_element_type=jnp.float32)
    out_ref[...] = (near_ref[...] + far).astype(jnp.bfloat16)


def local(queries, keys, values, w_out, block_order, chosen):
    n_blocks = block_order.shape[0]
    ctx = lax.axis_index("ctx")
    head_at = lax.axis_index("head")
    cols = w_out.shape[1] // 4
    share = BLK // 16
    bf16 = jnp.bfloat16
    smem = pl.BlockSpec(memory_space=pltpu.SMEM)
    vmem = pl.BlockSpec(memory_space=pltpu.VMEM)
    hbm = pl.BlockSpec(memory_space=pl.ANY)
    stay = pl.BlockSpec(memory_space=pltpu.HBM)
    params = pltpu.CompilerParams(vmem_limit_bytes=VMEM_MB * 1024 * 1024)
    k_own, v_own = keys[:, 0, :], values[:, 0, :]

    piece = jax.ShapeDtypeStruct((share, cols), bf16)
    near_rows = jax.ShapeDtypeStruct((BLK, cols), bf16)
    far_same, far_other, w_core, w_own = pl.pallas_call(
        cut_kernel,
        out_shape=(piece, piece, near_rows, near_rows),
        in_specs=[stay],
        out_specs=(vmem,) * 4,
        scratch_shapes=[pltpu.SemaphoreType.DMA((4,))],
        name="cut",
    )(w_out)
    far_same = lax.ppermute(far_same, "head", SWAP_Z)
    far_other = lax.ppermute(far_other, "head", SWAP_Z)

    spread = pl.pallas_call(
        spread_kernel,
        out_shape=jax.ShapeDtypeStruct((n_blocks, PIECE + NOTE, HEAD), bf16),
        in_specs=[smem, smem, vmem, vmem],
        out_specs=vmem,
        name="spread",
    )(block_order, chosen.reshape(TOPK), k_own, v_own)
    held = lax.all_to_all(spread, "ctx", 0, 0, tiled=True)

    both = jnp.stack([far_same, lax.ppermute(far_other, "head", SWAP_CORE)])
    quarter = pl.pallas_call(
        merge_x_kernel,
        out_shape=jax.ShapeDtypeStruct((2, 4, share, cols), bf16),
        in_specs=[hbm] * 4,
        out_specs=vmem,
        scratch_shapes=[pltpu.SemaphoreType.DMA((4,))],
        name="merge_x",
    )(both, *[lax.ppermute(both, "ctx", along_x(k)) for k in (1, 2, 3)])

    slots = held[:, PIECE, :TOPK].astype(jnp.int32)
    packed = pl.pallas_call(
        pack_kernel,
        out_shape=jax.ShapeDtypeStruct((n_blocks, TOPK * PIECE, HEAD), bf16),
        in_specs=[smem, vmem, hbm, hbm],
        out_specs=vmem,
        name="pack",
    )(slots, held, far_same, far_other)
    got = lax.all_to_all(packed, "ctx", 0, 0, tiled=True)

    own = lax.dynamic_slice_in_dim(block_order, ctx, 1)
    ok = (chosen[0, 0] != own).astype(jnp.int32)
    q = jnp.transpose(queries, (1, 0, 2))
    part = jax.ShapeDtypeStruct((BLK, HEAD * 4 // (CALLS * PARTS)), bf16)
    a_own, a_z = [], []
    for call in range(CALLS):
        heads = slice(call * 4 // CALLS, (call + 1) * 4 // CALLS)
        *parts, quarter = pl.pallas_call(
            functools.partial(attend_kernel, rows=256),
            out_shape=(part,) * PARTS + (jax.ShapeDtypeStruct(quarter.shape, bf16),),
            in_specs=[smem, vmem, vmem, vmem, vmem, hbm],
            out_specs=(vmem,) * PARTS + (hbm,),
            input_output_aliases={5: PARTS},
            compiler_params=params,
            cost_estimate=pl.CostEstimate(flops=1 << 20, bytes_accessed=1 << 10, transcendentals=0),
            name="attend",
        )(ok, q[heads], k_own, v_own, got, quarter)
        a_own += parts
        a_z += [over_z(a, step) for a, step in zip(parts, (2, -2))]
    a_core = [lax.ppermute(a, "head", SWAP_CORE) for a in a_own]
    a_zc = [lax.ppermute(a, "head", SWAP_CORE) for a in a_z]

    w_far = pl.pallas_call(
        weights_kernel,
        out_shape=jax.ShapeDtypeStruct((2, 4, 4, share, cols), bf16),
        in_specs=[hbm] * 4,
        out_specs=vmem,
        scratch_shapes=[pltpu.SemaphoreType.DMA((4,))],
        compiler_params=params,
        name="weights",
    )(quarter, *[lax.ppermute(quarter, "ctx", along_y(k)) for k in (1, 2, 3)])
    w_core = lax.ppermute(w_core, "head", SWAP_CORE)
    lhs = pltpu.VMEM((BLK, 8 * HEAD), bf16)
    near = pl.pallas_call(
        near_kernel,
        out_shape=jax.ShapeDtypeStruct((BLK, cols), jnp.float32),
        in_specs=[hbm] * (2 * len(a_own)) + [vmem] * 2,
        out_specs=vmem,
        scratch_shapes=[lhs, pltpu.SemaphoreType.DMA((2 * len(a_own),))],
        compiler_params=params,
        name="near",
    )(*a_own, *a_core, w_own, w_core)
    return pl.pallas_call(
        last_kernel,
        out_shape=jax.ShapeDtypeStruct((BLK, cols), bf16),
        in_specs=[hbm] * (2 * len(a_own)) + [vmem] * 2,
        out_specs=vmem,
        scratch_shapes=[lhs, pltpu.SemaphoreType.DMA((2 * len(a_own),))],
        compiler_params=params,
        name="last",
    )(*a_z, *a_zc, w_far, near)


def solution(mesh):
    in_specs = (
        P("ctx", "head", None),
        P("ctx", "head", None),
        P("ctx", "head", None),
        P("head", None),
        P(),
        P("ctx", "head", None),
    )
    out_specs = P("ctx", "head")
    return jax.shard_map(local, mesh=mesh, in_specs=in_specs, out_specs=out_specs, check_vma=False)
```

time: 115 us -> 113 us (0.983)
  local copies, waits for them, and re-layouts: 10 us -> 4.02 us
  Pallas kernels: 18.9 us -> 21.4 us
  starting transfers between devices: 58 us -> 59.2 us
    ppermute x2, starting transfers between devices: 2.12 us -> 8.96 us  [local(): a_zc = [lax.ppermute(a, 'head', SWAP_CORE) for a in a_z]]
    ppermute x2, starting transfers between devices: 8.37 us -> 2.76 us  [local(): a_core = [lax.ppermute(a, 'head', SWAP_CORE) for a in a_own]]
    unnamed x35 -> x23, local copies, waits for them, and re-layouts: 7.08 us -> 3.43 us
    dynamic_slice x1 -> x0, local copies, waits for them, and re-layouts: 2.27 us -> none  [local(): lax.dynamic_slice_in_dim(w_out, lax.bitwise_xor(head_at, 1) * cols, cols,...]
    ppermute x4, waiting for transfers between devices: 8.54 us -> 10.8 us  [over_z(): a = lax.ppermute(a, ('ctx', 'head'), along_z(step))]
    pallas_call x3 -> x4, Pallas kernels: 5.78 us -> 7.99 us  [the longest x1 3.05 us: local(): pl.pallas_call(cut_kernel, out_shape=(piece, piece, near_rows, near_rows)...]
    ppermute x3, starting transfers between devices: 5.16 us -> 3.19 us  [local(): lax.ppermute(quarter, 'ctx', along_y(k))]
    all_to_all x1, waiting for transfers between devices: 7.84 us -> 6.09 us  [local(): held = lax.all_to_all(spread, 'ctx', 0, 0, tiled=True)]
  transfers between devices with their start and end apart: 20 -> 20, of which waited for: 8 -> 9; matrix products, arithmetic and copies ran while one was open for 4% -> 4% of each run, Pallas kernels for 10% -> 13%
where the time goes in v3:
time: 113 us
  starting transfers between devices  59.2 us (52%)
  waiting for transfers between devices  25.4 us (22%)
  Pallas kernels  21.4 us (19%)
  local copies, waits for them, and re-layouts  4.02 us (4%)
  other arithmetic  2.21 us (2%)
    all_to_all x1, starting transfers between devices, local(): held = lax.all_to_all(spread, 'ctx', 0, 0, tiled=True)  12.6 us
    ppermute x4, waiting for transfers between devices, over_z(): a = lax.ppermute(a, ('ctx', 'head'), along_z(step))  10.8 us
    all_to_all x1, starting transfers between devices, local(): got = lax.all_to_all(packed, 'ctx', 0, 0, tiled=True)  9.99 us
    ppermute x2, starting transfers between devices, local(): a_zc = [lax.ppermute(a, 'head', SWAP_CORE) for a in a_z]  8.96 us
    ppermute x4, starting transfers between devices, over_z(): a = lax.ppermute(a, ('ctx', 'head'), along_z(step))  8.4 us
    pallas_call x1, Pallas kernels, local(): pl.pallas_call(functools.partial(attend_kernel, rows=256), out_shape=(par...  7.27 us
    ppermute x3, waiting for transfers between devices, local(): lax.ppermute(both, 'ctx', along_x(k))  6.5 us
    all_to_all x1, waiting for transfers between devices, local(): held = lax.all_to_all(spread, 'ctx', 0, 0, tiled=True)  6.09 us
  transfers between devices with their start and end apart: 20, of which 9 were waited for; matrix products, arithmetic and copies ran while one was open for 4% of the time, Pallas kernels for 13%

profile of v3, /device:TPU:1, one launch (start us, length us, event | category | flops | bytes accessed | tf_op | source)
XLA Modules:
  0.0 112.6 jit_solution(4969073516085505006)
XLA Ops:
  0.0 1.9 %spread.1 = bf16[64,24,128]{2,1,0:T(8,128)(2,1)} custom-call(s32[64]{0:T(128)} %order_ref.1, s32[3]{0:T(128)} %bitcast.18, bf16[512,128]{1,0:T(8,128)(2,1)} %bitcast.12, bf16[512,128]{1,0:T(8,128)(2,1)} %bitcast.14), custom_call_target="tpu_custom_call" | custom-call | tf_op jit(solution)/shard_map/spread/pallas_call | solution.py:209
  1.9 12.6 %all-to-all-start = ((bf16[64,24,128]{2,1,0:T(8,128)(2,1)}), bf16[64,24,128]{2,1,0:T(8,128)(2,1)S(1)}, u32[]{:S(2)}, u32[]{:S(2)}) async-start(bf16[64,24,128]{2,1,0:T(8,128)(2,1)} %spread.1), calls=%async_computation | async-start | bytes 786432 | tf_op jit(solution)/shard_map/all_to_all | solution.py:216
  14.4 3.0 %cut.1 = (bf16[32,1024]{1,0:T(8,128)(2,1)}, bf16[32,1024]{1,0:T(8,128)(2,1)}, bf16[512,1024]{1,0:T(8,128)(2,1)}, bf16[512,1024]{1,0:T(8,128)(2,1)}) custom-call(bf16[512,4096]{1,0:T(8,128)(2,1)} %w_ref.1), custom_call_target="tpu_custom_call" | custom-call | tf_op jit(solution)/shard_map/cut/pallas_call | solution.py:198
  17.5 4.3 %collective-permute-start.1 = (bf16[32,1024]{1,0:T(8,128)(2,1)}, bf16[32,1024]{1,0:T(8,128)(2,1)S(1)}, u32[]{:S(2)}, u32[]{:S(2)}) collective-permute-start(bf16[32,1024]{1,0:T(8,128)(2,1)} %get-tuple-element.13), channel_id=1, source_target_pairs={{0,2},{2,0},{1,3},{3,1},{4,6},{6,4},{5,7},{7,5},{8,10},{10,8},{9,1... | collective-permute-start | bytes 196616 | tf_op jit(solution)/shard_map/ppermute | solution.py:207
  21.8 1.2 %collective-permute-start = (bf16[32,1024]{1,0:T(8,128)(2,1)}, bf16[32,1024]{1,0:T(8,128)(2,1)S(1)}, u32[]{:S(2)}, u32[]{:S(2)}) collective-permute-start(bf16[32,1024]{1,0:T(8,128)(2,1)} %get-tuple-element.12), channel_id=1, source_target_pairs={{0,2},{2,0},{1,3},{3,1},{4,6},{6,4},{5,7},{7,5},{8,10},{10,8},{9,1... | collective-permute-start | bytes 196616 | tf_op jit(solution)/shard_map/ppermute | solution.py:206
  23.0 6.1 %all-to-all-done.held_ref = bf16[64,24,128]{2,1,0:T(8,128)(2,1)S(1)} async-done(((bf16[64,24,128]{2,1,0:T(8,128)(2,1)}), bf16[64,24,128]{2,1,0:T(8,128)(2,1)S(1)}, u32[]{:S(2)}, u32[]{:S(2)}) %all-to-all-start) | async-done | bytes 393248 | tf_op jit(solution)/shard_map/all_to_all | solution.py:216
  30.4 2.4 %pack.1 = bf16[64,48,128]{2,1,0:T(8,128)(2,1)} custom-call(s32[64,3]{1,0:T(8,128)} %bitcast.17, bf16[64,24,128]{2,1,0:T(8,128)(2,1)} %copy-done.3, bf16[32,1024]{1,0:T(8,128)(2,1)} %copy-done.5, bf16[32,1024]{1,0:T(8,128)(2,1)} %copy-done.8), custom_call_target="tpu_custom_call" | custom-call | tf_op jit(solution)/shard_map/pack/pallas_call | solution.py:229
  32.8 10.0 %all-to-all-start.1 = ((bf16[64,48,128]{2,1,0:T(8,128)(2,1)}), bf16[64,48,128]{2,1,0:T(8,128)(2,1)S(1)}, u32[]{:S(2)}, u32[]{:S(2)}) async-start(bf16[64,48,128]{2,1,0:T(8,128)(2,1)} %pack.1), calls=%async_computation.1 | async-start | bytes 1572864 | tf_op jit(solution)/shard_map/all_to_all | solution.py:236
  42.8 2.8 %collective-permute-start.17 = (bf16[512,1024]{1,0:T(8,128)(2,1)}, bf16[512,1024]{1,0:T(8,128)(2,1)S(1)}, u32[]{:S(2)}, u32[]{:S(2)}) collective-permute-start(bf16[512,1024]{1,0:T(8,128)(2,1)} %get-tuple-element.18), channel_id=1, source_target_pairs={{0,1},{1,0},{2,3},{3,2},{4,5},{5,4},{6,7},{7,6},{8,9},{9,8},{10,11... | collective-permute-start | bytes 3145736 | tf_op jit(solution)/shard_map/ppermute | solution.py:269
  46.3 1.2 %copy.10 = bf16[512,4,128]{2,0,1:T(8,128)(2,1)S(1)} copy(bf16[512,4,128]{2,1,0:T(4,128)(2,1)} %param.6) | data formatting | bytes 1048576 | tf_op args[0]
  49.1 1.4 %collective-permute-start.3 = (bf16[2,32,1024]{2,1,0:T(8,128)(2,1)S(1)}, bf16[2,32,1024]{2,1,0:T(8,128)(2,1)S(1)}, u32[]{:S(2)}, u32[]{:S(2)}) collective-permute-start(bf16[2,32,1024]{2,1,0:T(8,128)(2,1)S(1)} %pad_maximum_fusion.refs_0_), channel_id=1, source_target_pairs={{0,16},{4,20},{8,24},{12,28},{16,32},{20,36},{24,40},{28,44},{32,4... | collective-permute-start | bytes 393224 | tf_op jit(solution)/shard_map/ppermute | solution.py:226
  50.5 2.4 %collective-permute-start.4 = (bf16[2,32,1024]{2,1,0:T(8,128)(2,1)S(1)}, bf16[2,32,1024]{2,1,0:T(8,128)(2,1)S(1)}, u32[]{:S(2)}, u32[]{:S(2)}) collective-permute-start(bf16[2,32,1024]{2,1,0:T(8,128)(2,1)S(1)} %pad_maximum_fusion.refs_0_), channel_id=1, source_target_pairs={{0,32},{4,36},{8,40},{12,44},{16,48},{20,52},{24,56},{28,60},{32,0... | collective-permute-start | bytes 393224 | tf_op jit(solution)/shard_map/ppermute | solution.py:226
  52.9 1.2 %collective-permute-start.5 = (bf16[2,32,1024]{2,1,0:T(8,128)(2,1)S(1)}, bf16[2,32,1024]{2,1,0:T(8,128)(2,1)}, u32[]{:S(2)}, u32[]{:S(2)}) collective-permute-start(bf16[2,32,1024]{2,1,0:T(8,128)(2,1)S(1)} %pad_maximum_fusion.refs_0_), channel_id=1, source_target_pairs={{0,48},{4,52},{8,56},{12,60},{16,0},{20,4},{24,8},{28,12},{32,16},... | collective-permute-start | bytes 393224 | tf_op jit(solution)/shard_map/ppermute | solution.py:226
  54.7 2.3 %collective-permute-done.3.refs_1_ = bf16[2,32,1024]{2,1,0:T(8,128)(2,1)S(1)} collective-permute-done((bf16[2,32,1024]{2,1,0:T(8,128)(2,1)S(1)}, bf16[2,32,1024]{2,1,0:T(8,128)(2,1)S(1)}, u32[]{:S(2)}, u32[]{:S(2)}) %collective-permute-start.3) | collective-permute-done | bytes 131104 | tf_op jit(solution)/shard_map/ppermute | solution.py:226
  56.9 4.2 %collective-permute-done.4.refs_2_ = bf16[2,32,1024]{2,1,0:T(8,128)(2,1)S(1)} collective-permute-done((bf16[2,32,1024]{2,1,0:T(8,128)(2,1)S(1)}, bf16[2,32,1024]{2,1,0:T(8,128)(2,1)S(1)}, u32[]{:S(2)}, u32[]{:S(2)}) %collective-permute-start.4) | collective-permute-done | bytes 131104 | tf_op jit(solution)/shard_map/ppermute | solution.py:226
  61.8 1.9 %merge_x.1.pass_ref = bf16[2,4,32,1024]{3,2,1,0:T(8,128)(2,1)} custom-call(bf16[2,32,1024]{2,1,0:T(8,128)(2,1)} %copy-done.4, bf16[2,32,1024]{2,1,0:T(8,128)(2,1)} %copy-done.6, bf16[2,32,1024]{2,1,0:T(8,128)(2,1)} %copy-done.7, bf16[2,32,1024]{2,1,0:T(8,128)(2,1)} %collective-permute-done.5.refs_3_), custom_call_target="tpu_custom_call" | custom-call | tf_op jit(solution)/shard_map/merge_x/pallas_call | solution.py:219
  63.8 1.3 %all-to-all-done.1.got_ref = bf16[64,48,128]{2,1,0:T(8,128)(2,1)S(1)} async-done(((bf16[64,48,128]{2,1,0:T(8,128)(2,1)}), bf16[64,48,128]{2,1,0:T(8,128)(2,1)S(1)}, u32[]{:S(2)}, u32[]{:S(2)}) %all-to-all-start.1) | async-done | bytes 786464 | tf_op jit(solution)/shard_map/all_to_all | solution.py:236
  66.0 7.3 %attend.1 = (bf16[512,256]{1,0:T(8,128)(2,1)S(1)}, bf16[512,256]{1,0:T(8,128)(2,1)S(1)}, bf16[2,4,32,1024]{3,2,1,0:T(8,128)(2,1)}) custom-call(s32[3]{0:T(128)S(1)} %compare_convert_fusion.ok_ref, bf16[4,512,128]{2,1,0:T(8,128)(2,1)S(1)} %bitcast.11, bf16[512,128]{1,0:T(8,128)(2,1)S(1)} %bitcast.13, ...), custom_call_target="tpu_custom_call", output_to_operand_aliasing={{2}: (5, {})} | custom-call | flops 1048576 | bytes 1024 | tf_op jit(solution)/shard_map/attend/pallas_call | solution.py:245
  73.3 2.7 %collective-permute-start.15 = (bf16[512,256]{1,0:T(8,128)(2,1)S(1)}, bf16[512,256]{1,0:T(8,128)(2,1)S(1)}, u32[]{:S(2)}, u32[]{:S(2)}) collective-permute-start(bf16[512,256]{1,0:T(8,128)(2,1)S(1)} %get-tuple-element.14.refs_0_), channel_id=1, source_target_pairs={{0,1},{1,0},{2,3},{3,2},{4,5},{5,4},{6,7},{7,6},{8,9},{9,8},{10,11... | collective-permute-start | bytes 786440 | tf_op jit(solution)/shard_map/ppermute | solution.py:257
  76.3 3.4 %collective-permute-start.8 = (bf16[512,256]{1,0:T(8,128)(2,1)S(1)}, bf16[512,256]{1,0:T(8,128)(2,1)S(1)}, u32[]{:S(2)}, u32[]{:S(2)}) collective-permute-start(bf16[512,256]{1,0:T(8,128)(2,1)S(1)} %get-tuple-element.15.refs_1_), channel_id=1, source_target_pairs={{0,10},{1,11},{4,14},{5,15},{8,0},{9,1},{12,4},{13,5},{2,8},{3,9},... | collective-permute-start | bytes 786440 | tf_op jit(solution)/shard_map/ppermute | solution.py:45
  79.7 2.1 %collective-permute-start.13 = (bf16[2,4,32,1024]{3,2,1,0:T(8,128)(2,1)}, bf16[2,4,32,1024]{3,2,1,0:T(8,128)(2,1)S(1)}, u32[]{:S(2)}, u32[]{:S(2)}) collective-permute-start(bf16[2,4,32,1024]{3,2,1,0:T(8,128)(2,1)} %get-tuple-element.16.refs_0_), channel_id=1, source_target_pairs={{0,128},{4,132},{8,136},{12,140},{16,144},{20,148},{24,152},{28,15... | collective-permute-start | bytes 1572872 | tf_op jit(solution)/shard_map/ppermute | solution.py:268
  81.8 1.1 collective-permute-start.14
  82.8 6.0 %collective-permute-done.6 = bf16[512,256]{1,0:T(8,128)(2,1)S(1)} collective-permute-done((bf16[512,256]{1,0:T(8,128)(2,1)S(1)}, bf16[512,256]{1,0:T(8,128)(2,1)S(1)}, u32[]{:S(2)}, u32[]{:S(2)}) %collective-permute-start.6) | collective-permute-done | bytes 262176 | tf_op jit(solution)/shard_map/ppermute | solution.py:45
  88.9 1.5 %collective-permute-start.7 = (bf16[512,256]{1,0:T(8,128)(2,1)S(1)}, bf16[512,256]{1,0:T(8,128)(2,1)S(1)}, u32[]{:S(2)}, u32[]{:S(2)}) collective-permute-start(bf16[512,256]{1,0:T(8,128)(2,1)S(1)} %collective-permute-done.6), channel_id=1, source_target_pairs={{0,8},{1,9},{4,12},{5,13},{8,2},{9,3},{12,6},{13,7},{2,10},{3,11},... | collective-permute-start | bytes 786440 | tf_op jit(solution)/shard_map/ppermute | solution.py:45
  90.4 1.8 %collective-permute-done.8 = bf16[512,256]{1,0:T(8,128)(2,1)S(1)} collective-permute-done((bf16[512,256]{1,0:T(8,128)(2,1)S(1)}, bf16[512,256]{1,0:T(8,128)(2,1)S(1)}, u32[]{:S(2)}, u32[]{:S(2)}) %collective-permute-start.8) | collective-permute-done | bytes 262176 | tf_op jit(solution)/shard_map/ppermute | solution.py:45
  92.2 3.3 %collective-permute-start.9 = (bf16[512,256]{1,0:T(8,128)(2,1)S(1)}, bf16[512,256]{1,0:T(8,128)(2,1)S(1)}, u32[]{:S(2)}, u32[]{:S(2)}) collective-permute-start(bf16[512,256]{1,0:T(8,128)(2,1)S(1)} %collective-permute-done.8), channel_id=1, source_target_pairs={{0,10},{1,11},{4,14},{5,15},{8,0},{9,1},{12,4},{13,5},{2,8},{3,9},... | collective-permute-start | bytes 786440 | tf_op jit(solution)/shard_map/ppermute | solution.py:45
  95.5 1.5 %collective-permute-done.7.refs_0_ = bf16[512,256]{1,0:T(8,128)(2,1)S(1)} collective-permute-done((bf16[512,256]{1,0:T(8,128)(2,1)S(1)}, bf16[512,256]{1,0:T(8,128)(2,1)S(1)}, u32[]{:S(2)}, u32[]{:S(2)}) %collective-permute-start.7) | collective-permute-done | bytes 262176 | tf_op jit(solution)/shard_map/ppermute | solution.py:45
  97.1 8.4 %collective-permute-start.10 = (bf16[512,256]{1,0:T(8,128)(2,1)S(1)}, bf16[512,256]{1,0:T(8,128)(2,1)S(1)}, u32[]{:S(2)}, u32[]{:S(2)}) collective-permute-start(bf16[512,256]{1,0:T(8,128)(2,1)S(1)} %collective-permute-done.7.refs_0_), channel_id=1, source_target_pairs={{0,1},{1,0},{2,3},{3,2},{4,5},{5,4},{6,7},{7,6},{8,9},{9,8},{10,11... | collective-permute-start | bytes 786440 | tf_op jit(solution)/shard_map/ppermute | solution.py:258
  105.5 1.4 %collective-permute-done.9.refs_1_ = bf16[512,256]{1,0:T(8,128)(2,1)S(1)} collective-permute-done((bf16[512,256]{1,0:T(8,128)(2,1)S(1)}, bf16[512,256]{1,0:T(8,128)(2,1)S(1)}, u32[]{:S(2)}, u32[]{:S(2)}) %collective-permute-start.9) | collective-permute-done | bytes 262176 | tf_op jit(solution)/shard_map/ppermute | solution.py:45
  107.4 1.4 %near.1.refs_5_ = f32[512,1024]{1,0:T(8,128)S(1)} custom-call(bf16[512,256]{1,0:T(8,128)(2,1)S(1)} %get-tuple-element.14.refs_0_, bf16[512,256]{1,0:T(8,128)(2,1)S(1)} %get-tuple-element.15.refs_1_, bf16[512,256]{1,0:T(8,128)(2,1)S(1)} %collective-permute-done.15.refs_2_, bf16[512,256]{1,0:T(8,128)(2,1)S(1)} %collective-permute-done.16.refs_3_, ...), custom_call_target="tpu_custom_call" | custom-call | tf_op jit(solution)/shard_map/near/pallas_call | solution.py:271
  108.9 1.1 weights.1.refs_4_
  110.0 2.4 %last.1 = bf16[512,1024]{1,0:T(8,128)(2,1)} custom-call(bf16[512,256]{1,0:T(8,128)(2,1)S(1)} %collective-permute-done.7.refs_0_, bf16[512,256]{1,0:T(8,128)(2,1)S(1)} %collective-permute-done.9.refs_1_, bf16[512,256]{1,0:T(8,128)(2,1)S(1)} %collective-permute-done.10.refs_2_, bf16[512,256]{1,0:T(8,128)(2,1)S(1)} %collective-permute-done.11.refs_3_, ...), custom_call_target="tpu_custom_call" | custom-call | tf_op jit(solution)/shard_map/last/pallas_call | solution.py:280
  (43 shorter events, 6.8 us)
Async XLA Ops:
  1.9 27.2 %all-to-all-start = ((bf16[64,24,128]{2,1,0:T(8,128)(2,1)}), bf16[64,24,128]{2,1,0:T(8,128)(2,1)S(1)}, u32[]{:S(2)}, u32[]{:S(2)}) async-start(bf16[64,24,128]{2,1,0:T(8,128)(2,1)} %spread.1), calls=%async_computation | async-start | bytes 786432 | tf_op jit(solution)/shard_map/all_to_all | solution.py:216
  17.5 28.2 %copy-start.9 = (s32[64]{0:T(128)S(1)}, s32[64]{0:T(128)}, u32[]{:S(2)}) copy-start(s32[64]{0:T(128)} %order_ref.1) | copy-start | bytes 772
  17.5 12.3 %collective-permute-start.1 = (bf16[32,1024]{1,0:T(8,128)(2,1)}, bf16[32,1024]{1,0:T(8,128)(2,1)S(1)}, u32[]{:S(2)}, u32[]{:S(2)}) collective-permute-start(bf16[32,1024]{1,0:T(8,128)(2,1)} %get-tuple-element.13), channel_id=1, source_target_pairs={{0,2},{2,0},{1,3},{3,1},{4,6},{6,4},{5,7},{7,5},{8,10},{10,8},{9,1... | collective-permute-start | bytes 196616 | tf_op jit(solution)/shard_map/ppermute | solution.py:207
  21.8 8.0 %collective-permute-start = (bf16[32,1024]{1,0:T(8,128)(2,1)}, bf16[32,1024]{1,0:T(8,128)(2,1)S(1)}, u32[]{:S(2)}, u32[]{:S(2)}) collective-permute-start(bf16[32,1024]{1,0:T(8,128)(2,1)} %get-tuple-element.12), channel_id=1, source_target_pairs={{0,2},{2,0},{1,3},{3,1},{4,6},{6,4},{5,7},{7,5},{8,10},{10,8},{9,1... | collective-permute-start | bytes 196616 | tf_op jit(solution)/shard_map/ppermute | solution.py:206
  29.1 0.8 copy-start.3
  29.8 0.6 copy-start.8
  29.8 0.6 copy-start.5
  30.4 23.6 %copy-start.10 = (s32[1,1,3]{2,1,0:T(1,128)S(1)}, s32[1,1,3]{2,1,0:T(1,128)}, u32[]{:S(2)}) copy-start(s32[1,1,3]{2,1,0:T(1,128)} %param.11) | copy-start | bytes 40
  32.8 32.3 %copy-start.1 = (bf16[512,1,128]{2,0,1:T(8,128)(2,1)S(1)}, bf16[512,1,128]{2,0,1:T(8,128)(2,1)}, u32[]{:S(2)}) copy-start(bf16[512,1,128]{2,0,1:T(8,128)(2,1)} %param.7) | copy-start | bytes 393220
  32.8 32.3 %all-to-all-start.1 = ((bf16[64,48,128]{2,1,0:T(8,128)(2,1)}), bf16[64,48,128]{2,1,0:T(8,128)(2,1)S(1)}, u32[]{:S(2)}, u32[]{:S(2)}) async-start(bf16[64,48,128]{2,1,0:T(8,128)(2,1)} %pack.1), calls=%async_computation.1 | async-start | bytes 1572864 | tf_op jit(solution)/shard_map/all_to_all | solution.py:236
  42.8 36.8 %collective-permute-start.17 = (bf16[512,1024]{1,0:T(8,128)(2,1)}, bf16[512,1024]{1,0:T(8,128)(2,1)S(1)}, u32[]{:S(2)}, u32[]{:S(2)}) collective-permute-start(bf16[512,1024]{1,0:T(8,128)(2,1)} %get-tuple-element.18), channel_id=1, source_target_pairs={{0,1},{1,0},{2,3},{3,2},{4,5},{5,4},{6,7},{7,6},{8,9},{9,8},{10,11... | collective-permute-start | bytes 3145736 | tf_op jit(solution)/shard_map/ppermute | solution.py:269
  45.6 2.6 %collective-permute-start.2 = (bf16[32,1024]{1,0:T(8,128)(2,1)}, bf16[32,1024]{1,0:T(8,128)(2,1)}, u32[]{:S(2)}, u32[]{:S(2)}) collective-permute-start(bf16[32,1024]{1,0:T(8,128)(2,1)} %copy-done.8), channel_id=1, source_target_pairs={{0,1},{1,0},{2,3},{3,2},{4,5},{5,4},{6,7},{7,6},{8,9},{9,8},{10,11... | collective-permute-start | bytes 196616 | tf_op jit(solution)/shard_map/ppermute | solution.py:218
  46.3 61.1 %copy-start = (bf16[512,1024]{1,0:T(8,128)(2,1)S(1)}, bf16[512,1024]{1,0:T(8,128)(2,1)}, u32[]{:S(2)}) copy-start(bf16[512,1024]{1,0:T(8,128)(2,1)} %get-tuple-element.17.refs_4_) | copy-start | bytes 3145732
  49.1 5.0 %copy-start.4 = (bf16[2,32,1024]{2,1,0:T(8,128)(2,1)}, bf16[2,32,1024]{2,1,0:T(8,128)(2,1)S(1)}, u32[]{:S(2)}) copy-start(bf16[2,32,1024]{2,1,0:T(8,128)(2,1)S(1)} %pad_maximum_fusion.refs_0_) | copy-start | bytes 393220
  49.1 7.8 %collective-permute-start.3 = (bf16[2,32,1024]{2,1,0:T(8,128)(2,1)S(1)}, bf16[2,32,1024]{2,1,0:T(8,128)(2,1)S(1)}, u32[]{:S(2)}, u32[]{:S(2)}) collective-permute-start(bf16[2,32,1024]{2,1,0:T(8,128)(2,1)S(1)} %pad_maximum_fusion.refs_0_), channel_id=1, source_target_pairs={{0,16},{4,20},{8,24},{12,28},{16,32},{20,36},{24,40},{28,44},{32,4... | collective-permute-start | bytes 393224 | tf_op jit(solution)/shard_map/ppermute | solution.py:226
  50.5 10.7 %collective-permute-start.4 = (bf16[2,32,1024]{2,1,0:T(8,128)(2,1)S(1)}, bf16[2,32,1024]{2,1,0:T(8,128)(2,1)S(1)}, u32[]{:S(2)}, u32[]{:S(2)}) collective-permute-start(bf16[2,32,1024]{2,1,0:T(8,128)(2,1)S(1)} %pad_maximum_fusion.refs_0_), channel_id=1, source_target_pairs={{0,32},{4,36},{8,40},{12,44},{16,48},{20,52},{24,56},{28,60},{32,0... | collective-permute-start | bytes 393224 | tf_op jit(solution)/shard_map/ppermute | solution.py:226
  52.9 9.0 %collective-permute-start.5 = (bf16[2,32,1024]{2,1,0:T(8,128)(2,1)S(1)}, bf16[2,32,1024]{2,1,0:T(8,128)(2,1)}, u32[]{:S(2)}, u32[]{:S(2)}) collective-permute-start(bf16[2,32,1024]{2,1,0:T(8,128)(2,1)S(1)} %pad_maximum_fusion.refs_0_), channel_id=1, source_target_pairs={{0,48},{4,52},{8,56},{12,60},{16,0},{20,4},{24,8},{28,12},{32,16},... | collective-permute-start | bytes 393224 | tf_op jit(solution)/shard_map/ppermute | solution.py:226
  56.9 4.2 %copy-start.6 = (bf16[2,32,1024]{2,1,0:T(8,128)(2,1)}, bf16[2,32,1024]{2,1,0:T(8,128)(2,1)S(1)}, u32[]{:S(2)}) copy-start(bf16[2,32,1024]{2,1,0:T(8,128)(2,1)S(1)} %collective-permute-done.3.refs_1_) | copy-start | bytes 393220
  61.2 0.7 copy-start.7
  65.1 0.9 copy-start.2
  73.3 6.4 %collective-permute-start.15 = (bf16[512,256]{1,0:T(8,128)(2,1)S(1)}, bf16[512,256]{1,0:T(8,128)(2,1)S(1)}, u32[]{:S(2)}, u32[]{:S(2)}) collective-permute-start(bf16[512,256]{1,0:T(8,128)(2,1)S(1)} %get-tuple-element.14.refs_0_), channel_id=1, source_target_pairs={{0,1},{1,0},{2,3},{3,2},{4,5},{5,4},{6,7},{7,6},{8,9},{9,8},{10,11... | collective-permute-start | bytes 786440 | tf_op jit(solution)/shard_map/ppermute | solution.py:257
  76.0 5.8 %collective-permute-start.16 = (bf16[512,256]{1,0:T(8,128)(2,1)S(1)}, bf16[512,256]{1,0:T(8,128)(2,1)S(1)}, u32[]{:S(2)}, u32[]{:S(2)}) collective-permute-start(bf16[512,256]{1,0:T(8,128)(2,1)S(1)} %get-tuple-element.15.refs_1_), channel_id=1, source_target_pairs={{0,1},{1,0},{2,3},{3,2},{4,5},{5,4},{6,7},{7,6},{8,9},{9,8},{10,11... | collective-permute-start | bytes 786440 | tf_op jit(solution)/shard_map/ppermute | solution.py:257
  76.1 12.8 %collective-permute-start.6 = (bf16[512,256]{1,0:T(8,128)(2,1)S(1)}, bf16[512,256]{1,0:T(8,128)(2,1)S(1)}, u32[]{:S(2)}, u32[]{:S(2)}) collective-permute-start(bf16[512,256]{1,0:T(8,128)(2,1)S(1)} %get-tuple-element.14.refs_0_), channel_id=1, source_target_pairs={{0,8},{1,9},{4,12},{5,13},{8,2},{9,3},{12,6},{13,7},{2,10},{3,11},... | collective-permute-start | bytes 786440 | tf_op jit(solution)/shard_map/ppermute | solution.py:45
  76.3 16.0 %collective-permute-start.8 = (bf16[512,256]{1,0:T(8,128)(2,1)S(1)}, bf16[512,256]{1,0:T(8,128)(2,1)S(1)}, u32[]{:S(2)}, u32[]{:S(2)}) collective-permute-start(bf16[512,256]{1,0:T(8,128)(2,1)S(1)} %get-tuple-element.15.refs_1_), channel_id=1, source_target_pairs={{0,10},{1,11},{4,14},{5,15},{8,0},{9,1},{12,4},{13,5},{2,8},{3,9},... | collective-permute-start | bytes 786440 | tf_op jit(solution)/shard_map/ppermute | solution.py:45
  79.6 29.2 %collective-permute-start.12 = (bf16[2,4,32,1024]{3,2,1,0:T(8,128)(2,1)}, bf16[2,4,32,1024]{3,2,1,0:T(8,128)(2,1)S(1)}, u32[]{:S(2)}, u32[]{:S(2)}) collective-permute-start(bf16[2,4,32,1024]{3,2,1,0:T(8,128)(2,1)} %get-tuple-element.16.refs_0_), channel_id=1, source_target_pairs={{0,64},{4,68},{8,72},{12,76},{16,80},{20,84},{24,88},{28,92},{32,9... | collective-permute-start | bytes 1572872 | tf_op jit(solution)/shard_map/ppermute | solution.py:268
  79.7 29.2 %collective-permute-start.13 = (bf16[2,4,32,1024]{3,2,1,0:T(8,128)(2,1)}, bf16[2,4,32,1024]{3,2,1,0:T(8,128)(2,1)S(1)}, u32[]{:S(2)}, u32[]{:S(2)}) collective-permute-start(bf16[2,4,32,1024]{3,2,1,0:T(8,128)(2,1)} %get-tuple-element.16.refs_0_), channel_id=1, source_target_pairs={{0,128},{4,132},{8,136},{12,140},{16,144},{20,148},{24,152},{28,15... | collective-permute-start | bytes 1572872 | tf_op jit(solution)/shard_map/ppermute | solution.py:268
  81.8 27.1 %collective-permute-start.14 = (bf16[2,4,32,1024]{3,2,1,0:T(8,128)(2,1)}, bf16[2,4,32,1024]{3,2,1,0:T(8,128)(2,1)S(1)}, u32[]{:S(2)}, u32[]{:S(2)}) collective-permute-start(bf16[2,4,32,1024]{3,2,1,0:T(8,128)(2,1)} %get-tuple-element.16.refs_0_), channel_id=1, source_target_pairs={{0,192},{4,196},{8,200},{12,204},{16,208},{20,212},{24,216},{28,22... | collective-permute-start | bytes 1572872 | tf_op jit(solution)/shard_map/ppermute | solution.py:268
  88.9 8.2 %collective-permute-start.7 = (bf16[512,256]{1,0:T(8,128)(2,1)S(1)}, bf16[512,256]{1,0:T(8,128)(2,1)S(1)}, u32[]{:S(2)}, u32[]{:S(2)}) collective-permute-start(bf16[512,256]{1,0:T(8,128)(2,1)S(1)} %collective-permute-done.6), channel_id=1, source_target_pairs={{0,8},{1,9},{4,12},{5,13},{8,2},{9,3},{12,6},{13,7},{2,10},{3,11},... | collective-permute-start | bytes 786440 | tf_op jit(solution)/shard_map/ppermute | solution.py:45
  92.2 14.6 %collective-permute-start.9 = (bf16[512,256]{1,0:T(8,128)(2,1)S(1)}, bf16[512,256]{1,0:T(8,128)(2,1)S(1)}, u32[]{:S(2)}, u32[]{:S(2)}) collective-permute-start(bf16[512,256]{1,0:T(8,128)(2,1)S(1)} %collective-permute-done.8), channel_id=1, source_target_pairs={{0,10},{1,11},{4,14},{5,15},{8,0},{9,1},{12,4},{13,5},{2,8},{3,9},... | collective-permute-start | bytes 786440 | tf_op jit(solution)/shard_map/ppermute | solution.py:45
  97.1 12.9 %collective-permute-start.10 = (bf16[512,256]{1,0:T(8,128)(2,1)S(1)}, bf16[512,256]{1,0:T(8,128)(2,1)S(1)}, u32[]{:S(2)}, u32[]{:S(2)}) collective-permute-start(bf16[512,256]{1,0:T(8,128)(2,1)S(1)} %collective-permute-done.7.refs_0_), channel_id=1, source_target_pairs={{0,1},{1,0},{2,3},{3,2},{4,5},{5,4},{6,7},{7,6},{8,9},{9,8},{10,11... | collective-permute-start | bytes 786440 | tf_op jit(solution)/shard_map/ppermute | solution.py:258
  106.9 3.1 %collective-permute-start.11 = (bf16[512,256]{1,0:T(8,128)(2,1)S(1)}, bf16[512,256]{1,0:T(8,128)(2,1)S(1)}, u32[]{:S(2)}, u32[]{:S(2)}) collective-permute-start(bf16[512,256]{1,0:T(8,128)(2,1)S(1)} %collective-permute-done.9.refs_1_), channel_id=1, source_target_pairs={{0,1},{1,0},{2,3},{3,2},{4,5},{5,4},{6,7},{7,6},{8,9},{9,8},{10,11... | collective-permute-start | bytes 786440 | tf_op jit(solution)/shard_map/ppermute | solution.py:258

commit v4 on v3

--- a/solution.py
+++ b/solution.py
@@ -16,6 +16,7 @@
 FACTOR = HEAD ** -0.5
 LOG2E = 1.4426950408889634
 CALLS = 1
+TOGETHER = 2
 PARTS = 2
 
 SWAP_CORE = [(0, 1), (1, 0), (2, 3), (3, 2)]
@@ -102,43 +103,34 @@
         copy.wait()
 
 
-def weights_kernel(*refs):
-    *quarter_refs, out_ref, sems = refs
-    y = lax.shift_right_logical(lax.axis_index("ctx"), 4)
-    copies = []
-    for k, ref in enumerate(quarter_refs):
-        at = lax.bitwise_and(y + (4 - k), 3)
-        copies.append(pltpu.make_async_copy(ref, out_ref.at[:, at], sems.at[k]))
-        copies[-1].start()
-    for copy in copies:
-        copy.wait()
-
-
 def attend_kernel(ok_ref, q_ref, k_ref, v_ref, got_ref, pass_ref, *out_refs, rows):
     out_refs = out_refs[:PARTS]
     half = got_ref.shape[0] // 2
     heads = q_ref.shape[0]
     contract = (((1,), (1,)), ((), ()))
-    for h in range(heads):
-        for r in range(0, BLK, rows):
+    tiles = [(h, r) for h in range(heads) for r in range(0, BLK, rows)]
+    for first in range(0, len(tiles), TOGETHER):
+        group = tiles[first : first + TOGETHER]
+        scores = []
+        for h, r in group:
             q = q_ref[h, r : r + rows, :]
-            seen = r + rows
-            near = lax.dot_general(q, k_ref[:seen, :], contract, preferred_element_type=jnp.float32)
+            near = lax.dot_general(q, k_ref[: r + rows, :], contract, preferred_element_type=jnp.float32)
             row = lax.broadcasted_iota(jnp.int32, near.shape, 0) + r
             col = lax.broadcasted_iota(jnp.int32, near.shape, 1)
             near = jnp.where(col <= row, near, -jnp.inf)
             far = []
             for j in range(TOPK):
                 k_j = got_ref[:half, j * PIECE : (j + 1) * PIECE, :].reshape(BLK, HEAD)
-                s = lax.dot_general(q, k_j, contract, preferred_element_type=jnp.float32)
-                far.append(s)
+                far.append(lax.dot_general(q, k_j, contract, preferred_element_type=jnp.float32))
+            scores.append((near, far))
+        for (h, r), (near, far) in zip(group, scores):
             highest = jnp.max(near, axis=1, keepdims=True)
             for j, s in enumerate(far):
                 here = jnp.max(s, axis=1, keepdims=True)
                 highest = jnp.maximum(highest, jnp.where(ok_ref[j] != 0, here, -jnp.inf))
             w = jnp.exp2((near - highest) * (FACTOR * LOG2E))
             total = jnp.sum(w, axis=1, keepdims=True)
-            acc = jnp.dot(w.astype(jnp.bfloat16), v_ref[:seen, :], preferred_element_type=jnp.float32)
+            acc = jnp.dot(w.astype(jnp.bfloat16), v_ref[: r + rows, :], preferred_element_type=jnp.float32)
             for j in range(TOPK):
                 v_j = got_ref[half:, j * PIECE : (j + 1) * PIECE, :].reshape(BLK, HEAD)
                 w = jnp.exp2((far[j] - jnp.where(ok_ref[j] != 0, highest, jnp.inf)) * (FACTOR * LOG2E))
@@ -170,11 +162,17 @@
 
 
 def last_kernel(*refs):
-    *part_refs, w_ref, near_ref, out_ref, lhs, sems = refs
-    copies = fetch(part_refs, lhs, sems)
-    for copy in copies:
-        copy.wait()
-    w = w_ref[...].reshape(lhs.shape[1], -1)
+    *data_refs, near_ref, out_ref, lhs, w_far, sems = refs
+    part_refs, quarter_refs = data_refs[:-4], data_refs[-4:]
+    y = lax.shift_right_logical(lax.axis_index("ctx"), 4)
+    copies = []
+    for k, ref in enumerate(quarter_refs):
+        at = lax.bitwise_and(y + (4 - k), 3)
+        copies.append(pltpu.make_async_copy(ref, w_far.at[:, at], sems.at[len(part_refs) + k]))
+        copies[-1].start()
+    for copy in fetch(part_refs, lhs, sems) + copies:
+        copy.wait()
+    w = w_far[...].reshape(lhs.shape[1], -1)
     far = jnp.dot(lhs[...], w, preferred_element_type=jnp.float32)
     out_ref[...] = (near_ref[...] + far).astype(jnp.bfloat16)
 
@@ -257,15 +255,7 @@
     a_core = [lax.ppermute(a, "head", SWAP_CORE) for a in a_own]
     a_zc = [lax.ppermute(a, "head", SWAP_CORE) for a in a_z]
 
-    w_far = pl.pallas_call(
-        weights_kernel,
-        out_shape=jax.ShapeDtypeStruct((2, 4, 4, share, cols), bf16),
-        in_specs=[hbm] * 4,
-        out_specs=vmem,
-        scratch_shapes=[pltpu.SemaphoreType.DMA((4,))],
-        compiler_params=params,
-        name="weights",
-    )(quarter, *[lax.ppermute(quarter, "ctx", along_y(k)) for k in (1, 2, 3)])
+    quarters = [quarter] + [lax.ppermute(quarter, "ctx", along_y(k)) for k in (1, 2, 3)]
     w_core = lax.ppermute(w_core, "head", SWAP_CORE)
     lhs = pltpu.VMEM((BLK, 8 * HEAD), bf16)
     near = pl.pallas_call(
@@ -280,12 +270,16 @@
     return pl.pallas_call(
         last_kernel,
         out_shape=jax.ShapeDtypeStruct((BLK, cols), bf16),
-        in_specs=[hbm] * (2 * len(a_own)) + [vmem] * 2,
-        out_specs=vmem,
-        scratch_shapes=[lhs, pltpu.SemaphoreType.DMA((2 * len(a_own),))],
+        in_specs=[hbm] * (2 * len(a_own) + 4) + [vmem],
+        out_specs=vmem,
+        scratch_shapes=[
+            lhs,
+            pltpu.VMEM((2, 4, 4, share, cols), bf16),
+            pltpu.SemaphoreType.DMA((2 * len(a_own) + 4,)),
+        ],
         compiler_params=params,
         name="last",
-    )(*a_z, *a_zc, w_far, near)
+    )(*a_z, *a_zc, *quarters, near)
 
 
 def solution(mesh):

time: 113 us -> 112 us (level)
  starting transfers between devices: 59.2 us -> 54 us
  waiting for transfers between devices: 25.4 us -> 30.5 us
  Pallas kernels: 21.4 us -> 20.2 us
    ppermute x2, starting transfers between devices: 8.96 us -> 3.7 us  [local(): a_zc = [lax.ppermute(a, 'head', SWAP_CORE) for a in a_z]]
    ppermute x4, waiting for transfers between devices: 10.8 us -> 15.8 us  [over_z(): a = lax.ppermute(a, ('ctx', 'head'), along_z(step))]
  transfers between devices with their start and end apart: 20 -> 20, of which waited for: 9 -> 9; matrix products, arithmetic and copies ran while one was open for 4% -> 4% of each run, Pallas kernels for 13% -> 11%
where the time goes in v4:
time: 112 us; the launch traced here: 111 us
  starting transfers between devices  54 us (48%)
  waiting for transfers between devices  30.5 us (27%)
  Pallas kernels  20.2 us (18%)
  local copies, waits for them, and re-layouts  3.93 us (4%)
  other arithmetic  2.21 us (2%)
    ppermute x4, waiting for transfers between devices, over_z(): a = lax.ppermute(a, ('ctx', 'head'), along_z(step))  15.8 us
    all_to_all x1, starting transfers between devices, local(): held = lax.all_to_all(spread, 'ctx', 0, 0, tiled=True)  12.6 us
    all_to_all x1, starting transfers between devices, local(): got = lax.all_to_all(packed, 'ctx', 0, 0, tiled=True)  9.9 us
    ppermute x4, starting transfers between devices, over_z(): a = lax.ppermute(a, ('ctx', 'head'), along_z(step))  8.59 us
    ppermute x3, waiting for transfers between devices, local(): lax.ppermute(both, 'ctx', along_x(k))  6.5 us
    pallas_call x1, Pallas kernels, local(): pl.pallas_call(functools.partial(attend_kernel, rows=256), out_shape=(par...  6.25 us
    all_to_all x1, waiting for transfers between devices, local(): held = lax.all_to_all(spread, 'ctx', 0, 0, tiled=True)  6.03 us
    ppermute x3, starting transfers between devices, local(): lax.ppermute(both, 'ctx', along_x(k))  4.95 us
  transfers between devices with their start and end apart: 20, of which 9 were waited for; matrix products, arithmetic and copies ran while one was open for 4% of the time, Pallas kernels for 11%

profile of v4, /device:TPU:1, one launch (start us, length us, event | category | flops | bytes accessed | tf_op | source)
XLA Modules:
  0.0 111.2 jit_solution(4286521649845003599)
XLA Ops:
  0.0 1.9 %spread.1 = bf16[64,24,128]{2,1,0:T(8,128)(2,1)} custom-call(s32[64]{0:T(128)} %order_ref.1, s32[3]{0:T(128)} %bitcast.18, bf16[512,128]{1,0:T(8,128)(2,1)} %bitcast.12, bf16[512,128]{1,0:T(8,128)(2,1)} %bitcast.14), custom_call_target="tpu_custom_call" | custom-call | tf_op jit(solution)/shard_map/spread/pallas_call | solution.py:207
  1.9 12.6 %all-to-all-start = ((bf16[64,24,128]{2,1,0:T(8,128)(2,1)}), bf16[64,24,128]{2,1,0:T(8,128)(2,1)S(1)}, u32[]{:S(2)}, u32[]{:S(2)}) async-start(bf16[64,24,128]{2,1,0:T(8,128)(2,1)} %spread.1), calls=%async_computation | async-start | bytes 786432 | tf_op jit(solution)/shard_map/all_to_all | solution.py:214
  14.5 3.1 %cut.1 = (bf16[32,1024]{1,0:T(8,128)(2,1)}, bf16[32,1024]{1,0:T(8,128)(2,1)}, bf16[512,1024]{1,0:T(8,128)(2,1)}, bf16[512,1024]{1,0:T(8,128)(2,1)}) custom-call(bf16[512,4096]{1,0:T(8,128)(2,1)} %w_ref.1), custom_call_target="tpu_custom_call" | custom-call | tf_op jit(solution)/shard_map/cut/pallas_call | solution.py:196
  17.6 4.3 %collective-permute-start.1 = (bf16[32,1024]{1,0:T(8,128)(2,1)}, bf16[32,1024]{1,0:T(8,128)(2,1)S(1)}, u32[]{:S(2)}, u32[]{:S(2)}) collective-permute-start(bf16[32,1024]{1,0:T(8,128)(2,1)} %get-tuple-element.13), channel_id=1, source_target_pairs={{0,2},{2,0},{1,3},{3,1},{4,6},{6,4},{5,7},{7,5},{8,10},{10,8},{9,1... | collective-permute-start | bytes 196616 | tf_op jit(solution)/shard_map/ppermute | solution.py:205
  21.9 1.2 %collective-permute-start = (bf16[32,1024]{1,0:T(8,128)(2,1)}, bf16[32,1024]{1,0:T(8,128)(2,1)S(1)}, u32[]{:S(2)}, u32[]{:S(2)}) collective-permute-start(bf16[32,1024]{1,0:T(8,128)(2,1)} %get-tuple-element.12), channel_id=1, source_target_pairs={{0,2},{2,0},{1,3},{3,1},{4,6},{6,4},{5,7},{7,5},{8,10},{10,8},{9,1... | collective-permute-start | bytes 196616 | tf_op jit(solution)/shard_map/ppermute | solution.py:204
  23.0 6.0 %all-to-all-done.held_ref = bf16[64,24,128]{2,1,0:T(8,128)(2,1)S(1)} async-done(((bf16[64,24,128]{2,1,0:T(8,128)(2,1)}), bf16[64,24,128]{2,1,0:T(8,128)(2,1)S(1)}, u32[]{:S(2)}, u32[]{:S(2)}) %all-to-all-start) | async-done | bytes 393248 | tf_op jit(solution)/shard_map/all_to_all | solution.py:214
  30.4 2.2 %pack.1 = bf16[64,48,128]{2,1,0:T(8,128)(2,1)} custom-call(s32[64,3]{1,0:T(8,128)} %bitcast.17, bf16[64,24,128]{2,1,0:T(8,128)(2,1)} %copy-done.3, bf16[32,1024]{1,0:T(8,128)(2,1)} %copy-done.5, bf16[32,1024]{1,0:T(8,128)(2,1)} %copy-done.8), custom_call_target="tpu_custom_call" | custom-call | tf_op jit(solution)/shard_map/pack/pallas_call | solution.py:227
  32.7 9.9 %all-to-all-start.1 = ((bf16[64,48,128]{2,1,0:T(8,128)(2,1)}), bf16[64,48,128]{2,1,0:T(8,128)(2,1)S(1)}, u32[]{:S(2)}, u32[]{:S(2)}) async-start(bf16[64,48,128]{2,1,0:T(8,128)(2,1)} %pack.1), calls=%async_computation.1 | async-start | bytes 1572864 | tf_op jit(solution)/shard_map/all_to_all | solution.py:234
  42.6 2.8 %collective-permute-start.17 = (bf16[512,1024]{1,0:T(8,128)(2,1)}, bf16[512,1024]{1,0:T(8,128)(2,1)S(1)}, u32[]{:S(2)}, u32[]{:S(2)}) collective-permute-start(bf16[512,1024]{1,0:T(8,128)(2,1)} %get-tuple-element.18), channel_id=1, source_target_pairs={{0,1},{1,0},{2,3},{3,2},{4,5},{5,4},{6,7},{7,6},{8,9},{9,8},{10,11... | collective-permute-start | bytes 3145736 | tf_op jit(solution)/shard_map/ppermute | solution.py:259
  46.1 1.1 copy.10
  48.9 1.4 %collective-permute-start.3 = (bf16[2,32,1024]{2,1,0:T(8,128)(2,1)S(1)}, bf16[2,32,1024]{2,1,0:T(8,128)(2,1)S(1)}, u32[]{:S(2)}, u32[]{:S(2)}) collective-permute-start(bf16[2,32,1024]{2,1,0:T(8,128)(2,1)S(1)} %pad_maximum_fusion.refs_0_), channel_id=1, source_target_pairs={{0,16},{4,20},{8,24},{12,28},{16,32},{20,36},{24,40},{28,44},{32,4... | collective-permute-start | bytes 393224 | tf_op jit(solution)/shard_map/ppermute | solution.py:224
  50.2 2.4 %collective-permute-start.4 = (bf16[2,32,1024]{2,1,0:T(8,128)(2,1)S(1)}, bf16[2,32,1024]{2,1,0:T(8,128)(2,1)S(1)}, u32[]{:S(2)}, u32[]{:S(2)}) collective-permute-start(bf16[2,32,1024]{2,1,0:T(8,128)(2,1)S(1)} %pad_maximum_fusion.refs_0_), channel_id=1, source_target_pairs={{0,32},{4,36},{8,40},{12,44},{16,48},{20,52},{24,56},{28,60},{32,0... | collective-permute-start | bytes 393224 | tf_op jit(solution)/shard_map/ppermute | solution.py:224
  52.6 1.2 %collective-permute-start.5 = (bf16[2,32,1024]{2,1,0:T(8,128)(2,1)S(1)}, bf16[2,32,1024]{2,1,0:T(8,128)(2,1)}, u32[]{:S(2)}, u32[]{:S(2)}) collective-permute-start(bf16[2,32,1024]{2,1,0:T(8,128)(2,1)S(1)} %pad_maximum_fusion.refs_0_), channel_id=1, source_target_pairs={{0,48},{4,52},{8,56},{12,60},{16,0},{20,4},{24,8},{28,12},{32,16},... | collective-permute-start | bytes 393224 | tf_op jit(solution)/shard_map/ppermute | solution.py:224
  54.5 2.3 %collective-permute-done.3.refs_1_ = bf16[2,32,1024]{2,1,0:T(8,128)(2,1)S(1)} collective-permute-done((bf16[2,32,1024]{2,1,0:T(8,128)(2,1)S(1)}, bf16[2,32,1024]{2,1,0:T(8,128)(2,1)S(1)}, u32[]{:S(2)}, u32[]{:S(2)}) %collective-permute-start.3) | collective-permute-done | bytes 131104 | tf_op jit(solution)/shard_map/ppermute | solution.py:224
  56.7 4.2 %collective-permute-done.4.refs_2_ = bf16[2,32,1024]{2,1,0:T(8,128)(2,1)S(1)} collective-permute-done((bf16[2,32,1024]{2,1,0:T(8,128)(2,1)S(1)}, bf16[2,32,1024]{2,1,0:T(8,128)(2,1)S(1)}, u32[]{:S(2)}, u32[]{:S(2)}) %collective-permute-start.4) | collective-permute-done | bytes 131104 | tf_op jit(solution)/shard_map/ppermute | solution.py:224
  61.6 1.9 %merge_x.1.pass_ref = bf16[2,4,32,1024]{3,2,1,0:T(8,128)(2,1)} custom-call(bf16[2,32,1024]{2,1,0:T(8,128)(2,1)} %copy-done.4, bf16[2,32,1024]{2,1,0:T(8,128)(2,1)} %copy-done.6, bf16[2,32,1024]{2,1,0:T(8,128)(2,1)} %copy-done.7, bf16[2,32,1024]{2,1,0:T(8,128)(2,1)} %collective-permute-done.5.refs_3_), custom_call_target="tpu_custom_call" | custom-call | tf_op jit(solution)/shard_map/merge_x/pallas_call | solution.py:217
  63.6 1.3 %all-to-all-done.1.got_ref = bf16[64,48,128]{2,1,0:T(8,128)(2,1)S(1)} async-done(((bf16[64,48,128]{2,1,0:T(8,128)(2,1)}), bf16[64,48,128]{2,1,0:T(8,128)(2,1)S(1)}, u32[]{:S(2)}, u32[]{:S(2)}) %all-to-all-start.1) | async-done | bytes 786464 | tf_op jit(solution)/shard_map/all_to_all | solution.py:234
  64.9 0.9 copy-done.2
  65.8 6.2 %attend.1 = (bf16[512,256]{1,0:T(8,128)(2,1)S(1)}, bf16[512,256]{1,0:T(8,128)(2,1)S(1)}, bf16[2,4,32,1024]{3,2,1,0:T(8,128)(2,1)}) custom-call(s32[3]{0:T(128)S(1)} %compare_convert_fusion.ok_ref, bf16[4,512,128]{2,1,0:T(8,128)(2,1)S(1)} %bitcast.11, bf16[512,128]{1,0:T(8,128)(2,1)S(1)} %bitcast.13, ...), custom_call_target="tpu_custom_call", output_to_operand_aliasing={{2}: (5, {})} | custom-call | flops 1048576 | bytes 1024 | tf_op jit(solution)/shard_map/attend/pallas_call | solution.py:243
  72.1 2.7 %collective-permute-start.15 = (bf16[512,256]{1,0:T(8,128)(2,1)S(1)}, bf16[512,256]{1,0:T(8,128)(2,1)S(1)}, u32[]{:S(2)}, u32[]{:S(2)}) collective-permute-start(bf16[512,256]{1,0:T(8,128)(2,1)S(1)} %get-tuple-element.14.refs_0_), channel_id=1, source_target_pairs={{0,1},{1,0},{2,3},{3,2},{4,5},{5,4},{6,7},{7,6},{8,9},{9,8},{10,11... | collective-permute-start | bytes 786440 | tf_op jit(solution)/shard_map/ppermute | solution.py:255
  75.1 3.4 %collective-permute-start.8 = (bf16[512,256]{1,0:T(8,128)(2,1)S(1)}, bf16[512,256]{1,0:T(8,128)(2,1)S(1)}, u32[]{:S(2)}, u32[]{:S(2)}) collective-permute-start(bf16[512,256]{1,0:T(8,128)(2,1)S(1)} %get-tuple-element.15.refs_1_), channel_id=1, source_target_pairs={{0,10},{1,11},{4,14},{5,15},{8,0},{9,1},{12,4},{13,5},{2,8},{3,9},... | collective-permute-start | bytes 786440 | tf_op jit(solution)/shard_map/ppermute | solution.py:46
  78.5 2.1 %collective-permute-start.13 = (bf16[2,4,32,1024]{3,2,1,0:T(8,128)(2,1)}, bf16[2,4,32,1024]{3,2,1,0:T(8,128)(2,1)S(1)}, u32[]{:S(2)}, u32[]{:S(2)}) collective-permute-start(bf16[2,4,32,1024]{3,2,1,0:T(8,128)(2,1)} %get-tuple-element.16.refs_4_), channel_id=1, source_target_pairs={{0,128},{4,132},{8,136},{12,140},{16,144},{20,148},{24,152},{28,15... | collective-permute-start | bytes 1572872 | tf_op jit(solution)/shard_map/ppermute | solution.py:258
  80.6 1.1 collective-permute-start.14
  81.7 5.8 %collective-permute-done.6 = bf16[512,256]{1,0:T(8,128)(2,1)S(1)} collective-permute-done((bf16[512,256]{1,0:T(8,128)(2,1)S(1)}, bf16[512,256]{1,0:T(8,128)(2,1)S(1)}, u32[]{:S(2)}, u32[]{:S(2)}) %collective-permute-start.6) | collective-permute-done | bytes 262176 | tf_op jit(solution)/shard_map/ppermute | solution.py:46
  87.4 1.8 %collective-permute-start.7 = (bf16[512,256]{1,0:T(8,128)(2,1)S(1)}, bf16[512,256]{1,0:T(8,128)(2,1)S(1)}, u32[]{:S(2)}, u32[]{:S(2)}) collective-permute-start(bf16[512,256]{1,0:T(8,128)(2,1)S(1)} %collective-permute-done.6), channel_id=1, source_target_pairs={{0,8},{1,9},{4,12},{5,13},{8,2},{9,3},{12,6},{13,7},{2,10},{3,11},... | collective-permute-start | bytes 786440 | tf_op jit(solution)/shard_map/ppermute | solution.py:46
  89.2 1.8 %collective-permute-done.8 = bf16[512,256]{1,0:T(8,128)(2,1)S(1)} collective-permute-done((bf16[512,256]{1,0:T(8,128)(2,1)S(1)}, bf16[512,256]{1,0:T(8,128)(2,1)S(1)}, u32[]{:S(2)}, u32[]{:S(2)}) %collective-permute-start.8) | collective-permute-done | bytes 262176 | tf_op jit(solution)/shard_map/ppermute | solution.py:46
  91.1 3.2 %collective-permute-start.9 = (bf16[512,256]{1,0:T(8,128)(2,1)S(1)}, bf16[512,256]{1,0:T(8,128)(2,1)S(1)}, u32[]{:S(2)}, u32[]{:S(2)}) collective-permute-start(bf16[512,256]{1,0:T(8,128)(2,1)S(1)} %collective-permute-done.8), channel_id=1, source_target_pairs={{0,10},{1,11},{4,14},{5,15},{8,0},{9,1},{12,4},{13,5},{2,8},{3,9},... | collective-permute-start | bytes 786440 | tf_op jit(solution)/shard_map/ppermute | solution.py:46
  94.3 4.1 %collective-permute-done.7.refs_0_ = bf16[512,256]{1,0:T(8,128)(2,1)S(1)} collective-permute-done((bf16[512,256]{1,0:T(8,128)(2,1)S(1)}, bf16[512,256]{1,0:T(8,128)(2,1)S(1)}, u32[]{:S(2)}, u32[]{:S(2)}) %collective-permute-start.7) | collective-permute-done | bytes 262176 | tf_op jit(solution)/shard_map/ppermute | solution.py:46
  98.4 3.2 %collective-permute-start.10 = (bf16[512,256]{1,0:T(8,128)(2,1)S(1)}, bf16[512,256]{1,0:T(8,128)(2,1)S(1)}, u32[]{:S(2)}, u32[]{:S(2)}) collective-permute-start(bf16[512,256]{1,0:T(8,128)(2,1)S(1)} %collective-permute-done.7.refs_0_), channel_id=1, source_target_pairs={{0,1},{1,0},{2,3},{3,2},{4,5},{5,4},{6,7},{7,6},{8,9},{9,8},{10,11... | collective-permute-start | bytes 786440 | tf_op jit(solution)/shard_map/ppermute | solution.py:256
  101.5 4.1 %collective-permute-done.9.refs_1_ = bf16[512,256]{1,0:T(8,128)(2,1)S(1)} collective-permute-done((bf16[512,256]{1,0:T(8,128)(2,1)S(1)}, bf16[512,256]{1,0:T(8,128)(2,1)S(1)}, u32[]{:S(2)}, u32[]{:S(2)}) %collective-permute-start.9) | collective-permute-done | bytes 262176 | tf_op jit(solution)/shard_map/ppermute | solution.py:46
  106.2 1.4 %near.1.refs_8_ = f32[512,1024]{1,0:T(8,128)S(1)} custom-call(bf16[512,256]{1,0:T(8,128)(2,1)S(1)} %get-tuple-element.14.refs_0_, bf16[512,256]{1,0:T(8,128)(2,1)S(1)} %get-tuple-element.15.refs_1_, bf16[512,256]{1,0:T(8,128)(2,1)S(1)} %collective-permute-done.15.refs_2_, bf16[512,256]{1,0:T(8,128)(2,1)S(1)} %collective-permute-done.16.refs_3_, ...), custom_call_target="tpu_custom_call" | custom-call | tf_op jit(solution)/shard_map/near/pallas_call | solution.py:261
  107.7 3.4 %last.1 = bf16[512,1024]{1,0:T(8,128)(2,1)} custom-call(bf16[512,256]{1,0:T(8,128)(2,1)S(1)} %collective-permute-done.7.refs_0_, bf16[512,256]{1,0:T(8,128)(2,1)S(1)} %collective-permute-done.9.refs_1_, bf16[512,256]{1,0:T(8,128)(2,1)S(1)} %collective-permute-done.10.refs_2_, bf16[512,256]{1,0:T(8,128)(2,1)S(1)} %collective-permute-done.11.refs_3_, ...), custom_call_target="tpu_custom_call" | custom-call | tf_op jit(solution)/shard_map/last/pallas_call | solution.py:270
  (42 shorter events, 5.9 us)
Async XLA Ops:
  0.0 45.5 %copy-start.9 = (s32[64]{0:T(128)S(1)}, s32[64]{0:T(128)}, u32[]{:S(2)}) copy-start(s32[64]{0:T(128)} %order_ref.1) | copy-start | bytes 772
  1.9 27.2 %all-to-all-start = ((bf16[64,24,128]{2,1,0:T(8,128)(2,1)}), bf16[64,24,128]{2,1,0:T(8,128)(2,1)S(1)}, u32[]{:S(2)}, u32[]{:S(2)}) async-start(bf16[64,24,128]{2,1,0:T(8,128)(2,1)} %spread.1), calls=%async_computation | async-start | bytes 786432 | tf_op jit(solution)/shard_map/all_to_all | solution.py:214
  14.5 39.4 %copy-start.10 = (s32[1,1,3]{2,1,0:T(1,128)S(1)}, s32[1,1,3]{2,1,0:T(1,128)}, u32[]{:S(2)}) copy-start(s32[1,1,3]{2,1,0:T(1,128)} %param.11) | copy-start | bytes 40
  14.5 50.4 %copy-start.1 = (bf16[512,1,128]{2,0,1:T(8,128)(2,1)S(1)}, bf16[512,1,128]{2,0,1:T(8,128)(2,1)}, u32[]{:S(2)}) copy-start(bf16[512,1,128]{2,0,1:T(8,128)(2,1)} %param.7) | copy-start | bytes 393220
  17.6 88.6 %copy-start = (bf16[512,1024]{1,0:T(8,128)(2,1)S(1)}, bf16[512,1024]{1,0:T(8,128)(2,1)}, u32[]{:S(2)}) copy-start(bf16[512,1024]{1,0:T(8,128)(2,1)} %get-tuple-element.17.refs_4_) | copy-start | bytes 3145732
  17.6 12.2 %collective-permute-start.1 = (bf16[32,1024]{1,0:T(8,128)(2,1)}, bf16[32,1024]{1,0:T(8,128)(2,1)S(1)}, u32[]{:S(2)}, u32[]{:S(2)}) collective-permute-start(bf16[32,1024]{1,0:T(8,128)(2,1)} %get-tuple-element.13), channel_id=1, source_target_pairs={{0,2},{2,0},{1,3},{3,1},{4,6},{6,4},{5,7},{7,5},{8,10},{10,8},{9,1... | collective-permute-start | bytes 196616 | tf_op jit(solution)/shard_map/ppermute | solution.py:205
  21.9 7.9 %collective-permute-start = (bf16[32,1024]{1,0:T(8,128)(2,1)}, bf16[32,1024]{1,0:T(8,128)(2,1)S(1)}, u32[]{:S(2)}, u32[]{:S(2)}) collective-permute-start(bf16[32,1024]{1,0:T(8,128)(2,1)} %get-tuple-element.12), channel_id=1, source_target_pairs={{0,2},{2,0},{1,3},{3,1},{4,6},{6,4},{5,7},{7,5},{8,10},{10,8},{9,1... | collective-permute-start | bytes 196616 | tf_op jit(solution)/shard_map/ppermute | solution.py:204
  29.1 0.8 copy-start.3
  29.8 0.6 copy-start.8
  29.8 0.6 copy-start.5
  32.7 32.2 %all-to-all-start.1 = ((bf16[64,48,128]{2,1,0:T(8,128)(2,1)}), bf16[64,48,128]{2,1,0:T(8,128)(2,1)S(1)}, u32[]{:S(2)}, u32[]{:S(2)}) async-start(bf16[64,48,128]{2,1,0:T(8,128)(2,1)} %pack.1), calls=%async_computation.1 | async-start | bytes 1572864 | tf_op jit(solution)/shard_map/all_to_all | solution.py:234
  42.6 35.8 %collective-permute-start.17 = (bf16[512,1024]{1,0:T(8,128)(2,1)}, bf16[512,1024]{1,0:T(8,128)(2,1)S(1)}, u32[]{:S(2)}, u32[]{:S(2)}) collective-permute-start(bf16[512,1024]{1,0:T(8,128)(2,1)} %get-tuple-element.18), channel_id=1, source_target_pairs={{0,1},{1,0},{2,3},{3,2},{4,5},{5,4},{6,7},{7,6},{8,9},{9,8},{10,11... | collective-permute-start | bytes 3145736 | tf_op jit(solution)/shard_map/ppermute | solution.py:259
  45.4 2.6 %collective-permute-start.2 = (bf16[32,1024]{1,0:T(8,128)(2,1)}, bf16[32,1024]{1,0:T(8,128)(2,1)}, u32[]{:S(2)}, u32[]{:S(2)}) collective-permute-start(bf16[32,1024]{1,0:T(8,128)(2,1)} %copy-done.8), channel_id=1, source_target_pairs={{0,1},{1,0},{2,3},{3,2},{4,5},{5,4},{6,7},{7,6},{8,9},{9,8},{10,11... | collective-permute-start | bytes 196616 | tf_op jit(solution)/shard_map/ppermute | solution.py:216
  48.9 5.0 %copy-start.4 = (bf16[2,32,1024]{2,1,0:T(8,128)(2,1)}, bf16[2,32,1024]{2,1,0:T(8,128)(2,1)S(1)}, u32[]{:S(2)}) copy-start(bf16[2,32,1024]{2,1,0:T(8,128)(2,1)S(1)} %pad_maximum_fusion.refs_0_) | copy-start | bytes 393220
  48.9 7.9 %collective-permute-start.3 = (bf16[2,32,1024]{2,1,0:T(8,128)(2,1)S(1)}, bf16[2,32,1024]{2,1,0:T(8,128)(2,1)S(1)}, u32[]{:S(2)}, u32[]{:S(2)}) collective-permute-start(bf16[2,32,1024]{2,1,0:T(8,128)(2,1)S(1)} %pad_maximum_fusion.refs_0_), channel_id=1, source_target_pairs={{0,16},{4,20},{8,24},{12,28},{16,32},{20,36},{24,40},{28,44},{32,4... | collective-permute-start | bytes 393224 | tf_op jit(solution)/shard_map/ppermute | solution.py:224
  50.2 10.7 %collective-permute-start.4 = (bf16[2,32,1024]{2,1,0:T(8,128)(2,1)S(1)}, bf16[2,32,1024]{2,1,0:T(8,128)(2,1)S(1)}, u32[]{:S(2)}, u32[]{:S(2)}) collective-permute-start(bf16[2,32,1024]{2,1,0:T(8,128)(2,1)S(1)} %pad_maximum_fusion.refs_0_), channel_id=1, source_target_pairs={{0,32},{4,36},{8,40},{12,44},{16,48},{20,52},{24,56},{28,60},{32,0... | collective-permute-start | bytes 393224 | tf_op jit(solution)/shard_map/ppermute | solution.py:224
  52.6 9.0 %collective-permute-start.5 = (bf16[2,32,1024]{2,1,0:T(8,128)(2,1)S(1)}, bf16[2,32,1024]{2,1,0:T(8,128)(2,1)}, u32[]{:S(2)}, u32[]{:S(2)}) collective-permute-start(bf16[2,32,1024]{2,1,0:T(8,128)(2,1)S(1)} %pad_maximum_fusion.refs_0_), channel_id=1, source_target_pairs={{0,48},{4,52},{8,56},{12,60},{16,0},{20,4},{24,8},{28,12},{32,16},... | collective-permute-start | bytes 393224 | tf_op jit(solution)/shard_map/ppermute | solution.py:224
  56.7 4.2 %copy-start.6 = (bf16[2,32,1024]{2,1,0:T(8,128)(2,1)}, bf16[2,32,1024]{2,1,0:T(8,128)(2,1)S(1)}, u32[]{:S(2)}) copy-start(bf16[2,32,1024]{2,1,0:T(8,128)(2,1)S(1)} %collective-permute-done.3.refs_1_) | copy-start | bytes 393220
  61.0 0.7 copy-start.7
  64.9 0.9 copy-start.2
  72.1 6.4 %collective-permute-start.15 = (bf16[512,256]{1,0:T(8,128)(2,1)S(1)}, bf16[512,256]{1,0:T(8,128)(2,1)S(1)}, u32[]{:S(2)}, u32[]{:S(2)}) collective-permute-start(bf16[512,256]{1,0:T(8,128)(2,1)S(1)} %get-tuple-element.14.refs_0_), channel_id=1, source_target_pairs={{0,1},{1,0},{2,3},{3,2},{4,5},{5,4},{6,7},{7,6},{8,9},{9,8},{10,11... | collective-permute-start | bytes 786440 | tf_op jit(solution)/shard_map/ppermute | solution.py:255
  74.7 5.8 %collective-permute-start.16 = (bf16[512,256]{1,0:T(8,128)(2,1)S(1)}, bf16[512,256]{1,0:T(8,128)(2,1)S(1)}, u32[]{:S(2)}, u32[]{:S(2)}) collective-permute-start(bf16[512,256]{1,0:T(8,128)(2,1)S(1)} %get-tuple-element.15.refs_1_), channel_id=1, source_target_pairs={{0,1},{1,0},{2,3},{3,2},{4,5},{5,4},{6,7},{7,6},{8,9},{9,8},{10,11... | collective-permute-start | bytes 786440 | tf_op jit(solution)/shard_map/ppermute | solution.py:255
  74.8 12.6 %collective-permute-start.6 = (bf16[512,256]{1,0:T(8,128)(2,1)S(1)}, bf16[512,256]{1,0:T(8,128)(2,1)S(1)}, u32[]{:S(2)}, u32[]{:S(2)}) collective-permute-start(bf16[512,256]{1,0:T(8,128)(2,1)S(1)} %get-tuple-element.14.refs_0_), channel_id=1, source_target_pairs={{0,8},{1,9},{4,12},{5,13},{8,2},{9,3},{12,6},{13,7},{2,10},{3,11},... | collective-permute-start | bytes 786440 | tf_op jit(solution)/shard_map/ppermute | solution.py:46
  75.1 16.0 %collective-permute-start.8 = (bf16[512,256]{1,0:T(8,128)(2,1)S(1)}, bf16[512,256]{1,0:T(8,128)(2,1)S(1)}, u32[]{:S(2)}, u32[]{:S(2)}) collective-permute-start(bf16[512,256]{1,0:T(8,128)(2,1)S(1)} %get-tuple-element.15.refs_1_), channel_id=1, source_target_pairs={{0,10},{1,11},{4,14},{5,15},{8,0},{9,1},{12,4},{13,5},{2,8},{3,9},... | collective-permute-start | bytes 786440 | tf_op jit(solution)/shard_map/ppermute | solution.py:46
  78.4 29.2 %collective-permute-start.12 = (bf16[2,4,32,1024]{3,2,1,0:T(8,128)(2,1)}, bf16[2,4,32,1024]{3,2,1,0:T(8,128)(2,1)S(1)}, u32[]{:S(2)}, u32[]{:S(2)}) collective-permute-start(bf16[2,4,32,1024]{3,2,1,0:T(8,128)(2,1)} %get-tuple-element.16.refs_4_), channel_id=1, source_target_pairs={{0,64},{4,68},{8,72},{12,76},{16,80},{20,84},{24,88},{28,92},{32,9... | collective-permute-start | bytes 1572872 | tf_op jit(solution)/shard_map/ppermute | solution.py:258
  78.5 29.2 %collective-permute-start.13 = (bf16[2,4,32,1024]{3,2,1,0:T(8,128)(2,1)}, bf16[2,4,32,1024]{3,2,1,0:T(8,128)(2,1)S(1)}, u32[]{:S(2)}, u32[]{:S(2)}) collective-permute-start(bf16[2,4,32,1024]{3,2,1,0:T(8,128)(2,1)} %get-tuple-element.16.refs_4_), channel_id=1, source_target_pairs={{0,128},{4,132},{8,136},{12,140},{16,144},{20,148},{24,152},{28,15... | collective-permute-start | bytes 1572872 | tf_op jit(solution)/shard_map/ppermute | solution.py:258
  80.6 27.1 %collective-permute-start.14 = (bf16[2,4,32,1024]{3,2,1,0:T(8,128)(2,1)}, bf16[2,4,32,1024]{3,2,1,0:T(8,128)(2,1)S(1)}, u32[]{:S(2)}, u32[]{:S(2)}) collective-permute-start(bf16[2,4,32,1024]{3,2,1,0:T(8,128)(2,1)} %get-tuple-element.16.refs_4_), channel_id=1, source_target_pairs={{0,192},{4,196},{8,200},{12,204},{16,208},{20,212},{24,216},{28,22... | collective-permute-start | bytes 1572872 | tf_op jit(solution)/shard_map/ppermute | solution.py:258
  87.4 11.0 %collective-permute-start.7 = (bf16[512,256]{1,0:T(8,128)(2,1)S(1)}, bf16[512,256]{1,0:T(8,128)(2,1)S(1)}, u32[]{:S(2)}, u32[]{:S(2)}) collective-permute-start(bf16[512,256]{1,0:T(8,128)(2,1)S(1)} %collective-permute-done.6), channel_id=1, source_target_pairs={{0,8},{1,9},{4,12},{5,13},{8,2},{9,3},{12,6},{13,7},{2,10},{3,11},... | collective-permute-start | bytes 786440 | tf_op jit(solution)/shard_map/ppermute | solution.py:46
  91.1 14.6 %collective-permute-start.9 = (bf16[512,256]{1,0:T(8,128)(2,1)S(1)}, bf16[512,256]{1,0:T(8,128)(2,1)S(1)}, u32[]{:S(2)}, u32[]{:S(2)}) collective-permute-start(bf16[512,256]{1,0:T(8,128)(2,1)S(1)} %collective-permute-done.8), channel_id=1, source_target_pairs={{0,10},{1,11},{4,14},{5,15},{8,0},{9,1},{12,4},{13,5},{2,8},{3,9},... | collective-permute-start | bytes 786440 | tf_op jit(solution)/shard_map/ppermute | solution.py:46
  98.4 9.3 %collective-permute-start.10 = (bf16[512,256]{1,0:T(8,128)(2,1)S(1)}, bf16[512,256]{1,0:T(8,128)(2,1)S(1)}, u32[]{:S(2)}, u32[]{:S(2)}) collective-permute-start(bf16[512,256]{1,0:T(8,128)(2,1)S(1)} %collective-permute-done.7.refs_0_), channel_id=1, source_target_pairs={{0,1},{1,0},{2,3},{3,2},{4,5},{5,4},{6,7},{7,6},{8,9},{9,8},{10,11... | collective-permute-start | bytes 786440 | tf_op jit(solution)/shard_map/ppermute | solution.py:256
  105.6 2.0 %collective-permute-start.11 = (bf16[512,256]{1,0:T(8,128)(2,1)S(1)}, bf16[512,256]{1,0:T(8,128)(2,1)S(1)}, u32[]{:S(2)}, u32[]{:S(2)}) collective-permute-start(bf16[512,256]{1,0:T(8,128)(2,1)S(1)} %collective-permute-done.9.refs_1_), channel_id=1, source_target_pairs={{0,1},{1,0},{2,3},{3,2},{4,5},{5,4},{6,7},{7,6},{8,9},{9,8},{10,11... | collective-permute-start | bytes 786440 | tf_op jit(solution)/shard_map/ppermute | solution.py:256

commit v5 on v4

--- a/solution.py
+++ b/solution.py
@@ -162,19 +162,38 @@
 
 
 def last_kernel(*refs):
-    *data_refs, near_ref, out_ref, lhs, w_far, sems = refs
+    *data_refs, near_ref, out_ref, lhs, w_far, result, sems = refs
     part_refs, quarter_refs = data_refs[:-4], data_refs[-4:]
+    parts = len(part_refs)
     y = lax.shift_right_logical(lax.axis_index("ctx"), 4)
-    copies = []
-    for k, ref in enumerate(quarter_refs):
-        at = lax.bitwise_and(y + (4 - k), 3)
-        copies.append(pltpu.make_async_copy(ref, w_far.at[:, at], sems.at[len(part_refs) + k]))
-        copies[-1].start()
-    for copy in fetch(part_refs, lhs, sems) + copies:
-        copy.wait()
-    w = w_far[...].reshape(lhs.shape[1], -1)
-    far = jnp.dot(lhs[...], w, preferred_element_type=jnp.float32)
-    out_ref[...] = (near_ref[...] + far).astype(jnp.bfloat16)
+    sides = [[], []]
+    for side in range(2):
+        for k, ref in enumerate(quarter_refs):
+            at = lax.bitwise_and(y + (4 - k), 3)
+            sem = sems.at[parts + 4 * side + k]
+            sides[side].append(pltpu.make_async_copy(ref.at[side], w_far.at[side, at], sem))
+    for copy in sides[0]:
+        copy.start()
+    copies = fetch(part_refs, lhs, sems)
+    for copy in sides[1]:
+        copy.start()
+    half = lhs.shape[1] // 2
+    for copy in copies[: parts // 2] + sides[0]:
+        copy.wait()
+    first = jnp.dot(lhs[:, :half], w_far[0].reshape(half, -1), preferred_element_type=jnp.float32)
+    first = near_ref[...] + first
+    for copy in copies[parts // 2 :] + sides[1]:
+        copy.wait()
+    w = w_far[1].reshape(half, -1)
+    sends = []
+    for i in range(2):
+        rows = slice(i * BLK // 2, (i + 1) * BLK // 2)
+        second = jnp.dot(lhs[rows, half:], w, preferred_element_type=jnp.float32)
+        result[rows, :] = (first[rows, :] + second).astype(jnp.bfloat16)
+        sends.append(pltpu.make_async_copy(result.at[rows, :], out_ref.at[rows, :], sems.at[parts + 8 + i]))
+        sends[-1].start()
+    for send in sends:
+        send.wait()
 
 
 def local(queries, keys, values, w_out, block_order, chosen):
@@ -271,11 +290,12 @@
         last_kernel,
         out_shape=jax.ShapeDtypeStruct((BLK, cols), bf16),
         in_specs=[hbm] * (2 * len(a_own) + 4) + [vmem],
-        out_specs=vmem,
+        out_specs=hbm,
         scratch_shapes=[
             lhs,
             pltpu.VMEM((2, 4, 4, share, cols), bf16),
-            pltpu.SemaphoreType.DMA((2 * len(a_own) + 4,)),
+            pltpu.VMEM((BLK, cols), bf16),
+            pltpu.SemaphoreType.DMA((2 * len(a_own) + 10,)),
         ],
         compiler_params=params,
         name="last",

time: 112 us -> 112 us (level)
  no operation moved by 1% of the time
where the time goes in v5:
time: 112 us; the launch traced here: 111 us
  starting transfers between devices  54 us (48%)
  waiting for transfers between devices  30.5 us (27%)
  Pallas kernels  20.2 us (18%)
  local copies, waits for them, and re-layouts  3.93 us (4%)
  other arithmetic  2.21 us (2%)
    ppermute x4, waiting for transfers between devices, over_z(): a = lax.ppermute(a, ('ctx', 'head'), along_z(step))  15.8 us
    all_to_all x1, starting transfers between devices, local(): held = lax.all_to_all(spread, 'ctx', 0, 0, tiled=True)  12.6 us
    all_to_all x1, starting transfers between devices, local(): got = lax.all_to_all(packed, 'ctx', 0, 0, tiled=True)  9.9 us
    ppermute x4, starting transfers between devices, over_z(): a = lax.ppermute(a, ('ctx', 'head'), along_z(step))  8.59 us
    ppermute x3, waiting for transfers between devices, local(): lax.ppermute(both, 'ctx', along_x(k))  6.5 us
    pallas_call x1, Pallas kernels, local(): pl.pallas_call(functools.partial(attend_kernel, rows=256), out_shape=(par...  6.25 us
    all_to_all x1, waiting for transfers between devices, local(): held = lax.all_to_all(spread, 'ctx', 0, 0, tiled=True)  6.03 us
    ppermute x3, starting transfers between devices, local(): lax.ppermute(both, 'ctx', along_x(k))  4.95 us
  transfers between devices with their start and end apart: 20, of which 9 were waited for; matrix products, arithmetic and copies ran while one was open for 4% of the time, Pallas kernels for 11%

profile of v5, /device:TPU:1, one launch (start us, length us, event | category | flops | bytes accessed | tf_op | source)
XLA Modules:
  0.0 111.2 jit_solution(12765346153178645404)
XLA Ops:
  0.0 1.9 %spread.1 = bf16[64,24,128]{2,1,0:T(8,128)(2,1)} custom-call(s32[64]{0:T(128)} %order_ref.1, s32[3]{0:T(128)} %bitcast.18, bf16[512,128]{1,0:T(8,128)(2,1)} %bitcast.12, bf16[512,128]{1,0:T(8,128)(2,1)} %bitcast.14), custom_call_target="tpu_custom_call" | custom-call | tf_op jit(solution)/shard_map/spread/pallas_call | solution.py:226
  1.9 12.6 %all-to-all-start = ((bf16[64,24,128]{2,1,0:T(8,128)(2,1)}), bf16[64,24,128]{2,1,0:T(8,128)(2,1)S(1)}, u32[]{:S(2)}, u32[]{:S(2)}) async-start(bf16[64,24,128]{2,1,0:T(8,128)(2,1)} %spread.1), calls=%async_computation | async-start | bytes 786432 | tf_op jit(solution)/shard_map/all_to_all | solution.py:233
  14.5 3.1 %cut.1 = (bf16[32,1024]{1,0:T(8,128)(2,1)}, bf16[32,1024]{1,0:T(8,128)(2,1)}, bf16[512,1024]{1,0:T(8,128)(2,1)}, bf16[512,1024]{1,0:T(8,128)(2,1)}) custom-call(bf16[512,4096]{1,0:T(8,128)(2,1)} %w_ref.1), custom_call_target="tpu_custom_call" | custom-call | tf_op jit(solution)/shard_map/cut/pallas_call | solution.py:215
  17.6 4.3 %collective-permute-start.1 = (bf16[32,1024]{1,0:T(8,128)(2,1)}, bf16[32,1024]{1,0:T(8,128)(2,1)S(1)}, u32[]{:S(2)}, u32[]{:S(2)}) collective-permute-start(bf16[32,1024]{1,0:T(8,128)(2,1)} %get-tuple-element.13), channel_id=1, source_target_pairs={{0,2},{2,0},{1,3},{3,1},{4,6},{6,4},{5,7},{7,5},{8,10},{10,8},{9,1... | collective-permute-start | bytes 196616 | tf_op jit(solution)/shard_map/ppermute | solution.py:224
  21.9 1.2 %collective-permute-start = (bf16[32,1024]{1,0:T(8,128)(2,1)}, bf16[32,1024]{1,0:T(8,128)(2,1)S(1)}, u32[]{:S(2)}, u32[]{:S(2)}) collective-permute-start(bf16[32,1024]{1,0:T(8,128)(2,1)} %get-tuple-element.12), channel_id=1, source_target_pairs={{0,2},{2,0},{1,3},{3,1},{4,6},{6,4},{5,7},{7,5},{8,10},{10,8},{9,1... | collective-permute-start | bytes 196616 | tf_op jit(solution)/shard_map/ppermute | solution.py:223
  23.0 6.0 %all-to-all-done.held_ref = bf16[64,24,128]{2,1,0:T(8,128)(2,1)S(1)} async-done(((bf16[64,24,128]{2,1,0:T(8,128)(2,1)}), bf16[64,24,128]{2,1,0:T(8,128)(2,1)S(1)}, u32[]{:S(2)}, u32[]{:S(2)}) %all-to-all-start) | async-done | bytes 393248 | tf_op jit(solution)/shard_map/all_to_all | solution.py:233
  30.4 2.2 %pack.1 = bf16[64,48,128]{2,1,0:T(8,128)(2,1)} custom-call(s32[64,3]{1,0:T(8,128)} %bitcast.17, bf16[64,24,128]{2,1,0:T(8,128)(2,1)} %copy-done.3, bf16[32,1024]{1,0:T(8,128)(2,1)} %copy-done.5, bf16[32,1024]{1,0:T(8,128)(2,1)} %copy-done.8), custom_call_target="tpu_custom_call" | custom-call | tf_op jit(solution)/shard_map/pack/pallas_call | solution.py:246
  32.7 9.9 %all-to-all-start.1 = ((bf16[64,48,128]{2,1,0:T(8,128)(2,1)}), bf16[64,48,128]{2,1,0:T(8,128)(2,1)S(1)}, u32[]{:S(2)}, u32[]{:S(2)}) async-start(bf16[64,48,128]{2,1,0:T(8,128)(2,1)} %pack.1), calls=%async_computation.1 | async-start | bytes 1572864 | tf_op jit(solution)/shard_map/all_to_all | solution.py:253
  42.6 2.8 %collective-permute-start.17 = (bf16[512,1024]{1,0:T(8,128)(2,1)}, bf16[512,1024]{1,0:T(8,128)(2,1)S(1)}, u32[]{:S(2)}, u32[]{:S(2)}) collective-permute-start(bf16[512,1024]{1,0:T(8,128)(2,1)} %get-tuple-element.18), channel_id=1, source_target_pairs={{0,1},{1,0},{2,3},{3,2},{4,5},{5,4},{6,7},{7,6},{8,9},{9,8},{10,11... | collective-permute-start | bytes 3145736 | tf_op jit(solution)/shard_map/ppermute | solution.py:278
  46.1 1.1 copy.10
  48.9 1.4 %collective-permute-start.3 = (bf16[2,32,1024]{2,1,0:T(8,128)(2,1)S(1)}, bf16[2,32,1024]{2,1,0:T(8,128)(2,1)S(1)}, u32[]{:S(2)}, u32[]{:S(2)}) collective-permute-start(bf16[2,32,1024]{2,1,0:T(8,128)(2,1)S(1)} %pad_maximum_fusion.refs_0_), channel_id=1, source_target_pairs={{0,16},{4,20},{8,24},{12,28},{16,32},{20,36},{24,40},{28,44},{32,4... | collective-permute-start | bytes 393224 | tf_op jit(solution)/shard_map/ppermute | solution.py:243
  50.2 2.4 %collective-permute-start.4 = (bf16[2,32,1024]{2,1,0:T(8,128)(2,1)S(1)}, bf16[2,32,1024]{2,1,0:T(8,128)(2,1)S(1)}, u32[]{:S(2)}, u32[]{:S(2)}) collective-permute-start(bf16[2,32,1024]{2,1,0:T(8,128)(2,1)S(1)} %pad_maximum_fusion.refs_0_), channel_id=1, source_target_pairs={{0,32},{4,36},{8,40},{12,44},{16,48},{20,52},{24,56},{28,60},{32,0... | collective-permute-start | bytes 393224 | tf_op jit(solution)/shard_map/ppermute | solution.py:243
  52.6 1.2 %collective-permute-start.5 = (bf16[2,32,1024]{2,1,0:T(8,128)(2,1)S(1)}, bf16[2,32,1024]{2,1,0:T(8,128)(2,1)}, u32[]{:S(2)}, u32[]{:S(2)}) collective-permute-start(bf16[2,32,1024]{2,1,0:T(8,128)(2,1)S(1)} %pad_maximum_fusion.refs_0_), channel_id=1, source_target_pairs={{0,48},{4,52},{8,56},{12,60},{16,0},{20,4},{24,8},{28,12},{32,16},... | collective-permute-start | bytes 393224 | tf_op jit(solution)/shard_map/ppermute | solution.py:243
  54.5 2.3 %collective-permute-done.3.refs_1_ = bf16[2,32,1024]{2,1,0:T(8,128)(2,1)S(1)} collective-permute-done((bf16[2,32,1024]{2,1,0:T(8,128)(2,1)S(1)}, bf16[2,32,1024]{2,1,0:T(8,128)(2,1)S(1)}, u32[]{:S(2)}, u32[]{:S(2)}) %collective-permute-start.3) | collective-permute-done | bytes 131104 | tf_op jit(solution)/shard_map/ppermute | solution.py:243
  56.7 4.2 %collective-permute-done.4.refs_2_ = bf16[2,32,1024]{2,1,0:T(8,128)(2,1)S(1)} collective-permute-done((bf16[2,32,1024]{2,1,0:T(8,128)(2,1)S(1)}, bf16[2,32,1024]{2,1,0:T(8,128)(2,1)S(1)}, u32[]{:S(2)}, u32[]{:S(2)}) %collective-permute-start.4) | collective-permute-done | bytes 131104 | tf_op jit(solution)/shard_map/ppermute | solution.py:243
  61.6 1.9 %merge_x.1.pass_ref = bf16[2,4,32,1024]{3,2,1,0:T(8,128)(2,1)} custom-call(bf16[2,32,1024]{2,1,0:T(8,128)(2,1)} %copy-done.4, bf16[2,32,1024]{2,1,0:T(8,128)(2,1)} %copy-done.6, bf16[2,32,1024]{2,1,0:T(8,128)(2,1)} %copy-done.7, bf16[2,32,1024]{2,1,0:T(8,128)(2,1)} %collective-permute-done.5.refs_3_), custom_call_target="tpu_custom_call" | custom-call | tf_op jit(solution)/shard_map/merge_x/pallas_call | solution.py:236
  63.6 1.3 %all-to-all-done.1.got_ref = bf16[64,48,128]{2,1,0:T(8,128)(2,1)S(1)} async-done(((bf16[64,48,128]{2,1,0:T(8,128)(2,1)}), bf16[64,48,128]{2,1,0:T(8,128)(2,1)S(1)}, u32[]{:S(2)}, u32[]{:S(2)}) %all-to-all-start.1) | async-done | bytes 786464 | tf_op jit(solution)/shard_map/all_to_all | solution.py:253
  64.9 0.9 copy-done.2
  65.8 6.2 %attend.1 = (bf16[512,256]{1,0:T(8,128)(2,1)S(1)}, bf16[512,256]{1,0:T(8,128)(2,1)S(1)}, bf16[2,4,32,1024]{3,2,1,0:T(8,128)(2,1)}) custom-call(s32[3]{0:T(128)S(1)} %compare_convert_fusion.ok_ref, bf16[4,512,128]{2,1,0:T(8,128)(2,1)S(1)} %bitcast.11, bf16[512,128]{1,0:T(8,128)(2,1)S(1)} %bitcast.13, ...), custom_call_target="tpu_custom_call", output_to_operand_aliasing={{2}: (5, {})} | custom-call | flops 1048576 | bytes 1024 | tf_op jit(solution)/shard_map/attend/pallas_call | solution.py:262
  72.1 2.7 %collective-permute-start.15 = (bf16[512,256]{1,0:T(8,128)(2,1)S(1)}, bf16[512,256]{1,0:T(8,128)(2,1)S(1)}, u32[]{:S(2)}, u32[]{:S(2)}) collective-permute-start(bf16[512,256]{1,0:T(8,128)(2,1)S(1)} %get-tuple-element.14.refs_0_), channel_id=1, source_target_pairs={{0,1},{1,0},{2,3},{3,2},{4,5},{5,4},{6,7},{7,6},{8,9},{9,8},{10,11... | collective-permute-start | bytes 786440 | tf_op jit(solution)/shard_map/ppermute | solution.py:274
  75.1 3.4 %collective-permute-start.8 = (bf16[512,256]{1,0:T(8,128)(2,1)S(1)}, bf16[512,256]{1,0:T(8,128)(2,1)S(1)}, u32[]{:S(2)}, u32[]{:S(2)}) collective-permute-start(bf16[512,256]{1,0:T(8,128)(2,1)S(1)} %get-tuple-element.15.refs_1_), channel_id=1, source_target_pairs={{0,10},{1,11},{4,14},{5,15},{8,0},{9,1},{12,4},{13,5},{2,8},{3,9},... | collective-permute-start | bytes 786440 | tf_op jit(solution)/shard_map/ppermute | solution.py:46
  78.5 2.1 %collective-permute-start.13 = (bf16[2,4,32,1024]{3,2,1,0:T(8,128)(2,1)}, bf16[2,4,32,1024]{3,2,1,0:T(8,128)(2,1)S(1)}, u32[]{:S(2)}, u32[]{:S(2)}) collective-permute-start(bf16[2,4,32,1024]{3,2,1,0:T(8,128)(2,1)} %get-tuple-element.16.refs_4_), channel_id=1, source_target_pairs={{0,128},{4,132},{8,136},{12,140},{16,144},{20,148},{24,152},{28,15... | collective-permute-start | bytes 1572872 | tf_op jit(solution)/shard_map/ppermute | solution.py:277
  80.6 1.1 collective-permute-start.14
  81.7 5.8 %collective-permute-done.6 = bf16[512,256]{1,0:T(8,128)(2,1)S(1)} collective-permute-done((bf16[512,256]{1,0:T(8,128)(2,1)S(1)}, bf16[512,256]{1,0:T(8,128)(2,1)S(1)}, u32[]{:S(2)}, u32[]{:S(2)}) %collective-permute-start.6) | collective-permute-done | bytes 262176 | tf_op jit(solution)/shard_map/ppermute | solution.py:46
  87.4 1.8 %collective-permute-start.7 = (bf16[512,256]{1,0:T(8,128)(2,1)S(1)}, bf16[512,256]{1,0:T(8,128)(2,1)S(1)}, u32[]{:S(2)}, u32[]{:S(2)}) collective-permute-start(bf16[512,256]{1,0:T(8,128)(2,1)S(1)} %collective-permute-done.6), channel_id=1, source_target_pairs={{0,8},{1,9},{4,12},{5,13},{8,2},{9,3},{12,6},{13,7},{2,10},{3,11},... | collective-permute-start | bytes 786440 | tf_op jit(solution)/shard_map/ppermute | solution.py:46
  89.2 1.8 %collective-permute-done.8 = bf16[512,256]{1,0:T(8,128)(2,1)S(1)} collective-permute-done((bf16[512,256]{1,0:T(8,128)(2,1)S(1)}, bf16[512,256]{1,0:T(8,128)(2,1)S(1)}, u32[]{:S(2)}, u32[]{:S(2)}) %collective-permute-start.8) | collective-permute-done | bytes 262176 | tf_op jit(solution)/shard_map/ppermute | solution.py:46
  91.1 3.2 %collective-permute-start.9 = (bf16[512,256]{1,0:T(8,128)(2,1)S(1)}, bf16[512,256]{1,0:T(8,128)(2,1)S(1)}, u32[]{:S(2)}, u32[]{:S(2)}) collective-permute-start(bf16[512,256]{1,0:T(8,128)(2,1)S(1)} %collective-permute-done.8), channel_id=1, source_target_pairs={{0,10},{1,11},{4,14},{5,15},{8,0},{9,1},{12,4},{13,5},{2,8},{3,9},... | collective-permute-start | bytes 786440 | tf_op jit(solution)/shard_map/ppermute | solution.py:46
  94.3 4.1 %collective-permute-done.7.refs_0_ = bf16[512,256]{1,0:T(8,128)(2,1)S(1)} collective-permute-done((bf16[512,256]{1,0:T(8,128)(2,1)S(1)}, bf16[512,256]{1,0:T(8,128)(2,1)S(1)}, u32[]{:S(2)}, u32[]{:S(2)}) %collective-permute-start.7) | collective-permute-done | bytes 262176 | tf_op jit(solution)/shard_map/ppermute | solution.py:46
  98.4 3.2 %collective-permute-start.10 = (bf16[512,256]{1,0:T(8,128)(2,1)S(1)}, bf16[512,256]{1,0:T(8,128)(2,1)S(1)}, u32[]{:S(2)}, u32[]{:S(2)}) collective-permute-start(bf16[512,256]{1,0:T(8,128)(2,1)S(1)} %collective-permute-done.7.refs_0_), channel_id=1, source_target_pairs={{0,1},{1,0},{2,3},{3,2},{4,5},{5,4},{6,7},{7,6},{8,9},{9,8},{10,11... | collective-permute-start | bytes 786440 | tf_op jit(solution)/shard_map/ppermute | solution.py:275
  101.5 4.1 %collective-permute-done.9.refs_1_ = bf16[512,256]{1,0:T(8,128)(2,1)S(1)} collective-permute-done((bf16[512,256]{1,0:T(8,128)(2,1)S(1)}, bf16[512,256]{1,0:T(8,128)(2,1)S(1)}, u32[]{:S(2)}, u32[]{:S(2)}) %collective-permute-start.9) | collective-permute-done | bytes 262176 | tf_op jit(solution)/shard_map/ppermute | solution.py:46
  106.2 1.4 %near.1.refs_8_ = f32[512,1024]{1,0:T(8,128)S(1)} custom-call(bf16[512,256]{1,0:T(8,128)(2,1)S(1)} %get-tuple-element.14.refs_0_, bf16[512,256]{1,0:T(8,128)(2,1)S(1)} %get-tuple-element.15.refs_1_, bf16[512,256]{1,0:T(8,128)(2,1)S(1)} %collective-permute-done.15.refs_2_, bf16[512,256]{1,0:T(8,128)(2,1)S(1)} %collective-permute-done.16.refs_3_, ...), custom_call_target="tpu_custom_call" | custom-call | tf_op jit(solution)/shard_map/near/pallas_call | solution.py:280
  107.7 3.3 %last.1 = bf16[512,1024]{1,0:T(8,128)(2,1)} custom-call(bf16[512,256]{1,0:T(8,128)(2,1)S(1)} %collective-permute-done.7.refs_0_, bf16[512,256]{1,0:T(8,128)(2,1)S(1)} %collective-permute-done.9.refs_1_, bf16[512,256]{1,0:T(8,128)(2,1)S(1)} %collective-permute-done.10.refs_2_, bf16[512,256]{1,0:T(8,128)(2,1)S(1)} %collective-permute-done.11.refs_3_, ...), custom_call_target="tpu_custom_call" | custom-call | tf_op jit(solution)/shard_map/last/pallas_call | solution.py:289
  (42 shorter events, 5.9 us)
Async XLA Ops:
  0.0 45.5 %copy-start.9 = (s32[64]{0:T(128)S(1)}, s32[64]{0:T(128)}, u32[]{:S(2)}) copy-start(s32[64]{0:T(128)} %order_ref.1) | copy-start | bytes 772
  1.9 27.2 %all-to-all-start = ((bf16[64,24,128]{2,1,0:T(8,128)(2,1)}), bf16[64,24,128]{2,1,0:T(8,128)(2,1)S(1)}, u32[]{:S(2)}, u32[]{:S(2)}) async-start(bf16[64,24,128]{2,1,0:T(8,128)(2,1)} %spread.1), calls=%async_computation | async-start | bytes 786432 | tf_op jit(solution)/shard_map/all_to_all | solution.py:233
  14.5 39.4 %copy-start.10 = (s32[1,1,3]{2,1,0:T(1,128)S(1)}, s32[1,1,3]{2,1,0:T(1,128)}, u32[]{:S(2)}) copy-start(s32[1,1,3]{2,1,0:T(1,128)} %param.11) | copy-start | bytes 40
  14.5 50.4 %copy-start.1 = (bf16[512,1,128]{2,0,1:T(8,128)(2,1)S(1)}, bf16[512,1,128]{2,0,1:T(8,128)(2,1)}, u32[]{:S(2)}) copy-start(bf16[512,1,128]{2,0,1:T(8,128)(2,1)} %param.7) | copy-start | bytes 393220
  17.6 88.6 %copy-start = (bf16[512,1024]{1,0:T(8,128)(2,1)S(1)}, bf16[512,1024]{1,0:T(8,128)(2,1)}, u32[]{:S(2)}) copy-start(bf16[512,1024]{1,0:T(8,128)(2,1)} %get-tuple-element.17.refs_4_) | copy-start | bytes 3145732
  17.6 12.2 %collective-permute-start.1 = (bf16[32,1024]{1,0:T(8,128)(2,1)}, bf16[32,1024]{1,0:T(8,128)(2,1)S(1)}, u32[]{:S(2)}, u32[]{:S(2)}) collective-permute-start(bf16[32,1024]{1,0:T(8,128)(2,1)} %get-tuple-element.13), channel_id=1, source_target_pairs={{0,2},{2,0},{1,3},{3,1},{4,6},{6,4},{5,7},{7,5},{8,10},{10,8},{9,1... | collective-permute-start | bytes 196616 | tf_op jit(solution)/shard_map/ppermute | solution.py:224
  21.9 7.9 %collective-permute-start = (bf16[32,1024]{1,0:T(8,128)(2,1)}, bf16[32,1024]{1,0:T(8,128)(2,1)S(1)}, u32[]{:S(2)}, u32[]{:S(2)}) collective-permute-start(bf16[32,1024]{1,0:T(8,128)(2,1)} %get-tuple-element.12), channel_id=1, source_target_pairs={{0,2},{2,0},{1,3},{3,1},{4,6},{6,4},{5,7},{7,5},{8,10},{10,8},{9,1... | collective-permute-start | bytes 196616 | tf_op jit(solution)/shard_map/ppermute | solution.py:223
  29.1 0.8 copy-start.3
  29.8 0.6 copy-start.8
  29.8 0.6 copy-start.5
  32.7 32.2 %all-to-all-start.1 = ((bf16[64,48,128]{2,1,0:T(8,128)(2,1)}), bf16[64,48,128]{2,1,0:T(8,128)(2,1)S(1)}, u32[]{:S(2)}, u32[]{:S(2)}) async-start(bf16[64,48,128]{2,1,0:T(8,128)(2,1)} %pack.1), calls=%async_computation.1 | async-start | bytes 1572864 | tf_op jit(solution)/shard_map/all_to_all | solution.py:253
  42.6 35.8 %collective-permute-start.17 = (bf16[512,1024]{1,0:T(8,128)(2,1)}, bf16[512,1024]{1,0:T(8,128)(2,1)S(1)}, u32[]{:S(2)}, u32[]{:S(2)}) collective-permute-start(bf16[512,1024]{1,0:T(8,128)(2,1)} %get-tuple-element.18), channel_id=1, source_target_pairs={{0,1},{1,0},{2,3},{3,2},{4,5},{5,4},{6,7},{7,6},{8,9},{9,8},{10,11... | collective-permute-start | bytes 3145736 | tf_op jit(solution)/shard_map/ppermute | solution.py:278
  45.4 2.6 %collective-permute-start.2 = (bf16[32,1024]{1,0:T(8,128)(2,1)}, bf16[32,1024]{1,0:T(8,128)(2,1)}, u32[]{:S(2)}, u32[]{:S(2)}) collective-permute-start(bf16[32,1024]{1,0:T(8,128)(2,1)} %copy-done.8), channel_id=1, source_target_pairs={{0,1},{1,0},{2,3},{3,2},{4,5},{5,4},{6,7},{7,6},{8,9},{9,8},{10,11... | collective-permute-start | bytes 196616 | tf_op jit(solution)/shard_map/ppermute | solution.py:235
  48.9 5.0 %copy-start.4 = (bf16[2,32,1024]{2,1,0:T(8,128)(2,1)}, bf16[2,32,1024]{2,1,0:T(8,128)(2,1)S(1)}, u32[]{:S(2)}) copy-start(bf16[2,32,1024]{2,1,0:T(8,128)(2,1)S(1)} %pad_maximum_fusion.refs_0_) | copy-start | bytes 393220
  48.9 7.9 %collective-permute-start.3 = (bf16[2,32,1024]{2,1,0:T(8,128)(2,1)S(1)}, bf16[2,32,1024]{2,1,0:T(8,128)(2,1)S(1)}, u32[]{:S(2)}, u32[]{:S(2)}) collective-permute-start(bf16[2,32,1024]{2,1,0:T(8,128)(2,1)S(1)} %pad_maximum_fusion.refs_0_), channel_id=1, source_target_pairs={{0,16},{4,20},{8,24},{12,28},{16,32},{20,36},{24,40},{28,44},{32,4... | collective-permute-start | bytes 393224 | tf_op jit(solution)/shard_map/ppermute | solution.py:243
  50.2 10.7 %collective-permute-start.4 = (bf16[2,32,1024]{2,1,0:T(8,128)(2,1)S(1)}, bf16[2,32,1024]{2,1,0:T(8,128)(2,1)S(1)}, u32[]{:S(2)}, u32[]{:S(2)}) collective-permute-start(bf16[2,32,1024]{2,1,0:T(8,128)(2,1)S(1)} %pad_maximum_fusion.refs_0_), channel_id=1, source_target_pairs={{0,32},{4,36},{8,40},{12,44},{16,48},{20,52},{24,56},{28,60},{32,0... | collective-permute-start | bytes 393224 | tf_op jit(solution)/shard_map/ppermute | solution.py:243
  52.6 9.0 %collective-permute-start.5 = (bf16[2,32,1024]{2,1,0:T(8,128)(2,1)S(1)}, bf16[2,32,1024]{2,1,0:T(8,128)(2,1)}, u32[]{:S(2)}, u32[]{:S(2)}) collective-permute-start(bf16[2,32,1024]{2,1,0:T(8,128)(2,1)S(1)} %pad_maximum_fusion.refs_0_), channel_id=1, source_target_pairs={{0,48},{4,52},{8,56},{12,60},{16,0},{20,4},{24,8},{28,12},{32,16},... | collective-permute-start | bytes 393224 | tf_op jit(solution)/shard_map/ppermute | solution.py:243
  56.7 4.2 %copy-start.6 = (bf16[2,32,1024]{2,1,0:T(8,128)(2,1)}, bf16[2,32,1024]{2,1,0:T(8,128)(2,1)S(1)}, u32[]{:S(2)}) copy-start(bf16[2,32,1024]{2,1,0:T(8,128)(2,1)S(1)} %collective-permute-done.3.refs_1_) | copy-start | bytes 393220
  61.0 0.7 copy-start.7
  64.9 0.9 copy-start.2
  72.1 6.4 %collective-permute-start.15 = (bf16[512,256]{1,0:T(8,128)(2,1)S(1)}, bf16[512,256]{1,0:T(8,128)(2,1)S(1)}, u32[]{:S(2)}, u32[]{:S(2)}) collective-permute-start(bf16[512,256]{1,0:T(8,128)(2,1)S(1)} %get-tuple-element.14.refs_0_), channel_id=1, source_target_pairs={{0,1},{1,0},{2,3},{3,2},{4,5},{5,4},{6,7},{7,6},{8,9},{9,8},{10,11... | collective-permute-start | bytes 786440 | tf_op jit(solution)/shard_map/ppermute | solution.py:274
  74.7 5.8 %collective-permute-start.16 = (bf16[512,256]{1,0:T(8,128)(2,1)S(1)}, bf16[512,256]{1,0:T(8,128)(2,1)S(1)}, u32[]{:S(2)}, u32[]{:S(2)}) collective-permute-start(bf16[512,256]{1,0:T(8,128)(2,1)S(1)} %get-tuple-element.15.refs_1_), channel_id=1, source_target_pairs={{0,1},{1,0},{2,3},{3,2},{4,5},{5,4},{6,7},{7,6},{8,9},{9,8},{10,11... | collective-permute-start | bytes 786440 | tf_op jit(solution)/shard_map/ppermute | solution.py:274
  74.8 12.6 %collective-permute-start.6 = (bf16[512,256]{1,0:T(8,128)(2,1)S(1)}, bf16[512,256]{1,0:T(8,128)(2,1)S(1)}, u32[]{:S(2)}, u32[]{:S(2)}) collective-permute-start(bf16[512,256]{1,0:T(8,128)(2,1)S(1)} %get-tuple-element.14.refs_0_), channel_id=1, source_target_pairs={{0,8},{1,9},{4,12},{5,13},{8,2},{9,3},{12,6},{13,7},{2,10},{3,11},... | collective-permute-start | bytes 786440 | tf_op jit(solution)/shard_map/ppermute | solution.py:46
  75.1 16.0 %collective-permute-start.8 = (bf16[512,256]{1,0:T(8,128)(2,1)S(1)}, bf16[512,256]{1,0:T(8,128)(2,1)S(1)}, u32[]{:S(2)}, u32[]{:S(2)}) collective-permute-start(bf16[512,256]{1,0:T(8,128)(2,1)S(1)} %get-tuple-element.15.refs_1_), channel_id=1, source_target_pairs={{0,10},{1,11},{4,14},{5,15},{8,0},{9,1},{12,4},{13,5},{2,8},{3,9},... | collective-permute-start | bytes 786440 | tf_op jit(solution)/shard_map/ppermute | solution.py:46
  78.4 29.2 %collective-permute-start.12 = (bf16[2,4,32,1024]{3,2,1,0:T(8,128)(2,1)}, bf16[2,4,32,1024]{3,2,1,0:T(8,128)(2,1)S(1)}, u32[]{:S(2)}, u32[]{:S(2)}) collective-permute-start(bf16[2,4,32,1024]{3,2,1,0:T(8,128)(2,1)} %get-tuple-element.16.refs_4_), channel_id=1, source_target_pairs={{0,64},{4,68},{8,72},{12,76},{16,80},{20,84},{24,88},{28,92},{32,9... | collective-permute-start | bytes 1572872 | tf_op jit(solution)/shard_map/ppermute | solution.py:277
  78.5 29.2 %collective-permute-start.13 = (bf16[2,4,32,1024]{3,2,1,0:T(8,128)(2,1)}, bf16[2,4,32,1024]{3,2,1,0:T(8,128)(2,1)S(1)}, u32[]{:S(2)}, u32[]{:S(2)}) collective-permute-start(bf16[2,4,32,1024]{3,2,1,0:T(8,128)(2,1)} %get-tuple-element.16.refs_4_), channel_id=1, source_target_pairs={{0,128},{4,132},{8,136},{12,140},{16,144},{20,148},{24,152},{28,15... | collective-permute-start | bytes 1572872 | tf_op jit(solution)/shard_map/ppermute | solution.py:277
  80.6 27.1 %collective-permute-start.14 = (bf16[2,4,32,1024]{3,2,1,0:T(8,128)(2,1)}, bf16[2,4,32,1024]{3,2,1,0:T(8,128)(2,1)S(1)}, u32[]{:S(2)}, u32[]{:S(2)}) collective-permute-start(bf16[2,4,32,1024]{3,2,1,0:T(8,128)(2,1)} %get-tuple-element.16.refs_4_), channel_id=1, source_target_pairs={{0,192},{4,196},{8,200},{12,204},{16,208},{20,212},{24,216},{28,22... | collective-permute-start | bytes 1572872 | tf_op jit(solution)/shard_map/ppermute | solution.py:277
  87.4 11.0 %collective-permute-start.7 = (bf16[512,256]{1,0:T(8,128)(2,1)S(1)}, bf16[512,256]{1,0:T(8,128)(2,1)S(1)}, u32[]{:S(2)}, u32[]{:S(2)}) collective-permute-start(bf16[512,256]{1,0:T(8,128)(2,1)S(1)} %collective-permute-done.6), channel_id=1, source_target_pairs={{0,8},{1,9},{4,12},{5,13},{8,2},{9,3},{12,6},{13,7},{2,10},{3,11},... | collective-permute-start | bytes 786440 | tf_op jit(solution)/shard_map/ppermute | solution.py:46
  91.1 14.6 %collective-permute-start.9 = (bf16[512,256]{1,0:T(8,128)(2,1)S(1)}, bf16[512,256]{1,0:T(8,128)(2,1)S(1)}, u32[]{:S(2)}, u32[]{:S(2)}) collective-permute-start(bf16[512,256]{1,0:T(8,128)(2,1)S(1)} %collective-permute-done.8), channel_id=1, source_target_pairs={{0,10},{1,11},{4,14},{5,15},{8,0},{9,1},{12,4},{13,5},{2,8},{3,9},... | collective-permute-start | bytes 786440 | tf_op jit(solution)/shard_map/ppermute | solution.py:46
  98.4 9.3 %collective-permute-start.10 = (bf16[512,256]{1,0:T(8,128)(2,1)S(1)}, bf16[512,256]{1,0:T(8,128)(2,1)S(1)}, u32[]{:S(2)}, u32[]{:S(2)}) collective-permute-start(bf16[512,256]{1,0:T(8,128)(2,1)S(1)} %collective-permute-done.7.refs_0_), channel_id=1, source_target_pairs={{0,1},{1,0},{2,3},{3,2},{4,5},{5,4},{6,7},{7,6},{8,9},{9,8},{10,11... | collective-permute-start | bytes 786440 | tf_op jit(solution)/shard_map/ppermute | solution.py:275
  105.6 2.0 %collective-permute-start.11 = (bf16[512,256]{1,0:T(8,128)(2,1)S(1)}, bf16[512,256]{1,0:T(8,128)(2,1)S(1)}, u32[]{:S(2)}, u32[]{:S(2)}) collective-permute-start(bf16[512,256]{1,0:T(8,128)(2,1)S(1)} %collective-permute-done.9.refs_1_), channel_id=1, source_target_pairs={{0,1},{1,0},{2,3},{3,2},{4,5},{5,4},{6,7},{7,6},{8,9},{9,8},{10,11... | collective-permute-start | bytes 786440 | tf_op jit(solution)/shard_map/ppermute | solution.py:275
